TPU v7x, 32 devices: a whole 2x2x4 slice. The times are simulated.
32 devices in a mesh: rep: 4 (over z), fsdp: 8 (over y, x, core).
Axes of the slice: x: 2, y: 2, z: 4, core: 2. Of those that a mesh axis runs over, the one named last changes fastest.
Arguments:
- enc_in: bfloat16 [8192, 768], P(('rep', 'fsdp')), may hold values from -6 to 6
- dec_in: bfloat16 [8192, 768], P(('rep', 'fsdp')), may hold values from -6 to 6
- bucket: int32 [32], P(('rep', 'fsdp')), may hold values from 0 to 1, as said below
- enc_lengths: int32 [32, 4], P(('rep', 'fsdp')), may hold values from 0 to 256, as said below
- dec_lengths: int32 [32, 4], P(('rep', 'fsdp')), may hold values from 0 to 256, as said below
- enc_attn: bfloat16 [768, 3072], P('fsdp'), may hold values from -3 to 3
- enc_vec: bfloat16 [9216], P('fsdp'), may hold values from -1.2 to 1.6
- enc_w1: bfloat16 [768, 3072], P('fsdp'), may hold values from -0.21875 to 0.21875
- enc_w2: bfloat16 [3072, 768], P('fsdp'), may hold values from -0.109375 to 0.109375
- dec_attn: bfloat16 [768, 6144], P('fsdp'), may hold values from -3 to 3
- dec_vec: bfloat16 [13056], P('fsdp'), may hold values from -1.2 to 1.6
- dec_w1: bfloat16 [768, 3072], P('fsdp'), may hold values from -0.21875 to 0.21875
- dec_w2: bfloat16 [3072, 768], P('fsdp'), may hold values from -0.109375 to 0.109375
- enc_cot: bfloat16 [8192, 768], P(('rep', 'fsdp')), may hold values from -6 to 6
- dec_cot: bfloat16 [8192, 768], P(('rep', 'fsdp')), may hold values from -6 to 6
Outputs:
- enc_out: bfloat16 [8192, 768], P(('rep', 'fsdp'))
- dec_out: bfloat16 [8192, 768], P(('rep', 'fsdp'))
- enc_in_grad: float32 [8192, 768], P(('rep', 'fsdp'))
- dec_in_grad: float32 [8192, 768], P(('rep', 'fsdp'))
- enc_attn_grad: float32 [768, 3072], P('fsdp')
- enc_vec_grad: float32 [9216], P('fsdp')
- enc_w1_grad: float32 [768, 3072], P('fsdp')
- enc_w2_grad: float32 [3072, 768], P('fsdp')
- dec_attn_grad: float32 [768, 6144], P('fsdp')
- dec_vec_grad: float32 [13056], P('fsdp')
- dec_w1_grad: float32 [768, 3072], P('fsdp')
- dec_w2_grad: float32 [3072, 768], P('fsdp')
Inputs may be any that keep to these rules, and one draw needn't show every extreme that they name: Some block has bucket 1 in every draw. In a block with bucket 1, entry 0 is the length of its one sequence, half of 256 or more, and the other entries are 0; with bucket 0 all 4 entries are lengths between a quarter of 64 (rounded down) and 64. Some block with bucket 1 has length 256 in every draw, in enc_lengths and dec_lengths alike. `dec_lengths`: as for enc_lengths.
All inputs are finite; a program needn't handle non-finite values.
Results may differ from a plain program's by a relative error of at most 0.03.
Values may be sent and summed in bfloat16 or wider, within the bound.
No kernel may reach another device: no remote copies, remote signals or barrier semaphores. Data moves between devices by JAX's collectives and lax.ppermute only.
A program may use at most 256 MiB of HBM per device.

v0:
```python
import jax
import jax.numpy as jnp
from jax import lax
from jax.sharding import PartitionSpec as P

HEAD = 64


EPSILON = 1e-05
NEG_FILL = -1e30
SCORE_SCALE = 0.125


def norm_rows(hidden, gain_row, shift_row):
    row_mean = jnp.mean(hidden, axis=-1, keepdims=True)
    centred = hidden - row_mean
    variance = jnp.mean(centred * centred, axis=-1, keepdims=True)
    return centred * lax.rsqrt(variance + EPSILON) * gain_row + shift_row


def norm_back(hidden, gain_row, shift_row, gradient):
    unused, pullback = jax.vjp(norm_rows, hidden, gain_row, shift_row)
    return pullback(gradient)


def gelu_exact(hidden):
    return jax.nn.gelu(hidden, approximate=False)


def dot_plain(first_op, second_op):
    return jnp.dot(first_op, second_op, preferred_element_type=jnp.float32)


def dot_left(first_op, second_op):
    return lax.dot_general(
        first_op, second_op, (((0,), (0,)), ((), ())), preferred_element_type=jnp.float32
    )


def dot_right(first_op, second_op):
    return lax.dot_general(
        first_op, second_op, (((1,), (1,)), ((), ())), preferred_element_type=jnp.float32
    )


def build_masks(one_long, enc_len, dec_len, row_total, seg_count):
    span_rows = jnp.where(one_long == 1, row_total, row_total // seg_count).astype(jnp.int32)
    row_index = jnp.arange(row_total, dtype=jnp.int32)
    group_id = row_index // span_rows
    row_place = row_index - group_id * span_rows
    in_group = group_id[:, None] == jnp.arange(seg_count, dtype=jnp.int32)[None, :]
    enc_live = row_place < jnp.sum(jnp.where(in_group, enc_len[None, :], 0), axis=1)
    dec_live = row_place < jnp.sum(jnp.where(in_group, dec_len[None, :], 0), axis=1)
    same_group = group_id[:, None] == group_id[None, :]
    enc_mask = same_group & enc_live[None, :]
    self_mask = same_group & dec_live[None, :] & (row_index[None, :] <= row_index[:, None])
    return (enc_mask, self_mask, enc_mask)


def unpack(vector, row_count, feature):
    rows_part = vector[: row_count * feature].astype(jnp.float32).reshape(row_count, feature)
    return (rows_part, vector[row_count * feature :].astype(jnp.float32))


def fetch(attn_rows, vec_part, w_in, w_out):
    return (
        lax.all_gather(attn_rows, "fsdp", axis=0, tiled=True),
        lax.all_gather(vec_part, "fsdp", axis=0, tiled=True),
        lax.all_gather(w_in, "fsdp", axis=0, tiled=True),
        lax.all_gather(w_out, "fsdp", axis=0, tiled=True),
    )


def fetch_again(attn_rows, vec_part, w_in, w_out):
    return (
        lax.all_gather(attn_rows, "fsdp", axis=0, tiled=True),
        lax.all_gather(vec_part, "fsdp", axis=0, tiled=True),
        lax.all_gather(w_in, "fsdp", axis=0, tiled=True),
        lax.all_gather(w_out, "fsdp", axis=0, tiled=True),
    )


def reduce_grads(grad_attn, grad_vec, grad_in, grad_out):
    shard = (
        lax.psum_scatter(
            grad_attn.astype(jnp.bfloat16), "fsdp", scatter_dimension=0, tiled=True
        ).astype(jnp.float32),
        lax.psum_scatter(
            grad_vec.astype(jnp.bfloat16), "fsdp", scatter_dimension=0, tiled=True
        ).astype(jnp.float32),
        lax.psum_scatter(
            grad_in.astype(jnp.bfloat16), "fsdp", scatter_dimension=0, tiled=True
        ).astype(jnp.float32),
        lax.psum_scatter(
            grad_out.astype(jnp.bfloat16), "fsdp", scatter_dimension=0, tiled=True
        ).astype(jnp.float32),
    )
    return (
        lax.psum(shard[0].astype(jnp.bfloat16), "rep").astype(jnp.float32),
        lax.psum(shard[1].astype(jnp.bfloat16), "rep").astype(jnp.float32),
        lax.psum(shard[2].astype(jnp.bfloat16), "rep").astype(jnp.float32),
        lax.psum(shard[3].astype(jnp.bfloat16), "rep").astype(jnp.float32),
    )


def attend(q_in, kv_in, weights, biases, key_mask, one_source):
    row_total, feature = q_in.shape
    head_count = feature // HEAD
    if one_source:
        packed = dot_plain(q_in, weights[:, : 3 * feature])
        q_pre = packed[:, :feature]
        k_pre = packed[:, feature : 2 * feature]
        v_pre = packed[:, 2 * feature :]
    else:
        q_pre = dot_plain(q_in, weights[:, :feature])
        packed = dot_plain(kv_in, weights[:, feature : 3 * feature])
        k_pre = packed[:, :feature]
        v_pre = packed[:, feature:]
    queries = (q_pre + biases[0]).astype(jnp.bfloat16).reshape(row_total, head_count, HEAD)
    keys_low = k_pre.astype(jnp.bfloat16).reshape(row_total, head_count, HEAD)
    values = (v_pre + biases[1]).astype(jnp.bfloat16).reshape(row_total, head_count, HEAD)
    raw_score = jnp.einsum("qhd,khd->hqk", queries, keys_low, preferred_element_type=jnp.float32)
    probs = jax.nn.softmax(jnp.where(key_mask[None], raw_score * SCORE_SCALE, NEG_FILL), axis=-1)
    probs_low = probs.astype(jnp.bfloat16)
    mixed = jnp.einsum("hqk,khd->qhd", probs_low, values, preferred_element_type=jnp.float32)
    mixed = mixed.reshape(row_total, feature).astype(jnp.bfloat16)
    branch = dot_plain(mixed, weights[:, 3 * feature :]) + biases[2]
    return (branch, (queries, keys_low, values, probs, probs_low, mixed))


def attend_back(gradient, q_in, kv_in, weights, saved, one_source):
    queries, keys_low, values, probs, probs_low, mixed = saved
    row_total, feature = q_in.shape
    head_count = feature // HEAD
    grad_bias_o = jnp.sum(gradient, axis=0)
    grad_low = gradient.astype(jnp.bfloat16)
    grad_w_o = dot_left(mixed, grad_low)
    grad_mixed = dot_right(grad_low, weights[:, 3 * feature :]).astype(jnp.bfloat16)
    grad_mixed = grad_mixed.reshape(row_total, head_count, HEAD)
    grad_probs = jnp.einsum("qhd,khd->hqk", grad_mixed, values, preferred_element_type=jnp.float32)
    grad_values = jnp.einsum(
        "hqk,qhd->khd", probs_low, grad_mixed, preferred_element_type=jnp.float32
    )
    grad_score = probs * (grad_probs - jnp.sum(grad_probs * probs, axis=-1, keepdims=True))
    grad_raw = (grad_score * SCORE_SCALE).astype(jnp.bfloat16)
    grad_query = jnp.einsum(
        "hqk,khd->qhd", grad_raw, keys_low, preferred_element_type=jnp.float32
    ).reshape(row_total, feature)
    grad_keys = jnp.einsum(
        "hqk,qhd->khd", grad_raw, queries, preferred_element_type=jnp.float32
    ).reshape(row_total, feature)
    grad_values = grad_values.reshape(row_total, feature)
    grad_bias_q = jnp.sum(grad_query, axis=0)
    grad_bias_v = jnp.sum(grad_values, axis=0)
    low_query = grad_query.astype(jnp.bfloat16)
    low_kv = jnp.concatenate(
        [grad_keys.astype(jnp.bfloat16), grad_values.astype(jnp.bfloat16)], axis=1
    )
    if one_source:
        packed = jnp.concatenate([low_query, low_kv], axis=1)
        grad_weights = jnp.concatenate([dot_left(q_in, packed), grad_w_o], axis=1)
        grad_q_in = dot_right(packed, weights[:, : 3 * feature])
        grad_kv_in = grad_q_in
    else:
        grad_weights = jnp.concatenate(
            [dot_left(q_in, low_query), dot_left(kv_in, low_kv), grad_w_o], axis=1
        )
        grad_q_in = dot_right(low_query, weights[:, :feature])
        grad_kv_in = dot_right(low_kv, weights[:, feature : 3 * feature])
    return (grad_q_in, grad_kv_in, grad_weights, (grad_bias_q, grad_bias_v, grad_bias_o))


def feed(rows_in, w_in, b_in, w_out, b_out):
    hidden = dot_plain(rows_in, w_in) + b_in
    active = gelu_exact(hidden).astype(jnp.bfloat16)
    return (dot_plain(active, w_out) + b_out, (hidden, active))


def feed_back(gradient, rows_in, w_in, w_out, saved):
    hidden, active = saved
    grad_b_out = jnp.sum(gradient, axis=0)
    grad_low = gradient.astype(jnp.bfloat16)
    grad_w_out = dot_left(active, grad_low)
    grad_active = dot_right(grad_low, w_out)
    unused, pullback = jax.vjp(gelu_exact, hidden)
    grad_hidden = pullback(grad_active)[0]
    grad_b_in = jnp.sum(grad_hidden, axis=0)
    hidden_low = grad_hidden.astype(jnp.bfloat16)
    grad_w_in = dot_left(rows_in, hidden_low)
    grad_rows = dot_right(hidden_low, w_in)
    return (grad_rows, grad_w_in, grad_b_in, grad_w_out, grad_b_out)


def per_device(
    enc_in,
    dec_in,
    bucket,
    enc_lengths,
    dec_lengths,
    enc_attn,
    enc_vec,
    enc_w1,
    enc_w2,
    dec_attn,
    dec_vec,
    dec_w1,
    dec_w2,
    enc_cot,
    dec_cot,
):
    row_total, feature = enc_in.shape
    enc_mask, self_mask, cross_mask = build_masks(
        bucket[0], enc_lengths[0], dec_lengths[0], row_total, enc_lengths.shape[1]
    )
    enc_weights = fetch(enc_attn, enc_vec, enc_w1, enc_w2)
    e_attn, e_vec, e_in, e_out = enc_weights
    e_rows, e_tail = unpack(e_vec, 8, feature)
    branch, e_saved_a = attend(enc_in, enc_in, e_attn, e_rows[0:3], enc_mask, True)
    e_hid_a = enc_in.astype(jnp.float32) + branch
    e_first = norm_rows(e_hid_a, e_rows[3], e_rows[4]).astype(jnp.bfloat16)
    branch, e_saved_f = feed(e_first, e_in, e_tail, e_out, e_rows[5])
    e_hid_f = e_first.astype(jnp.float32) + branch
    encoded = norm_rows(e_hid_f, e_rows[6], e_rows[7]).astype(jnp.bfloat16)
    dec_weights = fetch(dec_attn, dec_vec, dec_w1, dec_w2)
    d_attn, d_vec, d_in, d_out = dec_weights
    d_rows, d_tail = unpack(d_vec, 13, feature)
    branch, d_saved_s = attend(
        dec_in, dec_in, d_attn[:, : 4 * feature], d_rows[0:3], self_mask, True
    )
    d_hid_s = dec_in.astype(jnp.float32) + branch
    d_first = norm_rows(d_hid_s, d_rows[3], d_rows[4]).astype(jnp.bfloat16)
    branch, d_saved_c = attend(
        d_first, encoded, d_attn[:, 4 * feature :], d_rows[5:8], cross_mask, False
    )
    d_hid_c = d_first.astype(jnp.float32) + branch
    d_second = norm_rows(d_hid_c, d_rows[8], d_rows[9]).astype(jnp.bfloat16)
    branch, d_saved_f = feed(d_second, d_in, d_tail, d_out, d_rows[10])
    d_hid_f = d_second.astype(jnp.float32) + branch
    decoded = norm_rows(d_hid_f, d_rows[11], d_rows[12]).astype(jnp.bfloat16)
    dec_weights = fetch_again(dec_attn, dec_vec, dec_w1, dec_w2)
    d_attn, d_vec, d_in, d_out = dec_weights
    d_rows, d_tail = unpack(d_vec, 13, feature)
    gradient, grad_g11, grad_n12 = norm_back(
        d_hid_f, d_rows[11], d_rows[12], dec_cot.astype(jnp.float32)
    )
    grad_rows, grad_d_in, grad_d_tail, grad_d_out, grad_b10 = feed_back(
        gradient, d_second, d_in, d_out, d_saved_f
    )
    gradient, grad_g8, grad_n9 = norm_back(d_hid_c, d_rows[8], d_rows[9], gradient + grad_rows)
    grad_q_in, grad_encoded, grad_cross, cross_bias = attend_back(
        gradient, d_first, encoded, d_attn[:, 4 * feature :], d_saved_c, False
    )
    gradient, grad_g3, grad_n4 = norm_back(d_hid_s, d_rows[3], d_rows[4], gradient + grad_q_in)
    grad_self_in, unused, grad_self, self_bias = attend_back(
        gradient, dec_in, dec_in, d_attn[:, : 4 * feature], d_saved_s, True
    )
    dec_in_grad = gradient + grad_self_in
    dec_stack = jnp.stack(
        [
            self_bias[0],
            self_bias[1],
            self_bias[2],
            grad_g3,
            grad_n4,
            cross_bias[0],
            cross_bias[1],
            cross_bias[2],
            grad_g8,
            grad_n9,
            grad_b10,
            grad_g11,
            grad_n12,
        ]
    )
    dec_vec_full = jnp.concatenate([dec_stack.reshape(-1), grad_d_tail])
    dec_shards = reduce_grads(
        jnp.concatenate([grad_self, grad_cross], axis=1), dec_vec_full, grad_d_in, grad_d_out
    )
    enc_weights = fetch_again(enc_attn, enc_vec, enc_w1, enc_w2)
    e_attn, e_vec, e_in, e_out = enc_weights
    e_rows, e_tail = unpack(e_vec, 8, feature)
    gradient, grad_g6, grad_n7 = norm_back(
        e_hid_f, e_rows[6], e_rows[7], enc_cot.astype(jnp.float32) + grad_encoded
    )
    grad_rows, grad_e_in, grad_e_tail, grad_e_out, grad_b5 = feed_back(
        gradient, e_first, e_in, e_out, e_saved_f
    )
    gradient, grad_g3e, grad_n4e = norm_back(e_hid_a, e_rows[3], e_rows[4], gradient + grad_rows)
    grad_self_in, unused, grad_e_attn, enc_bias = attend_back(
        gradient, enc_in, enc_in, e_attn, e_saved_a, True
    )
    enc_in_grad = gradient + grad_self_in
    enc_stack = jnp.stack(
        [enc_bias[0], enc_bias[1], enc_bias[2], grad_g3e, grad_n4e, grad_b5, grad_g6, grad_n7]
    )
    enc_vec_full = jnp.concatenate([enc_stack.reshape(-1), grad_e_tail])
    enc_shards = reduce_grads(grad_e_attn, enc_vec_full, grad_e_in, grad_e_out)
    return (
        encoded,
        decoded,
        enc_in_grad,
        dec_in_grad,
        enc_shards[0],
        enc_shards[1],
        enc_shards[2],
        enc_shards[3],
        dec_shards[0],
        dec_shards[1],
        dec_shards[2],
        dec_shards[3],
    )


def solution(mesh):
    in_specs = (
        P(("rep", "fsdp"), None),
        P(("rep", "fsdp"), None),
        P(("rep", "fsdp")),
        P(("rep", "fsdp"), None),
        P(("rep", "fsdp"), None),
        P("fsdp", None),
        P("fsdp"),
        P("fsdp", None),
        P("fsdp", None),
        P("fsdp", None),
        P("fsdp"),
        P("fsdp", None),
        P("fsdp", None),
        P(("rep", "fsdp"), None),
        P(("rep", "fsdp"), None),
    )
    out_specs = (
        P(("rep", "fsdp"), None),
        P(("rep", "fsdp"), None),
        P(("rep", "fsdp"), None),
        P(("rep", "fsdp"), None),
        P("fsdp", None),
        P("fsdp"),
        P("fsdp", None),
        P("fsdp", None),
        P("fsdp", None),
        P("fsdp"),
        P("fsdp", None),
        P("fsdp", None),
    )
    return jax.shard_map(
        per_device, mesh=mesh, in_specs=in_specs, out_specs=out_specs, check_vma=False
    )
```

profile of v0, /device:TPU:0, one launch (start us, length us, event | category | flops | bytes accessed | tf_op | source)
XLA Modules:
  0.0 916.7 jit_solution(11810132857031894653)
XLA Ops:
  11.3 10.6 %all-gather = bf16[8,1,1152]{2,1,0:T(2,128)(2,1)S(1)} all-gather(bf16[1,1,1152]{2,1,0:T(2,128)(2,1)S(1)} %reshape.503), channel_id=1, replica_groups=mesh['rep'=4,'fsdp'=8] {'fsdp'}, dimensions={0}, use_global_device_ids=true | all-gather | bytes 20736 | tf_op jit(solution)/shard_map/all_gather | solution.py:68
  23.6 24.1 %all-reduce = bf16[13056]{0:T(1024)(128)(2,1)S(1)} all-reduce(bf16[13056]{0:T(1024)(128)(2,1)S(1)} %dynamic-update-slice), channel_id=1, replica_groups=mesh['rep'=4,'fsdp'=8] {'fsdp'}, use_global_device_ids=true, to_apply=%add | all-reduce | flops 13056 | bytes 52224
  63.8 28.7 %all-gather.10.cloned.1.call-done = bf16[768,3072]{1,0:T(8,128)(2,1)} async-done(((bf16[96,3072]{1,0:T(8,128)(2,1)}), bf16[768,3072]{1,0:T(8,128)(2,1)}) %all-gather.10.cloned.1.call-update) | async-done | bytes 4718608 | tf_op jit(solution)/shard_map/all_gather | solution.py:69
  92.6 11.6 %multiply_convert_fusion.4 = (bf16[256,3072]{1,0:T(8,128)(2,1)S(1)}, f32[256,3072]{1,0:T(8,128)}, f32[256,3072]{1,0:T(8,128)}) fusion(f32[3072]{0:T(1024)S(1)} %slice_convert_fusion.6, bf16[768,3072]{1,0:T(8,128)(2,1)} %all-gather.10.cloned.1.call-done, f32[256,768]{1,0:T(8,128)S(1)} %get-tuple-element.145, f32[768]{0:T(1024)S(1)} %get-tuple-element.133, ...), kind=kOutput, calls=%fused_computation.52 | convolution fusion | flops 1260847104 | bytes 13389824 | tf_op jit(solution)/shard_map/dot_general | solution.py:31
  104.2 29.2 %all-gather.12.cloned.1.call-done = bf16[3072,768]{1,0:T(8,128)(2,1)} async-done(((bf16[384,768]{1,0:T(8,128)(2,1)}), bf16[3072,768]{1,0:T(8,128)(2,1)}) %all-gather.12.cloned.1.call-update) | async-done | bytes 4718608 | tf_op jit(solution)/shard_map/all_gather | solution.py:70
  137.8 56.3 %all-gather.14.cloned.1.call-done = bf16[768,6144]{1,0:T(8,128)(2,1)} async-done(((bf16[96,6144]{1,0:T(8,128)(2,1)}), bf16[768,6144]{1,0:T(8,128)(2,1)}) %all-gather.14.cloned.1.call-update) | async-done | bytes 9437200 | tf_op jit(solution)/shard_map/all_gather | solution.py:67
  214.9 4.8 fusion.203
  224.4 10.3 %all-gather.16.cloned.1.call-done = bf16[768,3072]{1,0:T(8,128)(2,1)} async-done(((bf16[96,3072]{1,0:T(8,128)(2,1)}), bf16[768,3072]{1,0:T(8,128)(2,1)}) %all-gather.16.cloned.1.call-update) | async-done | bytes 4718608 | tf_op jit(solution)/shard_map/all_gather | solution.py:69
  234.7 12.0 %multiply_convert_fusion.3 = (bf16[256,3072]{1,0:T(8,128)(2,1)}, f32[256,3072]{1,0:T(8,128)}, f32[256,3072]{1,0:T(8,128)}) fusion(f32[3072]{0:T(1024)} %slice_convert_fusion.5, bf16[768,3072]{1,0:T(8,128)(2,1)} %all-gather.16.cloned.1.call-done, f32[256,768]{1,0:T(8,128)S(1)} %get-tuple-element.156, f32[768]{0:T(1024)S(1)} %get-tuple-element.120, ...), kind=kOutput, calls=%fused_computation.35 | convolution fusion | flops 1260847104 | bytes 13389824 | tf_op jit(solution)/shard_map/dot_general | solution.py:31
  246.7 28.7 %all-gather.18.cloned.1.call-done = bf16[3072,768]{1,0:T(8,128)(2,1)} async-done(((bf16[384,768]{1,0:T(8,128)(2,1)}), bf16[3072,768]{1,0:T(8,128)(2,1)}) %all-gather.18.cloned.1.call-update) | async-done | bytes 4718608 | tf_op jit(solution)/shard_map/all_gather | solution.py:70
  299.3 6.6 fusion.112
  310.1 6.2 fusion.212
  330.5 6.6 fusion.109
  337.1 7.2 fusion.194
  350.8 6.7 copy.160
  357.8 7.2 fusion.190
  375.0 6.7 fusion.106
  381.7 7.2 fusion.192
  402.2 12.7 %copy.162 = bf16[768,6144]{1,0:T(8,128)(2,1)} copy(bf16[768,6144]{0,1:T(8,128)(2,1)} %fusion.80) | data formatting | bytes 18874368
  415.0 5.2 convolution_convert_fusion.4
  421.5 5.6 convolution_convert_fusion.3
  427.8 5.4 convolution_convert_fusion.1
  434.4 5.1 convolution_convert_fusion
  441.8 50.2 %reduce-scatter.21.cloned.1.call-done = bf16[96,6144]{1,0:T(8,128)(2,1)} async-done(((bf16[768,6144]{1,0:T(8,128)(2,1)}), bf16[96,6144]{1,0:T(8,128)(2,1)}) %reduce-scatter.21.cloned.1.call-update) | async-done | bytes 1179664
  494.5 55.3 %reduce-scatter.11.cloned.1.call-done = bf16[96,3072]{1,0:T(8,128)(2,1)} async-done(((bf16[768,3072]{1,0:T(8,128)(2,1)}), bf16[96,3072]{1,0:T(8,128)(2,1)}) %reduce-scatter.11.cloned.1.call-update) | async-done | bytes 589840 | tf_op jit(solution)/shard_map/reduce_scatter | solution.py:91
  549.8 57.2 %reduce-scatter.13.cloned.1.call-done = bf16[384,768]{1,0:T(8,128)(2,1)} async-done(((bf16[3072,768]{1,0:T(8,128)(2,1)}), bf16[384,768]{1,0:T(8,128)(2,1)}) %reduce-scatter.13.cloned.1.call-update) | async-done | bytes 589840 | tf_op jit(solution)/shard_map/reduce_scatter | solution.py:94
  607.0 57.8 %reduce-scatter.15.cloned.1.call-done = bf16[96,3072]{1,0:T(8,128)(2,1)} async-done(((bf16[768,3072]{1,0:T(8,128)(2,1)}), bf16[96,3072]{1,0:T(8,128)(2,1)}) %reduce-scatter.15.cloned.1.call-update) | async-done | bytes 589840 | tf_op jit(solution)/shard_map/reduce_scatter | solution.py:91
  664.7 57.2 %reduce-scatter.17.cloned.1.call-done = bf16[384,768]{1,0:T(8,128)(2,1)} async-done(((bf16[3072,768]{1,0:T(8,128)(2,1)}), bf16[384,768]{1,0:T(8,128)(2,1)}) %reduce-scatter.17.cloned.1.call-update) | async-done | bytes 589840 | tf_op jit(solution)/shard_map/reduce_scatter | solution.py:94
  736.6 25.1 %all-reduce.3 = (bf16[9216]{0:T(1024)(128)(2,1)S(1)}, bf16[13056]{0:T(1024)(128)(2,1)S(1)}) all-reduce(bf16[9216]{0:T(1024)(128)(2,1)S(1)} %pad_maximum_fusion.11, bf16[13056]{0:T(1024)(128)(2,1)S(1)} %pad_maximum_fusion.10), channel_id=3, replica_groups=mesh['rep'=4,'fsdp'=8] {'fsdp'}, use_global_device_ids=true, to_apply=%region_42.43.clone | all-reduce | flops 22272 | bytes 89088
  761.9 12.9 %all-reduce.4 = (bf16[1152]{0:T(1024)(128)(2,1)S(1)}, bf16[1632]{0:T(1024)(128)(2,1)S(1)}) all-reduce(bf16[1152]{0:T(1024)(128)(2,1)S(1)} %dynamic-slice.2, bf16[1632]{0:T(1024)(128)(2,1)S(1)} %dynamic-slice.4), channel_id=1, replica_groups=mesh['rep'=4,'fsdp'=8] {'rep'}, use_global_device_ids=true, to_apply=%region_43.44 | all-reduce | flops 2784 | bytes 11136 | tf_op jit(solution)/shard_map/psum | solution.py:100
  776.0 4.6 fusion.97
  784.6 115.3 %all-reduce.8.cloned.1.call-done = (bf16[96,3072]{0,1:T(8,128)(2,1)}, bf16[96,6144]{0,1:T(8,128)(2,1)}, bf16[96,3072]{1,0:T(8,128)(2,1)}, bf16[384,768]{1,0:T(8,...) async-done(((bf16[96,3072]{0,1:T(8,128)(2,1)}, bf16[96,6144]{0,1:T(8,128)(2,1)}, bf16[96,3072]{1,0:T(8,128)(2,1)}, bf16[384,768]{1,0:T(8,128)(2,1)}, ...) | async-done | bytes 4128784 | tf_op jit(solution)/shard_map/psum | solution.py:99
  (422 shorter events, 158.3 us)
Async XLA Ops:
  7.2 14.8 %copy-start.97 = (u32[32]{0:T(128)S(1)}, u32[32]{0:T(128)}, u32[]{:S(2)}) copy-start(u32[32]{0:T(128)} %constant.119) | copy-start | bytes 388
  7.2 16.1 %copy-start.93 = (bf16[1632]{0:T(1024)(128)(2,1)S(1)}, bf16[1632]{0:T(1024)(128)(2,1)}, u32[]{:S(2)}) copy-start(bf16[1632]{0:T(1024)(128)(2,1)} %param.25) | copy-start | bytes 9796
  7.2 41.9 %copy-start.98 = (s32[1,4]{1,0:T(1,128)S(1)}, s32[1,4]{1,0:T(1,128)}, u32[]{:S(2)}) copy-start(s32[1,4]{1,0:T(1,128)} %param.19) | copy-start | bytes 52
  7.2 41.9 %copy-start.99 = (s32[1,4]{1,0:T(1,128)S(1)}, s32[1,4]{1,0:T(1,128)}, u32[]{:S(2)}) copy-start(s32[1,4]{1,0:T(1,128)} %param.18) | copy-start | bytes 52
  7.2 44.6 %copy-start.100 = (bf16[256,768]{1,0:T(8,128)(2,1)S(1)}, bf16[256,768]{1,0:T(8,128)(2,1)}, u32[]{:S(2)}) copy-start(bf16[256,768]{1,0:T(8,128)(2,1)} %param.15) | copy-start | bytes 1179652
  7.2 44.5 %all-gather.8.cloned.1.call-start = ((), (), s32[]{:S(2)}) async-start(), calls=%async_computation.6 | async-start | bytes 5308416 | tf_op jit(solution)/shard_map/all_gather | solution.py:67
  8.0 84.6 %all-gather.10.cloned.1.call-start = ((), (), s32[]{:S(2)}) async-start(), calls=%async_computation.7 | async-start | bytes 5308416 | tf_op jit(solution)/shard_map/all_gather | solution.py:69
  8.7 124.7 %all-gather.12.cloned.1.call-start = ((), (), s32[]{:S(2)}) async-start(), calls=%async_computation.8 | async-start | bytes 5308416 | tf_op jit(solution)/shard_map/all_gather | solution.py:70
  9.5 184.6 %all-gather.14.cloned.1.call-start = ((), (), s32[]{:S(2)}) async-start(), calls=%async_computation.9 | async-start | bytes 10616832 | tf_op jit(solution)/shard_map/all_gather | solution.py:67
  10.0 224.7 %all-gather.16.cloned.1.call-start = ((), (), s32[]{:S(2)}) async-start(), calls=%async_computation.10 | async-start | bytes 5308416 | tf_op jit(solution)/shard_map/all_gather | solution.py:69
  10.6 264.8 %all-gather.18.cloned.1.call-start = ((), (), s32[]{:S(2)}) async-start(), calls=%async_computation.11 | async-start | bytes 5308416 | tf_op jit(solution)/shard_map/all_gather | solution.py:70
  11.2 428.4 %reduce-scatter.19.cloned.1.call-start = ((), (), s32[]{:S(2)}) async-start(), calls=%async_computation.16 | async-start | bytes 5308416
  48.3 89.2 %copy-start.41 = (f32[768]{0:T(1024)}, f32[768]{0:T(1024)S(1)}, u32[]{:S(2)}) copy-start(f32[768]{0:T(1024)S(1)} %get-tuple-element.130) | copy-start | bytes 9220
  63.6 69.8 %copy-start.46 = (f32[256]{0:T(256)}, f32[256]{0:T(256)S(1)}, u32[]{:S(2)}) copy-start(f32[256]{0:T(256)S(1)} %broadcast_multiply_fusion.4) | copy-start | bytes 3076
  63.8 40.4 %copy-start.77 = (f32[256]{0:T(256)}, f32[256]{0:T(256)S(1)}, u32[]{:S(2)}) copy-start(f32[256]{0:T(256)S(1)} %multiply_reduce_fusion.15) | copy-start | bytes 3076
  63.8 69.6 %copy-start.60 = (f32[256]{0:T(256)}, f32[256]{0:T(256)S(1)}, u32[]{:S(2)}) copy-start(f32[256]{0:T(256)S(1)} %fusion.157) | copy-start | bytes 3076
  104.2 33.1 %copy-start.10 = (bf16[256,3072]{1,0:T(8,128)(2,1)}, bf16[256,3072]{1,0:T(8,128)(2,1)S(1)}, u32[]{:S(2)}) copy-start(bf16[256,3072]{1,0:T(8,128)(2,1)S(1)} %get-tuple-element.98) | copy-start | bytes 4718596
  137.3 60.0 %copy-start.53 = (f32[256]{0:T(256)}, f32[256]{0:T(256)S(1)}, u32[]{:S(2)}) copy-start(f32[256]{0:T(256)S(1)} %broadcast_multiply_fusion.3) | copy-start | bytes 3076
  137.5 59.8 %copy-start.81 = (f32[256]{0:T(256)}, f32[256]{0:T(256)S(1)}, u32[]{:S(2)}) copy-start(f32[256]{0:T(256)S(1)} %multiply_reduce_fusion.14) | copy-start | bytes 3076
  137.5 59.8 %copy-start.75 = (f32[256]{0:T(256)}, f32[256]{0:T(256)S(1)}, u32[]{:S(2)}) copy-start(f32[256]{0:T(256)S(1)} %fusion.158) | copy-start | bytes 3076
  137.7 59.6 %copy-start.32 = (bf16[256,768]{1,0:T(8,128)(2,1)}, bf16[256,768]{1,0:T(8,128)(2,1)S(1)}, u32[]{:S(2)}) copy-start(bf16[256,768]{1,0:T(8,128)(2,1)S(1)} %add_convert_fusion.3) | copy-start | bytes 1179652
  224.1 22.6 %copy-start.48 = (f32[256]{0:T(256)}, f32[256]{0:T(256)S(1)}, u32[]{:S(2)}) copy-start(f32[256]{0:T(256)S(1)} %broadcast_multiply_fusion.1) | copy-start | bytes 3076
  224.3 22.4 %copy-start.83 = (f32[256]{0:T(256)}, f32[256]{0:T(256)S(1)}, u32[]{:S(2)}) copy-start(f32[256]{0:T(256)S(1)} %multiply_reduce_fusion.12) | copy-start | bytes 3076
  224.4 22.3 %copy-start.62 = (f32[256]{0:T(256)}, f32[256]{0:T(256)S(1)}, u32[]{:S(2)}) copy-start(f32[256]{0:T(256)S(1)} %fusion.160) | copy-start | bytes 3076
  357.5 134.5 %reduce-scatter.21.cloned.1.call-start = ((), (), s32[]{:S(2)}) async-start(), calls=%async_computation.17 | async-start | bytes 10616832
  415.0 134.8 %reduce-scatter.11.cloned.1.call-start = ((), (), s32[]{:S(2)}) async-start(), calls=%async_computation.12 | async-start | bytes 5308416 | tf_op jit(solution)/shard_map/reduce_scatter | solution.py:91
  420.2 186.8 %reduce-scatter.13.cloned.1.call-start = ((), (), s32[]{:S(2)}) async-start(), calls=%async_computation.13 | async-start | bytes 5308416 | tf_op jit(solution)/shard_map/reduce_scatter | solution.py:94
  427.1 237.6 %reduce-scatter.15.cloned.1.call-start = ((), (), s32[]{:S(2)}) async-start(), calls=%async_computation.14 | async-start | bytes 5308416 | tf_op jit(solution)/shard_map/reduce_scatter | solution.py:91
  433.2 288.7 %reduce-scatter.17.cloned.1.call-start = ((), (), s32[]{:S(2)}) async-start(), calls=%async_computation.15 | async-start | bytes 5308416 | tf_op jit(solution)/shard_map/reduce_scatter | solution.py:94
  439.5 460.4 %all-reduce.8.cloned.1.call-start = ((), (), s32[]{:S(2)}) async-start(), calls=%async_computation.18 | async-start | bytes 9437184 | tf_op jit(solution)/shard_map/psum | solution.py:99
  494.5 231.7 %copy-start.66 = (f32[256]{0:T(256)S(1)}, f32[256]{0:T(256)}, u32[]{:S(2)}) copy-start(f32[256]{0:T(256)} %copy-done.65) | copy-start | bytes 3076
  722.6 13.9 %copy-start.91 = (bf16[3072]{0:T(1024)(128)(2,1)S(1)}, bf16[3072]{0:T(1024)(128)(2,1)}, u32[]{:S(2)}) copy-start(bf16[3072]{0:T(1024)(128)(2,1)} %get-tuple-element.172) | copy-start | bytes 18436
  (102 other events, 398.8 us)
Sparse Core Ops, SparseCore 0:
  10.0 41.7 all-gather.7
  53.7 38.8 all-gather.9
  94.5 38.9 all-gather.11
  135.2 58.8 all-gather.13
  195.8 38.9 all-gather.15
  236.5 38.9 all-gather.17
  357.7 53.8 reduce-scatter.18
  415.5 76.4 reduce-scatter.20
  495.8 53.8 reduce-scatter.10
  553.1 53.8 reduce-scatter.12
  610.8 53.8 reduce-scatter.14
  668.0 53.8 reduce-scatter.16
  725.6 174.2 all-reduce.7
where the time goes:
time: 926 us; the launch traced here: 917 us
  waiting for transfers between devices  551 us (60%)
  matrix products  199 us (21%)
  blocking collectives  72.6 us (8%)
  local copies, waits for them, and re-layouts  55.4 us (6%)
  other arithmetic  19.1 us (2%)
  between operations  18.4 us (2%)
    psum x1, waiting for transfers between devices, reduce_grads(): lax.psum(shard[0].astype(jnp.bfloat16), 'rep').astype(jnp.float32)  115 us
    reduce_scatter x2, waiting for transfers between devices, reduce_grads(): lax.psum_scatter(grad_out.astype(jnp.bfloat16), 'fsdp', scatter_dimension...  114 us
    reduce_scatter x2, waiting for transfers between devices, reduce_grads(): lax.psum_scatter(grad_in.astype(jnp.bfloat16), 'fsdp', scatter_dimension=...  113 us
    all_gather x2, waiting for transfers between devices, fetch(): lax.all_gather(w_out, 'fsdp', axis=0, tiled=True)  57.9 us
    all_gather x2, waiting for transfers between devices, fetch(): lax.all_gather(attn_rows, 'fsdp', axis=0, tiled=True)  57.2 us
    unnamed x15, waiting for transfers between devices  54 us
    unnamed x2, blocking collectives  49.2 us
    dot_general x11, matrix products, dot_plain(): return jnp.dot(first_op, second_op, preferred_element_type=jnp.float32)  48.5 us
  transfers between devices with their start and end apart: 13, of which 12 were waited for; matrix products, arithmetic and copies ran while one was open for 19% of the time, Pallas kernels for 0%

commit v1 on v0

--- a/solution.py
+++ b/solution.py
@@ -1,9 +1,14 @@
+import functools
+
 import jax
 import jax.numpy as jnp
 from jax import lax
+from jax.experimental import pallas as pl
+from jax.experimental.pallas import tpu as pltpu
 from jax.sharding import PartitionSpec as P
 
 HEAD = 64
+ROW_TILE = 16
 
 
 EPSILON = 1e-05
@@ -63,15 +68,6 @@
 
 
 def fetch(attn_rows, vec_part, w_in, w_out):
-    return (
-        lax.all_gather(attn_rows, "fsdp", axis=0, tiled=True),
-        lax.all_gather(vec_part, "fsdp", axis=0, tiled=True),
-        lax.all_gather(w_in, "fsdp", axis=0, tiled=True),
-        lax.all_gather(w_out, "fsdp", axis=0, tiled=True),
-    )
-
-
-def fetch_again(attn_rows, vec_part, w_in, w_out):
     return (
         lax.all_gather(attn_rows, "fsdp", axis=0, tiled=True),
         lax.all_gather(vec_part, "fsdp", axis=0, tiled=True),
@@ -101,6 +97,201 @@
         lax.psum(shard[2].astype(jnp.bfloat16), "rep").astype(jnp.float32),
         lax.psum(shard[3].astype(jnp.bfloat16), "rep").astype(jnp.float32),
     )
+
+
+def swap(value, bit):
+    return lax.ppermute(value, "fsdp", [(i, i ^ bit) for i in range(8)])
+
+
+def tile_up(rows):
+    return -(-rows // ROW_TILE) * ROW_TILE
+
+
+def piece_plan(shards, feature):
+    plan = []
+    offset = 0
+    for index, (rows, columns) in enumerate(shards):
+        for block in range(columns // feature):
+            plan.append((index, rows, block, offset))
+            offset += rows
+    return (plan, offset)
+
+
+def pack_shards(shards, feature):
+    parts = []
+    for shard in shards:
+        for block in range(shard.shape[1] // feature):
+            parts.append(shard[:, block * feature : (block + 1) * feature])
+    return jnp.concatenate(parts, axis=0)
+
+
+def vec_rows(vec_part, feature):
+    rows = tile_up(-(-vec_part.shape[0] // feature))
+    padded = jnp.pad(vec_part, (0, rows * feature - vec_part.shape[0]))
+    return padded.reshape(rows, feature)
+
+
+def gather_piece(packed):
+    cut = tile_up(packed.shape[0] // 2)
+    from_x = swap(packed, 2)
+    from_y = swap(packed, 4)
+    corner_top = swap(from_x[:cut], 4)
+    corner_low = swap(from_y[cut:], 2)
+    mine = [packed, from_x, from_y, corner_top, corner_low]
+    return mine + [swap(value, 1) for value in mine]
+
+
+def unpack_body(plan, cut, table, *refs):
+    sources, outs, sems = refs[:10], refs[10:-1], refs[-1]
+    copies = []
+
+    def add(source, first, count, out, row, column):
+        feature = source.shape[1]
+        copies.append(
+            pltpu.make_async_copy(
+                source.at[pl.ds(first, count), :],
+                out.at[pl.ds(row, count), pl.ds(column * feature, feature)],
+                sems.at[len(copies)],
+            )
+        )
+
+    for core in range(2):
+        group = sources[5 * core : 5 * core + 5]
+        for chip in range(4):
+            place = table[2 * chip + core]
+            for index, rows, block, offset in plan:
+                row = pl.multiple_of(place * rows, ROW_TILE)
+                if chip < 3:
+                    add(group[chip], offset, rows, outs[index], row, block)
+                    continue
+                top = max(0, min(cut - offset, rows))
+                if top > 0:
+                    add(group[3], offset, top, outs[index], row, block)
+                if top < rows:
+                    row = pl.multiple_of(row + top, ROW_TILE)
+                    add(group[4], offset + top - cut, rows - top, outs[index], row, block)
+    for copy in copies:
+        copy.start()
+    for copy in copies:
+        copy.wait()
+
+
+def unpack_piece(sources, table, shards, feature):
+    plan, total = piece_plan(shards, feature)
+    cut = tile_up(total // 2)
+    return pl.pallas_call(
+        functools.partial(unpack_body, plan, cut),
+        out_shape=[
+            jax.ShapeDtypeStruct((8 * rows, columns), jnp.bfloat16) for rows, columns in shards
+        ],
+        in_specs=[pl.BlockSpec(memory_space=pltpu.SMEM)] + [pl.BlockSpec(memory_space=pl.ANY)] * 10,
+        out_specs=[pl.BlockSpec(memory_space=pl.ANY)] * len(shards),
+        scratch_shapes=[pltpu.SemaphoreType.DMA((8 * len(plan) + 2,))],
+    )(table, *sources)
+
+
+def pack_body(plan, count, table, *refs):
+    sources, keep, send, sems = refs[:count], refs[count], refs[count + 1], refs[-1]
+    copies = []
+    for core, out in ((1, send), (0, keep)):
+        for chip in range(4):
+            place = table[2 * chip + core]
+            for index, rows, block, offset in plan:
+                feature = out.shape[2]
+                row = pl.multiple_of(place * rows, ROW_TILE)
+                copies.append(
+                    pltpu.make_async_copy(
+                        sources[index].at[pl.ds(row, rows), pl.ds(block * feature, feature)],
+                        out.at[chip, pl.ds(offset, rows), :],
+                        sems.at[len(copies)],
+                    )
+                )
+    for copy in copies:
+        copy.start()
+    for copy in copies:
+        copy.wait()
+
+
+def pack_piece(grads, table, feature):
+    shards = [(grad.shape[0] // 8, grad.shape[1]) for grad in grads]
+    plan, total = piece_plan(shards, feature)
+    out = jax.ShapeDtypeStruct((4, total, feature), jnp.bfloat16)
+    keep, send = pl.pallas_call(
+        functools.partial(pack_body, plan, len(grads)),
+        out_shape=[out, out],
+        in_specs=[pl.BlockSpec(memory_space=pltpu.SMEM)]
+        + [pl.BlockSpec(memory_space=pl.ANY)] * len(grads),
+        out_specs=[pl.BlockSpec(memory_space=pl.ANY)] * 2,
+        scratch_shapes=[pltpu.SemaphoreType.DMA((8 * len(plan),))],
+    )(table, *grads)
+    return (keep, send, plan)
+
+
+def add_low(*terms):
+    total = terms[0].astype(jnp.float32)
+    for term in terms[1:]:
+        total = total + term.astype(jnp.float32)
+    return total.astype(jnp.bfloat16)
+
+
+def line_sum(value):
+    place = lax.axis_index("rep")
+    inner = (place == 1) | (place == 2)
+    inward = lax.ppermute(value, "rep", [(0, 1), (3, 2)])
+    half = add_low(value, inward)
+    total = add_low(half, lax.ppermute(half, "rep", [(1, 2), (2, 1)]))
+    outward = lax.ppermute(total, "rep", [(1, 0), (2, 3)])
+    return jnp.where(inner, total, outward)
+
+
+def reduce_piece(grads, table, feature):
+    keep, send, plan = pack_piece(grads, table, feature)
+    full = add_low(keep, swap(send, 1))
+    cut = tile_up(full.shape[1] // 2)
+    low_x = swap(full[3, :cut], 2)
+    low_y = swap(full[3, cut:], 4)
+    to_x = jnp.concatenate([full[1, :cut], add_low(full[1, cut:], low_y)], axis=0)
+    to_y = jnp.concatenate([add_low(full[2, :cut], low_x), full[2, cut:]], axis=0)
+    own = add_low(full[0], swap(to_x, 2), swap(to_y, 4))
+    own = line_sum(own).astype(jnp.float32)
+    results = []
+    for index in range(len(grads)):
+        blocks = [own[offset : offset + rows] for which, rows, block, offset in plan if which == index]
+        results.append(jnp.concatenate(blocks, axis=1))
+    return results
+
+
+def fetch_pieces(attn_rows, vec_part, w_in, w_out, table):
+    feature = w_out.shape[1]
+    vec_block = vec_rows(vec_part, feature)
+    first = pack_shards([attn_rows, vec_block], feature)
+    second = pack_shards([w_in, w_out], feature)
+    attn, vec = unpack_piece(
+        gather_piece(first), table, [attn_rows.shape, vec_block.shape], feature
+    )
+    w_in_all, w_out_all = unpack_piece(
+        gather_piece(second), table, [w_in.shape, w_out.shape], feature
+    )
+    vec = vec.reshape(8, -1)[:, : vec_part.shape[0]].reshape(-1)
+    return (attn, vec, w_in_all, w_out_all)
+
+
+def reduce_vec(grad_vec, feature):
+    parts = grad_vec.astype(jnp.bfloat16).reshape(8, -1)
+    rows = tile_up(-(-parts.shape[1] // feature))
+    return jnp.pad(parts, ((0, 0), (0, rows * feature - parts.shape[1]))).reshape(8 * rows, feature)
+
+
+def reduce_pieces(grad_attn, grad_vec, grad_in, grad_out, table):
+    feature = grad_out.shape[1]
+    w_in, w_out = reduce_piece(
+        [grad_in.astype(jnp.bfloat16), grad_out.astype(jnp.bfloat16)], table, feature
+    )
+    attn, vec = reduce_piece(
+        [grad_attn.astype(jnp.bfloat16), reduce_vec(grad_vec, feature)], table, feature
+    )
+    vec = vec.reshape(-1)[: grad_vec.shape[0] // 8]
+    return (attn, vec, w_in, w_out)
 
 
 def attend(q_in, kv_in, weights, biases, key_mask, one_source):
@@ -192,6 +383,8 @@
 
 
 def per_device(
+    fsdp_size,
+    rep_size,
     enc_in,
     dec_in,
     bucket,
@@ -212,7 +405,14 @@
     enc_mask, self_mask, cross_mask = build_masks(
         bucket[0], enc_lengths[0], dec_lengths[0], row_total, enc_lengths.shape[1]
     )
-    enc_weights = fetch(enc_attn, enc_vec, enc_w1, enc_w2)
+    small = fsdp_size == 8 and rep_size == 4
+    if small:
+        table = lax.axis_index("fsdp").astype(jnp.int32) ^ jnp.arange(8, dtype=jnp.int32)
+        enc_weights = fetch_pieces(enc_attn, enc_vec, enc_w1, enc_w2, table)
+        dec_weights = fetch_pieces(dec_attn, dec_vec, dec_w1, dec_w2, table)
+    else:
+        enc_weights = fetch(enc_attn, enc_vec, enc_w1, enc_w2)
+        dec_weights = fetch(dec_attn, dec_vec, dec_w1, dec_w2)
     e_attn, e_vec, e_in, e_out = enc_weights
     e_rows, e_tail = unpack(e_vec, 8, feature)
     branch, e_saved_a = attend(enc_in, enc_in, e_attn, e_rows[0:3], enc_mask, True)
@@ -221,7 +421,6 @@
     branch, e_saved_f = feed(e_first, e_in, e_tail, e_out, e_rows[5])
     e_hid_f = e_first.astype(jnp.float32) + branch
     encoded = norm_rows(e_hid_f, e_rows[6], e_rows[7]).astype(jnp.bfloat16)
-    dec_weights = fetch(dec_attn, dec_vec, dec_w1, dec_w2)
     d_attn, d_vec, d_in, d_out = dec_weights
     d_rows, d_tail = unpack(d_vec, 13, feature)
     branch, d_saved_s = attend(
@@ -237,9 +436,6 @@
     branch, d_saved_f = feed(d_second, d_in, d_tail, d_out, d_rows[10])
     d_hid_f = d_second.astype(jnp.float32) + branch
     decoded = norm_rows(d_hid_f, d_rows[11], d_rows[12]).astype(jnp.bfloat16)
-    dec_weights = fetch_again(dec_attn, dec_vec, dec_w1, dec_w2)
-    d_attn, d_vec, d_in, d_out = dec_weights
-    d_rows, d_tail = unpack(d_vec, 13, feature)
     gradient, grad_g11, grad_n12 = norm_back(
         d_hid_f, d_rows[11], d_rows[12], dec_cot.astype(jnp.float32)
     )
@@ -273,12 +469,11 @@
         ]
     )
     dec_vec_full = jnp.concatenate([dec_stack.reshape(-1), grad_d_tail])
-    dec_shards = reduce_grads(
-        jnp.concatenate([grad_self, grad_cross], axis=1), dec_vec_full, grad_d_in, grad_d_out
-    )
-    enc_weights = fetch_again(enc_attn, enc_vec, enc_w1, enc_w2)
-    e_attn, e_vec, e_in, e_out = enc_weights
-    e_rows, e_tail = unpack(e_vec, 8, feature)
+    grad_d_attn = jnp.concatenate([grad_self, grad_cross], axis=1)
+    if small:
+        dec_shards = reduce_pieces(grad_d_attn, dec_vec_full, grad_d_in, grad_d_out, table)
+    else:
+        dec_shards = reduce_grads(grad_d_attn, dec_vec_full, grad_d_in, grad_d_out)
     gradient, grad_g6, grad_n7 = norm_back(
         e_hid_f, e_rows[6], e_rows[7], enc_cot.astype(jnp.float32) + grad_encoded
     )
@@ -294,7 +489,10 @@
         [enc_bias[0], enc_bias[1], enc_bias[2], grad_g3e, grad_n4e, grad_b5, grad_g6, grad_n7]
     )
     enc_vec_full = jnp.concatenate([enc_stack.reshape(-1), grad_e_tail])
-    enc_shards = reduce_grads(grad_e_attn, enc_vec_full, grad_e_in, grad_e_out)
+    if small:
+        enc_shards = reduce_pieces(grad_e_attn, enc_vec_full, grad_e_in, grad_e_out, table)
+    else:
+        enc_shards = reduce_grads(grad_e_attn, enc_vec_full, grad_e_in, grad_e_out)
     return (
         encoded,
         decoded,
@@ -344,5 +542,5 @@
         P("fsdp", None),
     )
     return jax.shard_map(
-        per_device, mesh=mesh, in_specs=in_specs, out_specs=out_specs, check_vma=False
-    )
+        functools.partial(per_device, mesh.shape["fsdp"], mesh.shape["rep"]), mesh=mesh, in_specs=in_specs, out_specs=out_specs, check_vma=False
+    )

time: 926 us -> 2720 us (2.94)
  Pallas kernels: 0 us -> 2040 us
  waiting for transfers between devices: 551 us -> 287 us
  blocking collectives: 72.6 us -> 0 us
  starting transfers between devices: 0.98 us -> 62.7 us
  other arithmetic: 19.1 us -> 56.7 us
    pallas_call x0 -> x8, Pallas kernels: none -> 2040 us  [the longest x4 1020 us: pack_piece(): pl.pallas_call(functools.partial(pack_body, plan, len(grads)), out_shape=...]
    ppermute x0 -> x68, waiting for transfers between devices: none -> 287 us  [the longest x56 189 us: swap(): return lax.ppermute(value, 'fsdp', [(i, i ^ bit) for i in range(8)])]
    reduce_scatter x4 -> x0, waiting for transfers between devices: 227 us -> none  [the longest x2 114 us: reduce_grads(): lax.psum_scatter(grad_out.astype(jnp.bfloat16), 'fsdp', scatter_dimension...]
    all_gather x6 -> x0, waiting for transfers between devices: 154 us -> none  [the longest x2 57.9 us: fetch(): lax.all_gather(w_out, 'fsdp', axis=0, tiled=True)]
    psum x1 -> x0, waiting for transfers between devices: 115 us -> none  [reduce_grads(): lax.psum(shard[0].astype(jnp.bfloat16), 'rep').astype(jnp.float32)]
    ppermute x0 -> x68, starting transfers between devices: none -> 62.7 us  [the longest x56 42.8 us: swap(): return lax.ppermute(value, 'fsdp', [(i, i ^ bit) for i in range(8)])]
    unnamed x15 -> x0, waiting for transfers between devices: 54 us -> none
    unnamed x2 -> x0, blocking collectives: 49.2 us -> none
  transfers between devices with their start and end apart: 13 -> 68, of which waited for: 12 -> 25; matrix products, arithmetic and copies ran while one was open for 19% -> 5% of each run, Pallas kernels for 0% -> 59%
where the time goes in v1:
time: 2720 us; the launch traced here: 2710 us
  Pallas kernels  2040 us (75%)
  waiting for transfers between devices  287 us (11%)
  matrix products  187 us (7%)
  local copies, waits for them, and re-layouts  66.9 us (2%)
  starting transfers between devices  62.7 us (2%)
  other arithmetic  56.7 us (2%)
    pallas_call x4, Pallas kernels, pack_piece(): pl.pallas_call(functools.partial(pack_body, plan, len(grads)), out_shape=...  1020 us
    pallas_call x4, Pallas kernels, unpack_piece(): pl.pallas_call(functools.partial(unpack_body, plan, cut), out_shape=[jax....  1020 us
    ppermute x56, waiting for transfers between devices, swap(): return lax.ppermute(value, 'fsdp', [(i, i ^ bit) for i in range(8)])  189 us
    ppermute x4, waiting for transfers between devices, line_sum(): outward = lax.ppermute(total, 'rep', [(1, 0), (2, 3)])  64.8 us
  transfers between devices with their start and end apart: 68, of which 25 were waited for; matrix products, arithmetic and copies ran while one was open for 5% of the time, Pallas kernels for 59%

profile of v1, /device:TPU:0, one launch (start us, length us, event | category | flops | bytes accessed | tf_op | source)
XLA Modules:
  0.0 2707.1 jit_solution(15753605854673998312)
XLA Ops:
  36.2 46.1 %collective-permute-done.3.refs_4_ = bf16[192,768]{1,0:T(8,128)(2,1)} collective-permute-done((bf16[192,768]{1,0:T(8,128)(2,1)S(1)}, bf16[192,768]{1,0:T(8,128)(2,1)}, u32[]{:S(2)}, u32[]{:S(2)}) %collective-permute-start.3) | collective-permute-done | bytes 294944 | tf_op jit(solution)/shard_map/ppermute | solution.py:103
  96.5 21.6 collective-permute-done.18.refs_1_
  133.7 151.0 %shard_map.238 = (bf16[768,3072]{1,0:T(8,128)(2,1)}, bf16[128,768]{1,0:T(8,128)(2,1)}) custom-call(s32[8]{0:T(128)} %iota_xor_fusion.table, bf16[400,768]{1,0:T(8,128)(2,1)} %constant_dynamic-update-slice_fusion.refs_0_, bf16[400,768]{1,0:T(8,128)(2,1)} %collective-permute-done.refs_1_, bf16[400,768]{1,0:T(8,128)(2,1)} %copy-done.31, ...), custom_call_target="tpu_custom_call" | custom-call | tf_op jit(solution)/shard_map/pallas_call | solution.py:182
  300.8 10.6 collective-permute-done.12.refs_4_
  316.8 288.0 %shard_map.239 = (bf16[768,3072]{1,0:T(8,128)(2,1)}, bf16[3072,768]{1,0:T(8,128)(2,1)}) custom-call(s32[8]{0:T(128)} %iota_xor_fusion.table, bf16[768,768]{1,0:T(8,128)(2,1)} %copy-done.30, bf16[768,768]{1,0:T(8,128)(2,1)} %copy-done.15, bf16[768,768]{1,0:T(8,128)(2,1)} %collective-permute-done.10.refs_2_, bf16[384,768]{1,0:T(8,128)(2,1)} %collective-permute-done.11.refs_3_, ...), custom_call_target="tpu_custom_call" | custom-call | tf_op jit(solution)/shard_map/pallas_call | solution.py:182
  607.1 11.5 multiply_convert_fusion.4
  622.4 288.0 %shard_map.241 = (bf16[768,3072]{1,0:T(8,128)(2,1)}, bf16[3072,768]{1,0:T(8,128)(2,1)}) custom-call(s32[8]{0:T(128)} %iota_xor_fusion.table, bf16[768,768]{1,0:T(8,128)(2,1)} %constant_dynamic-update-slice_fusion.3.refs_0_, bf16[768,768]{1,0:T(8,128)(2,1)} %collective-permute-done.27.refs_1_, bf16[768,768]{1,0:T(8,128)(2,1)} %collective-permute-done.28.refs_2_, ...), custom_call_target="tpu_custom_call" | custom-call | tf_op jit(solution)/shard_map/pallas_call | solution.py:182
  915.4 294.3 %shard_map.240 = (bf16[768,6144]{1,0:T(8,128)(2,1)}, bf16[128,768]{1,0:T(8,128)(2,1)}) custom-call(s32[8]{0:T(128)} %iota_xor_fusion.table, bf16[784,768]{1,0:T(8,128)(2,1)} %constant_dynamic-update-slice_fusion.2.refs_0_, bf16[784,768]{1,0:T(8,128)(2,1)} %collective-permute-done.18.refs_1_, bf16[784,768]{1,0:T(8,128)(2,1)} %collective-permute-done.19.refs_2_, ...), custom_call_target="tpu_custom_call" | custom-call | tf_op jit(solution)/shard_map/pallas_call | solution.py:182
  1244.1 8.5 multiply_convert_fusion.3
  1272.8 7.4 fusion.207
  1280.2 6.7 fusion.116
  1294.2 5.4 fusion.228
  1313.8 6.8 fusion.113
  1320.6 7.1 fusion.211
  1355.2 6.5 fusion.209
  1368.4 151.0 %shard_map.242 = (bf16[4,400,768]{2,1,0:T(8,128)(2,1)}, bf16[4,400,768]{2,1,0:T(8,128)(2,1)}) custom-call(s32[8]{0:T(128)} %iota_xor_fusion.table, bf16[768,3072]{1,0:T(8,128)(2,1)} %pad_maximum_fusion.refs_0_, bf16[128,768]{1,0:T(8,128)(2,1)} %reshape.557.refs_1_), custom_call_target="tpu_custom_call" | custom-call | tf_op jit(solution)/shard_map/pallas_call | solution.py:219
  1520.1 288.0 %shard_map.243 = (bf16[4,768,768]{2,1,0:T(8,128)(2,1)}, bf16[4,768,768]{2,1,0:T(8,128)(2,1)}) custom-call(s32[8]{0:T(128)} %iota_xor_fusion.table, bf16[768,3072]{1,0:T(8,128)(2,1)} %convolution_convert_fusion.4.refs_0_, bf16[3072,768]{1,0:T(8,128)(2,1)} %convolution_convert_fusion.3.refs_1_), custom_call_target="tpu_custom_call" | custom-call | tf_op jit(solution)/shard_map/pallas_call | solution.py:219
  1814.8 288.1 %shard_map.245 = (bf16[4,768,768]{2,1,0:T(8,128)(2,1)}, bf16[4,768,768]{2,1,0:T(8,128)(2,1)}) custom-call(s32[8]{0:T(128)} %iota_xor_fusion.table, bf16[768,3072]{1,0:T(8,128)(2,1)} %convolution_convert_fusion.1.refs_0_, bf16[3072,768]{1,0:T(8,128)(2,1)} %convolution_convert_fusion.refs_1_), custom_call_target="tpu_custom_call" | custom-call | tf_op jit(solution)/shard_map/pallas_call | solution.py:219
  2103.5 6.4 fusion.110
  2121.2 294.2 %shard_map.244 = (bf16[4,784,768]{2,1,0:T(8,128)(2,1)}, bf16[4,784,768]{2,1,0:T(8,128)(2,1)}) custom-call(s32[8]{0:T(128)} %iota_xor_fusion.table, bf16[768,6144]{1,0:T(8,128)(2,1)} %fusion.83.refs_0_, bf16[128,768]{1,0:T(8,128)(2,1)} %reshape.566.refs_1_), custom_call_target="tpu_custom_call" | custom-call | tf_op jit(solution)/shard_map/pallas_call | solution.py:219
  2421.2 6.9 collective-permute-done.37
  2432.3 12.5 collective-permute-done.38
  2480.2 8.3 collective-permute-done.61
  2493.4 7.6 collective-permute-done.53
  2504.9 21.4 collective-permute-done.48
  2529.5 22.1 collective-permute-done.64
  2558.9 17.1 collective-permute-done.54
  2582.3 22.2 collective-permute-done.65
  2612.5 11.2 collective-permute-done.57
  2635.3 26.1 collective-permute-done.51
  2662.7 24.0 collective-permute-done.67
  2690.4 14.6 collective-permute-done.59
  (708 shorter events, 321.5 us)
Async XLA Ops:
  17.7 74.8 %collective-permute-start.9 = (bf16[768,768]{1,0:T(8,128)(2,1)S(1)}, bf16[768,768]{1,0:T(8,128)(2,1)S(1)}, u32[]{:S(2)}, u32[]{:S(2)}) collective-permute-start(bf16[768,768]{1,0:T(8,128)(2,1)S(1)} %constant_dynamic-update-slice_fusion.1.refs_0_), channel_id=1, source_target_pairs={{0,2},{1,3},{2,0},{3,1},{4,6},{5,7},{6,4},{7,5},{8,10},{9,11},{10,... | collective-permute-start | bytes 3538952 | tf_op jit(solution)/shard_map/ppermute | solution.py:103
  18.3 76.6 %collective-permute-start.10 = (bf16[768,768]{1,0:T(8,128)(2,1)S(1)}, bf16[768,768]{1,0:T(8,128)(2,1)}, u32[]{:S(2)}, u32[]{:S(2)}) collective-permute-start(bf16[768,768]{1,0:T(8,128)(2,1)S(1)} %constant_dynamic-update-slice_fusion.1.refs_0_), channel_id=1, source_target_pairs={{0,4},{1,5},{2,6},{3,7},{4,0},{5,1},{6,2},{7,3},{8,12},{9,13},{10,... | collective-permute-start | bytes 3538952 | tf_op jit(solution)/shard_map/ppermute | solution.py:103
  25.5 69.5 %collective-permute-start.27 = (bf16[768,768]{1,0:T(8,128)(2,1)}, bf16[768,768]{1,0:T(8,128)(2,1)}, u32[]{:S(2)}, u32[]{:S(2)}) collective-permute-start(bf16[768,768]{1,0:T(8,128)(2,1)} %constant_dynamic-update-slice_fusion.3.refs_0_), channel_id=1, source_target_pairs={{0,2},{1,3},{2,0},{3,1},{4,6},{5,7},{6,4},{7,5},{8,10},{9,11},{10,... | collective-permute-start | bytes 3538952 | tf_op jit(solution)/shard_map/ppermute | solution.py:103
  31.7 50.7 %collective-permute-start.3 = (bf16[192,768]{1,0:T(8,128)(2,1)S(1)}, bf16[192,768]{1,0:T(8,128)(2,1)}, u32[]{:S(2)}, u32[]{:S(2)}) collective-permute-start(bf16[192,768]{1,0:T(8,128)(2,1)S(1)} %slice.557), channel_id=1, source_target_pairs={{0,2},{1,3},{2,0},{3,1},{4,6},{5,7},{6,4},{7,5},{8,10},{9,11},{10,... | collective-permute-start | bytes 884744 | tf_op jit(solution)/shard_map/ppermute | solution.py:103
  32.5 63.0 %collective-permute-start.28 = (bf16[768,768]{1,0:T(8,128)(2,1)}, bf16[768,768]{1,0:T(8,128)(2,1)}, u32[]{:S(2)}, u32[]{:S(2)}) collective-permute-start(bf16[768,768]{1,0:T(8,128)(2,1)} %constant_dynamic-update-slice_fusion.3.refs_0_), channel_id=1, source_target_pairs={{0,4},{1,5},{2,6},{3,7},{4,0},{5,1},{6,2},{7,3},{8,12},{9,13},{10,... | collective-permute-start | bytes 3538952 | tf_op jit(solution)/shard_map/ppermute | solution.py:103
  130.7 164.9 %collective-permute-start.13 = (bf16[768,768]{1,0:T(8,128)(2,1)S(1)}, bf16[768,768]{1,0:T(8,128)(2,1)}, u32[]{:S(2)}, u32[]{:S(2)}) collective-permute-start(bf16[768,768]{1,0:T(8,128)(2,1)S(1)} %constant_dynamic-update-slice_fusion.1.refs_0_), channel_id=1, source_target_pairs={{0,1},{1,0},{2,3},{3,2},{4,5},{5,4},{6,7},{7,6},{8,9},{9,8},{10,11... | collective-permute-start | bytes 3538952 | tf_op jit(solution)/shard_map/ppermute | solution.py:103
  131.2 473.6 %collective-permute-start.31 = (bf16[768,768]{1,0:T(8,128)(2,1)}, bf16[768,768]{1,0:T(8,128)(2,1)}, u32[]{:S(2)}, u32[]{:S(2)}) collective-permute-start(bf16[768,768]{1,0:T(8,128)(2,1)} %constant_dynamic-update-slice_fusion.3.refs_0_), channel_id=1, source_target_pairs={{0,1},{1,0},{2,3},{3,2},{4,5},{5,4},{6,7},{7,6},{8,9},{9,8},{10,11... | collective-permute-start | bytes 3538952 | tf_op jit(solution)/shard_map/ppermute | solution.py:103
  131.3 164.8 %collective-permute-start.11 = (bf16[384,768]{1,0:T(8,128)(2,1)}, bf16[384,768]{1,0:T(8,128)(2,1)}, u32[]{:S(2)}, u32[]{:S(2)}) collective-permute-start(bf16[384,768]{1,0:T(8,128)(2,1)} %slice.568), channel_id=1, source_target_pairs={{0,4},{1,5},{2,6},{3,7},{4,0},{5,1},{6,2},{7,3},{8,12},{9,13},{10,... | collective-permute-start | bytes 1769480 | tf_op jit(solution)/shard_map/ppermute | solution.py:103
  132.9 179.0 %collective-permute-start.14 = (bf16[768,768]{1,0:T(8,128)(2,1)S(1)}, bf16[768,768]{1,0:T(8,128)(2,1)}, u32[]{:S(2)}, u32[]{:S(2)}) collective-permute-start(bf16[768,768]{1,0:T(8,128)(2,1)S(1)} %collective-permute-done.9.refs_1_), channel_id=1, source_target_pairs={{0,1},{1,0},{2,3},{3,2},{4,5},{5,4},{6,7},{7,6},{8,9},{9,8},{10,11... | collective-permute-start | bytes 3538952 | tf_op jit(solution)/shard_map/ppermute | solution.py:103
  133.0 179.8 %collective-permute-start.15 = (bf16[768,768]{1,0:T(8,128)(2,1)}, bf16[768,768]{1,0:T(8,128)(2,1)}, u32[]{:S(2)}, u32[]{:S(2)}) collective-permute-start(bf16[768,768]{1,0:T(8,128)(2,1)} %collective-permute-done.10.refs_2_), channel_id=1, source_target_pairs={{0,1},{1,0},{2,3},{3,2},{4,5},{5,4},{6,7},{7,6},{8,9},{9,8},{10,11... | collective-permute-start | bytes 3538952 | tf_op jit(solution)/shard_map/ppermute | solution.py:103
  311.4 293.6 %collective-permute-start.29 = (bf16[384,768]{1,0:T(8,128)(2,1)}, bf16[384,768]{1,0:T(8,128)(2,1)}, u32[]{:S(2)}, u32[]{:S(2)}) collective-permute-start(bf16[384,768]{1,0:T(8,128)(2,1)} %slice.593), channel_id=1, source_target_pairs={{0,4},{1,5},{2,6},{3,7},{4,0},{5,1},{6,2},{7,3},{8,12},{9,13},{10,... | collective-permute-start | bytes 1769480 | tf_op jit(solution)/shard_map/ppermute | solution.py:103
  311.9 294.6 %collective-permute-start.30 = (bf16[384,768]{1,0:T(8,128)(2,1)}, bf16[384,768]{1,0:T(8,128)(2,1)}, u32[]{:S(2)}, u32[]{:S(2)}) collective-permute-start(bf16[384,768]{1,0:T(8,128)(2,1)} %slice.594), channel_id=1, source_target_pairs={{0,2},{1,3},{2,0},{3,1},{4,6},{5,7},{6,4},{7,5},{8,10},{9,11},{10,... | collective-permute-start | bytes 1769480 | tf_op jit(solution)/shard_map/ppermute | solution.py:103
  312.8 293.8 %collective-permute-start.21 = (bf16[384,768]{1,0:T(8,128)(2,1)}, bf16[384,768]{1,0:T(8,128)(2,1)}, u32[]{:S(2)}, u32[]{:S(2)}) collective-permute-start(bf16[384,768]{1,0:T(8,128)(2,1)} %slice.575), channel_id=1, source_target_pairs={{0,2},{1,3},{2,0},{3,1},{4,6},{5,7},{6,4},{7,5},{8,10},{9,11},{10,... | collective-permute-start | bytes 1769480 | tf_op jit(solution)/shard_map/ppermute | solution.py:103
  316.0 305.3 %collective-permute-start.32 = (bf16[768,768]{1,0:T(8,128)(2,1)}, bf16[768,768]{1,0:T(8,128)(2,1)}, u32[]{:S(2)}, u32[]{:S(2)}) collective-permute-start(bf16[768,768]{1,0:T(8,128)(2,1)} %collective-permute-done.27.refs_1_), channel_id=1, source_target_pairs={{0,1},{1,0},{2,3},{3,2},{4,5},{5,4},{6,7},{7,6},{8,9},{9,8},{10,11... | collective-permute-start | bytes 3538952 | tf_op jit(solution)/shard_map/ppermute | solution.py:103
  621.3 294.0 %collective-permute-start.22 = (bf16[784,768]{1,0:T(8,128)(2,1)}, bf16[784,768]{1,0:T(8,128)(2,1)}, u32[]{:S(2)}, u32[]{:S(2)}) collective-permute-start(bf16[784,768]{1,0:T(8,128)(2,1)} %constant_dynamic-update-slice_fusion.2.refs_0_), channel_id=1, source_target_pairs={{0,1},{1,0},{2,3},{3,2},{4,5},{5,4},{6,7},{7,6},{8,9},{9,8},{10,11... | collective-permute-start | bytes 3612680 | tf_op jit(solution)/shard_map/ppermute | solution.py:103
  621.3 294.1 %collective-permute-start.23 = (bf16[784,768]{1,0:T(8,128)(2,1)}, bf16[784,768]{1,0:T(8,128)(2,1)}, u32[]{:S(2)}, u32[]{:S(2)}) collective-permute-start(bf16[784,768]{1,0:T(8,128)(2,1)} %collective-permute-done.18.refs_1_), channel_id=1, source_target_pairs={{0,1},{1,0},{2,3},{3,2},{4,5},{5,4},{6,7},{7,6},{8,9},{9,8},{10,11... | collective-permute-start | bytes 3612680 | tf_op jit(solution)/shard_map/ppermute | solution.py:103
  621.8 293.6 %collective-permute-start.24 = (bf16[784,768]{1,0:T(8,128)(2,1)}, bf16[784,768]{1,0:T(8,128)(2,1)}, u32[]{:S(2)}, u32[]{:S(2)}) collective-permute-start(bf16[784,768]{1,0:T(8,128)(2,1)} %collective-permute-done.19.refs_2_), channel_id=1, source_target_pairs={{0,1},{1,0},{2,3},{3,2},{4,5},{5,4},{6,7},{7,6},{8,9},{9,8},{10,11... | collective-permute-start | bytes 3612680 | tf_op jit(solution)/shard_map/ppermute | solution.py:103
  621.8 293.5 %collective-permute-start.26 = (bf16[384,768]{1,0:T(8,128)(2,1)}, bf16[384,768]{1,0:T(8,128)(2,1)}, u32[]{:S(2)}, u32[]{:S(2)}) collective-permute-start(bf16[384,768]{1,0:T(8,128)(2,1)} %collective-permute-done.21.refs_4_), channel_id=1, source_target_pairs={{0,1},{1,0},{2,3},{3,2},{4,5},{5,4},{6,7},{7,6},{8,9},{9,8},{10,11... | collective-permute-start | bytes 1769480 | tf_op jit(solution)/shard_map/ppermute | solution.py:103
  622.3 293.1 %collective-permute-start.25 = (bf16[400,768]{1,0:T(8,128)(2,1)}, bf16[400,768]{1,0:T(8,128)(2,1)}, u32[]{:S(2)}, u32[]{:S(2)}) collective-permute-start(bf16[400,768]{1,0:T(8,128)(2,1)} %collective-permute-done.20.refs_3_), channel_id=1, source_target_pairs={{0,1},{1,0},{2,3},{3,2},{4,5},{5,4},{6,7},{7,6},{8,9},{9,8},{10,11... | collective-permute-start | bytes 1843208 | tf_op jit(solution)/shard_map/ppermute | solution.py:103
  1519.5 896.1 %collective-permute-start.36 = (bf16[4,400,768]{2,1,0:T(8,128)(2,1)}, bf16[4,400,768]{2,1,0:T(8,128)(2,1)}, u32[]{:S(2)}, u32[]{:S(2)}) collective-permute-start(bf16[4,400,768]{2,1,0:T(8,128)(2,1)} %get-tuple-element.37), channel_id=1, source_target_pairs={{0,1},{1,0},{2,3},{3,2},{4,5},{5,4},{6,7},{7,6},{8,9},{9,8},{10,11... | collective-permute-start | bytes 7372808 | tf_op jit(solution)/shard_map/ppermute | solution.py:103
  1808.1 645.0 %collective-permute-start.44 = (bf16[4,768,768]{2,1,0:T(8,128)(2,1)}, bf16[4,768,768]{2,1,0:T(8,128)(2,1)}, u32[]{:S(2)}, u32[]{:S(2)}) collective-permute-start(bf16[4,768,768]{2,1,0:T(8,128)(2,1)} %get-tuple-element.39), channel_id=1, source_target_pairs={{0,1},{1,0},{2,3},{3,2},{4,5},{5,4},{6,7},{7,6},{8,9},{9,8},{10,11... | collective-permute-start | bytes 14155784 | tf_op jit(solution)/shard_map/ppermute | solution.py:103
  2103.0 358.9 %collective-permute-start.60 = (bf16[4,768,768]{2,1,0:T(8,128)(2,1)}, bf16[4,768,768]{2,1,0:T(8,128)(2,1)}, u32[]{:S(2)}, u32[]{:S(2)}) collective-permute-start(bf16[4,768,768]{2,1,0:T(8,128)(2,1)} %get-tuple-element.43), channel_id=1, source_target_pairs={{0,1},{1,0},{2,3},{3,2},{4,5},{5,4},{6,7},{7,6},{8,9},{9,8},{10,11... | collective-permute-start | bytes 14155784 | tf_op jit(solution)/shard_map/ppermute | solution.py:103
  2415.5 51.7 %collective-permute-start.52 = (bf16[4,784,768]{2,1,0:T(8,128)(2,1)}, bf16[4,784,768]{2,1,0:T(8,128)(2,1)}, u32[]{:S(2)}, u32[]{:S(2)}) collective-permute-start(bf16[4,784,768]{2,1,0:T(8,128)(2,1)} %get-tuple-element.41), channel_id=1, source_target_pairs={{0,1},{1,0},{2,3},{3,2},{4,5},{5,4},{6,7},{7,6},{8,9},{9,8},{10,11... | collective-permute-start | bytes 14450696 | tf_op jit(solution)/shard_map/ppermute | solution.py:103
  2492.9 58.7 %collective-permute-start.64 = (bf16[768,768]{1,0:T(8,128)(2,1)S(1)}, bf16[768,768]{1,0:T(8,128)(2,1)S(1)}, u32[]{:S(2)}, u32[]{:S(2)}) collective-permute-start(bf16[768,768]{1,0:T(8,128)(2,1)S(1)} %pad_maximum_fusion.10), channel_id=1, source_target_pairs={{0,4},{1,5},{2,6},{3,7},{4,0},{5,1},{6,2},{7,3},{8,12},{9,13},{10,... | collective-permute-start | bytes 3538952 | tf_op jit(solution)/shard_map/ppermute | solution.py:103
  2501.0 52.4 %collective-permute-start.62 = (bf16[768,768]{1,0:T(8,128)(2,1)S(1)}, bf16[768,768]{1,0:T(8,128)(2,1)S(1)}, u32[]{:S(2)}, u32[]{:S(2)}) collective-permute-start(bf16[768,768]{1,0:T(8,128)(2,1)S(1)} %pad_maximum_fusion.9), channel_id=1, source_target_pairs={{0,2},{1,3},{2,0},{3,1},{4,6},{5,7},{6,4},{7,5},{8,10},{9,11},{10,... | collective-permute-start | bytes 3538952 | tf_op jit(solution)/shard_map/ppermute | solution.py:103
  2503.8 53.6 %collective-permute-start.42 = (bf16[400,768]{1,0:T(8,128)(2,1)S(1)}, bf16[400,768]{1,0:T(8,128)(2,1)S(1)}, u32[]{:S(2)}, u32[]{:S(2)}) collective-permute-start(bf16[400,768]{1,0:T(8,128)(2,1)S(1)} %add_convert_fusion.11), channel_id=1, source_target_pairs={{8,16},{16,8},{9,17},{17,9},{10,18},{18,10},{11,19},{19,11},{12,20... | collective-permute-start | bytes 1843208 | tf_op jit(solution)/shard_map/ppermute | solution.py:242
  2526.3 49.7 %collective-permute-start.54 = (bf16[784,768]{1,0:T(8,128)(2,1)S(1)}, bf16[784,768]{1,0:T(8,128)(2,1)S(1)}, u32[]{:S(2)}, u32[]{:S(2)}) collective-permute-start(bf16[784,768]{1,0:T(8,128)(2,1)S(1)} %pad_maximum_fusion.1), channel_id=1, source_target_pairs={{0,2},{1,3},{2,0},{3,1},{4,6},{5,7},{6,4},{7,5},{8,10},{9,11},{10,... | collective-permute-start | bytes 3612680 | tf_op jit(solution)/shard_map/ppermute | solution.py:103
  2528.1 47.9 %collective-permute-start.56 = (bf16[784,768]{1,0:T(8,128)(2,1)S(1)}, bf16[784,768]{1,0:T(8,128)(2,1)S(1)}, u32[]{:S(2)}, u32[]{:S(2)}) collective-permute-start(bf16[784,768]{1,0:T(8,128)(2,1)S(1)} %pad_maximum_fusion.2), channel_id=1, source_target_pairs={{0,4},{1,5},{2,6},{3,7},{4,0},{5,1},{6,2},{7,3},{8,12},{9,13},{10,... | collective-permute-start | bytes 3612680 | tf_op jit(solution)/shard_map/ppermute | solution.py:103
  2553.9 50.6 %collective-permute-start.65 = (bf16[768,768]{1,0:T(8,128)(2,1)S(1)}, bf16[768,768]{1,0:T(8,128)(2,1)S(1)}, u32[]{:S(2)}, u32[]{:S(2)}) collective-permute-start(bf16[768,768]{1,0:T(8,128)(2,1)S(1)} %fusion.43), channel_id=1, source_target_pairs={{0,8},{24,16},{1,9},{25,17},{2,10},{26,18},{3,11},{27,19},{4,12},{... | collective-permute-start | bytes 3538952 | tf_op jit(solution)/shard_map/ppermute | solution.py:240
  2557.6 54.2 %collective-permute-start.43 = (bf16[400,768]{1,0:T(8,128)(2,1)S(1)}, bf16[400,768]{1,0:T(8,128)(2,1)S(1)}, u32[]{:S(2)}, u32[]{:S(2)}) collective-permute-start(bf16[400,768]{1,0:T(8,128)(2,1)S(1)} %add_convert_fusion.10), channel_id=1, source_target_pairs={{8,0},{16,24},{9,1},{17,25},{10,2},{18,26},{11,3},{19,27},{12,4},{... | collective-permute-start | bytes 1843208 | tf_op jit(solution)/shard_map/ppermute | solution.py:243
  2631.2 55.5 %collective-permute-start.67 = (bf16[768,768]{1,0:T(8,128)(2,1)S(1)}, bf16[768,768]{1,0:T(8,128)(2,1)S(1)}, u32[]{:S(2)}, u32[]{:S(2)}) collective-permute-start(bf16[768,768]{1,0:T(8,128)(2,1)S(1)} %add_convert_fusion.6), channel_id=1, source_target_pairs={{8,0},{16,24},{9,1},{17,25},{10,2},{18,26},{11,3},{19,27},{12,4},{... | collective-permute-start | bytes 3538952 | tf_op jit(solution)/shard_map/ppermute | solution.py:243
  2634.0 71.0 %collective-permute-start.59 = (bf16[784,768]{1,0:T(8,128)(2,1)S(1)}, bf16[784,768]{1,0:T(8,128)(2,1)S(1)}, u32[]{:S(2)}, u32[]{:S(2)}) collective-permute-start(bf16[784,768]{1,0:T(8,128)(2,1)S(1)} %add_convert_fusion.4), channel_id=1, source_target_pairs={{8,0},{16,24},{9,1},{17,25},{10,2},{18,26},{11,3},{19,27},{12,4},{... | collective-permute-start | bytes 3612680 | tf_op jit(solution)/shard_map/ppermute | solution.py:243
  (206 other events, 9920.1 us)

commit v2 on v0

--- a/solution.py
+++ b/solution.py
@@ -1,9 +1,19 @@
+import functools
+
 import jax
 import jax.numpy as jnp
 from jax import lax
+from jax.experimental import pallas as pl
+from jax.experimental.pallas import tpu as pltpu
 from jax.sharding import PartitionSpec as P
 
 HEAD = 64
+PAIR = 2 * HEAD
+ROW_TILE = 16
+VMEM_BYTES = 56 * 1024 * 1024
+ANY = pl.BlockSpec(memory_space=pl.ANY)
+SMEM = pl.BlockSpec(memory_space=pltpu.SMEM)
+VMEM = pl.BlockSpec(memory_space=pltpu.VMEM)
 
 
 EPSILON = 1e-05
@@ -191,7 +201,7 @@
     return (grad_rows, grad_w_in, grad_b_in, grad_w_out, grad_b_out)
 
 
-def per_device(
+def per_device_any(
     enc_in,
     dec_in,
     bucket,
@@ -311,6 +321,635 @@
     )
 
 
+def swap(value, bit):
+    return lax.ppermute(value, "fsdp", [(i, i ^ bit) for i in range(8)])
+
+
+def add_low(*terms):
+    total = terms[0].astype(jnp.float32)
+    for term in terms[1:]:
+        total = total + term.astype(jnp.float32)
+    return total.astype(jnp.bfloat16)
+
+
+def tile_up(rows):
+    return -(-rows // ROW_TILE) * ROW_TILE
+
+
+def pack_units(shards, feature):
+    unit_rows = feature // 8
+    parts = []
+    for shard in shards:
+        rows, columns = shard.shape
+        if rows == unit_rows:
+            for block in range(columns // feature):
+                parts.append(shard[:, block * feature : (block + 1) * feature])
+        else:
+            parts.append(shard)
+    return jnp.concatenate(parts, axis=0)
+
+
+def vec_rows(vec_part, feature):
+    rows = tile_up(-(-vec_part.shape[0] // feature))
+    padded = jnp.pad(vec_part, (0, rows * feature - vec_part.shape[0]))
+    return padded.reshape(rows, feature)
+
+
+def gather_piece(packed, cut):
+    from_x = swap(packed, 2)
+    from_y = swap(packed, 4)
+    corner_top = swap(from_x[:cut], 4)
+    corner_low = swap(from_y[cut:], 2)
+    mine = [packed, from_x, from_y, corner_top, corner_low]
+    return mine + [swap(value, 1) for value in mine]
+
+
+def gathered_vec(buffers, cut, offset, table, length, feature):
+    rows = tile_up(-(-length // feature))
+    parts = []
+    for chip in range(4):
+        for core in range(2):
+            group = buffers[5 * core : 5 * core + 5]
+            source = group[chip] if chip < 3 else group[4]
+            first = offset if chip < 3 else offset - cut
+            parts.append(source[first : first + rows].reshape(1, rows * feature)[:, :length])
+    stacked = jnp.concatenate(parts, axis=0)
+    chosen = (table[:, None] == jnp.arange(8, dtype=jnp.int32)[None, :]).astype(jnp.bfloat16)
+    return dot_left(chosen, stacked).reshape(-1)
+
+
+class Loader:
+    def __init__(self, buffers, table, cut, sems):
+        self.buffers = buffers
+        self.table = table
+        self.cut = cut
+        self.sems = sems
+        self.used = 0
+
+    def unit(self, number, target, stride, first):
+        rows = target.shape[1] // 8
+        copies = []
+        for chip in range(4):
+            for core in range(2):
+                group = self.buffers[5 * core : 5 * core + 5]
+                offset = number * rows
+                if chip < 3:
+                    source = group[chip]
+                elif offset < self.cut:
+                    source = group[3]
+                else:
+                    source = group[4]
+                    offset -= self.cut
+                place = pl.multiple_of(self.table[2 * chip + core] * stride + first, ROW_TILE)
+                copy = pltpu.make_async_copy(
+                    source.at[pl.ds(offset, rows), :],
+                    target.at[pl.ds(place, rows), :],
+                    self.sems.at[self.used],
+                )
+                copy.start()
+                self.used += 1
+                copies.append(copy)
+        return copies
+
+    def wide(self, number, target):
+        return self.unit(number, target, target.shape[1] // 8, 0)
+
+    def tall(self, number, target):
+        rows = target.shape[1] // 8
+        copies = []
+        for block in range(4):
+            copies += self.unit(number + block, target, 4 * rows, block * rows)
+        return copies
+
+
+def wait_all(copies):
+    for copy in copies:
+        copy.wait()
+
+
+class Storer:
+    def __init__(self, keep, send, table, sems):
+        self.keep = keep
+        self.send = send
+        self.table = table
+        self.sems = sems
+        self.copies = []
+
+    def rows(self, source, stride, count, offset, chips_of=None):
+        for core, out in ((1, self.send), (0, self.keep)):
+            for chip in range(4):
+                place = pl.multiple_of(self.table[2 * chip + core] * stride, ROW_TILE)
+                copy = pltpu.make_async_copy(
+                    source.at[pl.ds(place, count), :],
+                    out.at[chip, pl.ds(offset, count), :],
+                    self.sems.at[len(self.copies)],
+                )
+                copy.start()
+                self.copies.append(copy)
+
+    def finish(self):
+        wait_all(self.copies)
+
+
+def low(value):
+    return value.astype(jnp.bfloat16)
+
+
+def layer_norm(hidden, gain, shift):
+    mean = jnp.mean(hidden, axis=-1, keepdims=True)
+    centred = hidden - mean
+    variance = jnp.mean(centred * centred, axis=-1, keepdims=True)
+    return centred * lax.rsqrt(variance + EPSILON) * gain + shift
+
+
+def layer_norm_back(hidden, gain, gradient):
+    mean = jnp.mean(hidden, axis=-1, keepdims=True)
+    centred = hidden - mean
+    variance = jnp.mean(centred * centred, axis=-1, keepdims=True)
+    scale = lax.rsqrt(variance + EPSILON)
+    unit = centred * scale
+    grad_gain = jnp.sum(gradient * unit, axis=0, keepdims=True)
+    grad_shift = jnp.sum(gradient, axis=0, keepdims=True)
+    inner = gradient * gain
+    mean_inner = jnp.mean(inner, axis=-1, keepdims=True)
+    mean_unit = jnp.mean(inner * unit, axis=-1, keepdims=True)
+    return (scale * (inner - mean_inner - unit * mean_unit), grad_gain, grad_shift)
+
+
+def key_mask(bucket, lengths, rows, segs, causal):
+    span = rows // segs
+    one_long = bucket[0] == 1
+    query = lax.broadcasted_iota(jnp.int32, (rows, rows), 0)
+    key = lax.broadcasted_iota(jnp.int32, (rows, rows), 1)
+    key_row = lax.broadcasted_iota(jnp.int32, (1, rows), 1)
+    limit = jnp.zeros((1, rows), jnp.int32)
+    start = jnp.zeros((1, rows), jnp.int32)
+    first = jnp.zeros((rows, 1), jnp.int32)
+    query_col = lax.broadcasted_iota(jnp.int32, (rows, 1), 0)
+    for seg in range(segs):
+        inside = (key_row >= seg * span) & (key_row < (seg + 1) * span)
+        limit = jnp.where(inside, seg * span + lengths[0, seg], limit)
+        start = jnp.where(inside, seg * span, start)
+        first = jnp.where((query_col >= seg * span) & (query_col < (seg + 1) * span), seg * span, first)
+    limit = jnp.where(one_long, lengths[0, 0], limit)
+    start = jnp.where(one_long, 0, start)
+    first = jnp.where(one_long, 0, first)
+    mask = (first == start) & (key < limit)
+    if causal:
+        mask = mask & (key <= query)
+    return mask
+
+
+def head_lanes(rows):
+    return lax.broadcasted_iota(jnp.int32, (rows, PAIR), 1) < HEAD
+
+
+def attn_body(
+    cross, causal, first_unit, cut, segs, table, bucket, lengths, *refs
+):
+    refs = list(refs)
+    q_in = refs.pop(0)
+    kv_in = refs.pop(0) if cross else q_in
+    vec = refs.pop(0)
+    buffers = [refs.pop(0) for _ in range(10)]
+    hidden_out, norm_out, q_out, k_out, v_out, o_out, p_out = refs[:7]
+    w_q, w_k, w_v, w_o, sems = refs[7:]
+    rows, feature = q_in.shape
+    load = Loader(buffers, table, cut, sems)
+    waits = [load.wide(first_unit + i, w) for i, w in enumerate((w_q, w_k, w_v, w_o))]
+    mask = key_mask(bucket, lengths, rows, segs, causal)
+    lanes = head_lanes(rows)
+    wait_all(waits[0])
+    q_out[...] = low(dot_plain(q_in[...], w_q[...]) + vec[0:1, :])
+    wait_all(waits[1])
+    k_out[...] = low(dot_plain(kv_in[...], w_k[...]))
+    wait_all(waits[2])
+    v_out[...] = low(dot_plain(kv_in[...], w_v[...]) + vec[1:2, :])
+    for pair in range(feature // PAIR):
+        columns = slice(pair * PAIR, (pair + 1) * PAIR)
+        q_pair, k_pair, v_pair = q_out[:, columns], k_out[:, columns], v_out[:, columns]
+        mixed = []
+        for half in range(2):
+            mine = lanes if half == 0 else ~lanes
+            score = dot_right(jnp.where(mine, q_pair, jnp.zeros_like(q_pair)), k_pair)
+            score = jnp.where(mask, score * SCORE_SCALE, NEG_FILL)
+            power = jnp.exp(score - jnp.max(score, axis=-1, keepdims=True))
+            probs = low(power / jnp.sum(power, axis=-1, keepdims=True))
+            p_out[2 * pair + half] = probs
+            mixed.append(dot_plain(probs, v_pair))
+        o_out[:, columns] = low(jnp.where(lanes, mixed[0], mixed[1]))
+    wait_all(waits[3])
+    hidden = q_in[...].astype(jnp.float32) + (dot_plain(o_out[...], w_o[...]) + vec[2:3, :])
+    hidden_out[...] = hidden
+    norm_out[...] = low(layer_norm(hidden, vec[3:4, :], vec[4:5, :]))
+
+
+def params(flops, moved):
+    return dict(
+        compiler_params=pltpu.CompilerParams(vmem_limit_bytes=VMEM_BYTES),
+        cost_estimate=pl.CostEstimate(flops=flops, bytes_accessed=moved, transcendentals=0),
+    )
+
+
+def attn_forward(q_in, kv_in, vec, buffers, ids, lengths, first_unit, cut, causal, name):
+    table, bucket = ids
+    rows, feature = q_in.shape
+    heads = feature // HEAD
+    cross = kv_in is not None
+    wide = jax.ShapeDtypeStruct((rows, feature), jnp.bfloat16)
+    sources = [q_in] + ([kv_in] if cross else []) + [vec]
+    square = pltpu.VMEM((feature, feature), jnp.bfloat16)
+    return pl.pallas_call(
+        functools.partial(attn_body, cross, causal, first_unit, cut, lengths.shape[1]),
+        out_shape=[
+            jax.ShapeDtypeStruct((rows, feature), jnp.float32),
+            wide,
+            wide,
+            wide,
+            wide,
+            wide,
+            jax.ShapeDtypeStruct((heads, rows, rows), jnp.bfloat16),
+        ],
+        in_specs=[SMEM] * 3 + [VMEM] * len(sources) + [ANY] * 10,
+        out_specs=[VMEM] * 7,
+        scratch_shapes=[square] * 4 + [pltpu.SemaphoreType.DMA((32,))],
+        name=name,
+        **params(8 * rows * feature * feature, 10 * feature * feature),
+    )(table, bucket, lengths, *sources, *buffers)
+
+
+def gelu_parts(hidden):
+    phi = 0.5 * (1.0 + lax.erf(hidden * 0.7071067811865476))
+    slope = phi + hidden * (0.3989422804014327 * jnp.exp(-0.5 * hidden * hidden))
+    return (hidden * phi, slope)
+
+
+def feed_body(cut, table, rows_in, vec, b_in, *refs):
+    buffers = refs[:10]
+    hidden_out, norm_out, r_out, slope_out, w_in, w_out, sems = refs[10:]
+    feature = rows_in.shape[1]
+    load = Loader(buffers, table, cut, sems)
+    waits = [load.wide(j, w_in.at[j]) for j in range(4)]
+    tail = load.tall(4, w_out)
+    total = None
+    for j in range(4):
+        columns = slice(j * feature, (j + 1) * feature)
+        wait_all(waits[j])
+        hidden = dot_plain(rows_in[...], w_in[j]) + b_in[:, columns]
+        active, slope = gelu_parts(hidden)
+        r_out[:, columns] = low(active)
+        slope_out[:, columns] = low(slope)
+    wait_all(tail)
+    total = dot_plain(r_out[...], w_out[...]) + vec[0:1, :]
+    hidden = rows_in[...].astype(jnp.float32) + total
+    hidden_out[...] = hidden
+    norm_out[...] = low(layer_norm(hidden, vec[1:2, :], vec[2:3, :]))
+
+
+def feed_forward(rows_in, vec, b_in, buffers, table, cut, name):
+    rows, feature = rows_in.shape
+    width = b_in.shape[1]
+    return pl.pallas_call(
+        functools.partial(feed_body, cut),
+        out_shape=[
+            jax.ShapeDtypeStruct((rows, feature), jnp.float32),
+            jax.ShapeDtypeStruct((rows, feature), jnp.bfloat16),
+            jax.ShapeDtypeStruct((rows, width), jnp.bfloat16),
+            jax.ShapeDtypeStruct((rows, width), jnp.bfloat16),
+        ],
+        in_specs=[SMEM] + [VMEM] * 3 + [ANY] * 10,
+        out_specs=[VMEM] * 4,
+        scratch_shapes=[
+            pltpu.VMEM((4, feature, feature), jnp.bfloat16),
+            pltpu.VMEM((width, feature), jnp.bfloat16),
+            pltpu.SemaphoreType.DMA((64,)),
+        ],
+        name=name,
+        **params(4 * rows * feature * width, 8 * feature * width),
+    )(table, rows_in, vec, b_in, *buffers)
+
+
+def feed_back_out_body(cut, extra, table, *refs):
+    refs = list(refs)
+    gradient = refs.pop(0)[...].astype(jnp.float32)
+    if extra:
+        gradient = gradient + refs.pop(0)[...].astype(jnp.float32)
+    hidden, gain, active, slope = refs[:4]
+    buffers = refs[4:14]
+    g_out, gu_out, sums, bias_in, keep, send, w_out, stage, sems, out_sems = refs[14:]
+    feature = hidden.shape[1]
+    load = Loader(buffers, table, cut, sems)
+    tail = load.tall(4, w_out)
+    store = Storer(keep, send, table, out_sems)
+    gradient, grad_gain, grad_shift = layer_norm_back(hidden[...], gain[...], gradient)
+    sums[0:1, :] = jnp.sum(gradient, axis=0, keepdims=True)
+    sums[1:2, :] = grad_gain
+    sums[2:3, :] = grad_shift
+    g_out[...] = gradient
+    grad_low = low(gradient)
+    for j in range(4):
+        columns = slice(j * feature, (j + 1) * feature)
+        stage[columns, :] = low(dot_left(active[:, columns], grad_low))
+    store.rows(stage, feature // 2, feature // 2, 0)
+    wait_all(tail)
+    for j in range(4):
+        columns = slice(j * feature, (j + 1) * feature)
+        grad_hidden = dot_right(grad_low, w_out[columns, :]) * slope[:, columns].astype(jnp.float32)
+        bias_in[0:1, columns] = jnp.sum(grad_hidden, axis=0, keepdims=True)
+        gu_out[:, columns] = low(grad_hidden)
+    store.finish()
+
+
+def feed_back_out(gradients, hidden, gain, active, slope, buffers, table, cut, name):
+    rows, feature = hidden.shape
+    width = active.shape[1]
+    block = jax.ShapeDtypeStruct((4, feature // 2, feature), jnp.bfloat16)
+    return pl.pallas_call(
+        functools.partial(feed_back_out_body, cut, len(gradients) == 2),
+        out_shape=[
+            jax.ShapeDtypeStruct((rows, feature), jnp.float32),
+            jax.ShapeDtypeStruct((rows, width), jnp.bfloat16),
+            jax.ShapeDtypeStruct((3, feature), jnp.float32),
+            jax.ShapeDtypeStruct((1, width), jnp.float32),
+            block,
+            block,
+        ],
+        in_specs=[SMEM] + [VMEM] * (len(gradients) + 4) + [ANY] * 10,
+        out_specs=[VMEM] * 4 + [ANY] * 2,
+        scratch_shapes=[
+            pltpu.VMEM((width, feature), jnp.bfloat16),
+            pltpu.VMEM((width, feature), jnp.bfloat16),
+            pltpu.SemaphoreType.DMA((32,)),
+            pltpu.SemaphoreType.DMA((8,)),
+        ],
+        name=name,
+        **params(4 * rows * feature * width, 6 * feature * width),
+    )(table, *gradients, hidden, gain, active, slope, *buffers)
+
+
+def feed_back_in_body(cut, table, gradient, grad_hidden, rows_in, *refs):
+    buffers = refs[:10]
+    total_out, keep, send, w_in, stage, sems, out_sems = refs[10:]
+    feature = rows_in.shape[1]
+    load = Loader(buffers, table, cut, sems)
+    waits = [load.wide(j, w_in.at[j]) for j in range(4)]
+    store = Storer(keep, send, table, out_sems)
+    total = gradient[...]
+    for j in range(4):
+        columns = slice(j * feature, (j + 1) * feature)
+        stage[j] = low(dot_left(rows_in[...], grad_hidden[:, columns]))
+        store.rows(stage.at[j], feature // 8, feature // 8, j * (feature // 8))
+    for j in range(4):
+        columns = slice(j * feature, (j + 1) * feature)
+        wait_all(waits[j])
+        total = total + dot_right(grad_hidden[:, columns], w_in[j])
+    total_out[...] = total
+    store.finish()
+
+
+def feed_back_in(gradient, grad_hidden, rows_in, buffers, table, cut, name):
+    rows, feature = rows_in.shape
+    width = grad_hidden.shape[1]
+    block = jax.ShapeDtypeStruct((4, feature // 2, feature), jnp.bfloat16)
+    return pl.pallas_call(
+        functools.partial(feed_back_in_body, cut),
+        out_shape=[jax.ShapeDtypeStruct((rows, feature), jnp.float32), block, block],
+        in_specs=[SMEM] + [VMEM] * 3 + [ANY] * 10,
+        out_specs=[VMEM] + [ANY] * 2,
+        scratch_shapes=[
+            pltpu.VMEM((4, feature, feature), jnp.bfloat16),
+            pltpu.VMEM((4, feature, feature), jnp.bfloat16),
+            pltpu.SemaphoreType.DMA((32,)),
+            pltpu.SemaphoreType.DMA((32,)),
+        ],
+        name=name,
+        **params(4 * rows * feature * width, 6 * feature * width),
+    )(table, gradient, grad_hidden, rows_in, *buffers)
+
+
+def attn_back_body(cross, first_unit, cut, table, gradient, *refs):
+    refs = list(refs)
+    hidden, gain, q_in = refs[:3]
+    refs = refs[3:]
+    kv_in = refs.pop(0) if cross else q_in
+    queries, keys, values, mixed, probs_in = refs[:5]
+    buffers = refs[5:15]
+    refs = refs[15:]
+    q_grad_out = refs.pop(0)
+    kv_grad_out = refs.pop(0) if cross else None
+    sums, keep, send, w_q, w_k, w_v, w_o, stage, go, gq, gk, gv, sems, out_sems = refs
+    rows, feature = hidden.shape
+    unit = feature // 8
+    load = Loader(buffers, table, cut, sems)
+    wait_o = load.wide(first_unit + 3, w_o)
+    waits = [load.wide(first_unit + i, w) for i, w in enumerate((w_q, w_k, w_v))]
+    store = Storer(keep, send, table, out_sems)
+    lanes = head_lanes(rows)
+    total, grad_gain, grad_shift = layer_norm_back(hidden[...], gain[...], gradient[...])
+    sums[2:3, :] = jnp.sum(total, axis=0, keepdims=True)
+    sums[3:4, :] = grad_gain
+    sums[4:5, :] = grad_shift
+    grad_low = low(total)
+    stage[3] = low(dot_left(mixed[...], grad_low))
+    store.rows(stage.at[3], unit, unit, 3 * unit)
+    wait_all(wait_o)
+    go[...] = low(dot_right(grad_low, w_o[...]))
+    for pair in range(feature // PAIR):
+        columns = slice(pair * PAIR, (pair + 1) * PAIR)
+        q_pair, k_pair, v_pair = queries[:, columns], keys[:, columns], values[:, columns]
+        go_pair = go[:, columns]
+        parts = []
+        for half in range(2):
+            mine = lanes if half == 0 else ~lanes
+            probs_low = probs_in[2 * pair + half]
+            probs = probs_low.astype(jnp.float32)
+            grad_probs = dot_right(jnp.where(mine, go_pair, jnp.zeros_like(go_pair)), v_pair)
+            weighted = grad_probs * probs
+            row_sum = jnp.sum(weighted, axis=-1, keepdims=True)
+            grad_raw = low((weighted - probs * row_sum) * SCORE_SCALE)
+            parts.append(
+                (
+                    dot_plain(grad_raw, k_pair),
+                    dot_left(grad_raw, q_pair),
+                    dot_left(probs_low, go_pair),
+                )
+            )
+        grad_q, grad_k, grad_v = (jnp.where(lanes, a, b) for a, b in zip(*parts))
+        sums[0:1, columns] = jnp.sum(grad_q, axis=0, keepdims=True)
+        sums[1:2, columns] = jnp.sum(grad_v, axis=0, keepdims=True)
+        gq[:, columns] = low(grad_q)
+        gk[:, columns] = low(grad_k)
+        gv[:, columns] = low(grad_v)
+    for index, (source, grad) in enumerate(((q_in, gq), (kv_in, gk), (kv_in, gv))):
+        stage[index] = low(dot_left(source[...], grad[...]))
+        store.rows(stage.at[index], unit, unit, index * unit)
+    for copies in waits:
+        wait_all(copies)
+    total = total + dot_right(gq[...], w_q[...])
+    kv_total = dot_right(gk[...], w_k[...]) + dot_right(gv[...], w_v[...])
+    if cross:
+        q_grad_out[...] = total
+        kv_grad_out[...] = kv_total
+    else:
+        q_grad_out[...] = total + kv_total
+    store.finish()
+
+
+def attn_back(gradient, hidden, gain, q_in, kv_in, saved, buffers, table, first_unit, cut, name):
+    rows, feature = hidden.shape
+    cross = kv_in is not None
+    wide = jax.ShapeDtypeStruct((rows, feature), jnp.float32)
+    block = jax.ShapeDtypeStruct((4, feature // 2, feature), jnp.bfloat16)
+    sources = [gradient, hidden, gain, q_in] + ([kv_in] if cross else []) + list(saved)
+    square = pltpu.VMEM((feature, feature), jnp.bfloat16)
+    low_rows = pltpu.VMEM((rows, feature), jnp.bfloat16)
+    return pl.pallas_call(
+        functools.partial(attn_back_body, cross, first_unit, cut),
+        out_shape=[wide] * (1 + cross)
+        + [jax.ShapeDtypeStruct((5, feature), jnp.float32), block, block],
+        in_specs=[SMEM] + [VMEM] * len(sources) + [ANY] * 10,
+        out_specs=[VMEM] * (2 + cross) + [ANY] * 2,
+        scratch_shapes=[square] * 4
+        + [pltpu.VMEM((4, feature, feature), jnp.bfloat16)]
+        + [low_rows] * 4
+        + [pltpu.SemaphoreType.DMA((32,)), pltpu.SemaphoreType.DMA((32,))],
+        name=name,
+        **params(16 * rows * feature * feature, 20 * feature * feature),
+    )(table, *sources, *buffers)
+
+
+def line_sum(value):
+    place = lax.axis_index("rep")
+    inner = (place == 1) | (place == 2)
+    half = add_low(value, lax.ppermute(value, "rep", [(0, 1), (3, 2)]))
+    total = add_low(half, lax.ppermute(half, "rep", [(1, 2), (2, 1)]))
+    return jnp.where(inner, total, lax.ppermute(total, "rep", [(1, 0), (2, 3)]))
+
+
+def reduce_blocks(keep, send, vec_blocks=None):
+    full = add_low(keep, swap(send, 1))
+    if vec_blocks is not None:
+        full = jnp.concatenate([full, add_low(vec_blocks[0], swap(vec_blocks[1], 1))], axis=1)
+    cut = tile_up(full.shape[1] // 2)
+    low_x = swap(full[3, :cut], 2)
+    low_y = swap(full[3, cut:], 4)
+    to_x = jnp.concatenate([full[1, :cut], add_low(full[1, cut:], low_y)], axis=0)
+    to_y = jnp.concatenate([add_low(full[2, :cut], low_x), full[2, cut:]], axis=0)
+    return line_sum(add_low(full[0], swap(to_x, 2), swap(to_y, 4)))
+
+
+def vec_blocks(rows_list, tail, table, feature):
+    flat = jnp.concatenate([rows.reshape(-1) for rows in rows_list] + [tail.reshape(-1)])
+    parts = flat.astype(jnp.bfloat16).reshape(8, -1)
+    chosen = (table[:, None] == jnp.arange(8, dtype=jnp.int32)[None, :]).astype(jnp.bfloat16)
+    placed = dot_plain(chosen, parts).astype(jnp.bfloat16)
+    count = tile_up(-(-parts.shape[1] // feature))
+    placed = jnp.pad(placed, ((0, 0), (0, count * feature - parts.shape[1])))
+    placed = placed.reshape(4, 2, count, feature)
+    return (placed[:, 0], placed[:, 1])
+
+
+def wide_out(block, feature):
+    unit = feature // 8
+    parts = [block[j * unit : (j + 1) * unit] for j in range(4)]
+    return jnp.concatenate(parts, axis=1).astype(jnp.float32)
+
+
+def per_device(
+    enc_in,
+    dec_in,
+    bucket,
+    enc_lengths,
+    dec_lengths,
+    enc_attn,
+    enc_vec,
+    enc_w1,
+    enc_w2,
+    dec_attn,
+    dec_vec,
+    dec_w1,
+    dec_w2,
+    enc_cot,
+    dec_cot,
+):
+    feature = enc_in.shape[1]
+    unit = feature // 8
+    table = lax.axis_index("fsdp").astype(jnp.int32) ^ jnp.arange(8, dtype=jnp.int32)
+    ids = (table, bucket)
+    e_attn = gather_piece(pack_units([enc_attn, vec_rows(enc_vec, feature)], feature), 2 * unit)
+    e_feed = gather_piece(pack_units([enc_w1, enc_w2], feature), 4 * unit)
+    d_attn = gather_piece(pack_units([dec_attn, vec_rows(dec_vec, feature)], feature), 4 * unit)
+    d_feed = gather_piece(pack_units([dec_w1, dec_w2], feature), 4 * unit)
+    e_vec = gathered_vec(e_attn, 2 * unit, 4 * unit, table, enc_vec.shape[0], feature)
+    e_rows, e_tail = unpack(e_vec, 8, feature)
+    e_tail = e_tail.reshape(1, -1)
+    e_hid_a, e_first, *e_saved = attn_forward(
+        enc_in, None, e_rows[0:5], e_attn, ids, enc_lengths, 0, 2 * unit, False, "enc_attn"
+    )
+    e_hid_f, encoded, e_act, e_slope = feed_forward(
+        e_first, e_rows[5:8], e_tail, e_feed, table, 4 * unit, "enc_feed"
+    )
+    d_vec = gathered_vec(d_attn, 4 * unit, 8 * unit, table, dec_vec.shape[0], feature)
+    d_rows, d_tail = unpack(d_vec, 13, feature)
+    d_tail = d_tail.reshape(1, -1)
+    d_hid_s, d_first, *s_saved = attn_forward(
+        dec_in, None, d_rows[0:5], d_attn, ids, dec_lengths, 0, 4 * unit, True, "dec_self"
+    )
+    d_hid_c, d_second, *c_saved = attn_forward(
+        d_first, encoded, d_rows[5:10], d_attn, ids, enc_lengths, 4, 4 * unit, False, "dec_cross"
+    )
+    d_hid_f, decoded, d_act, d_slope = feed_forward(
+        d_second, d_rows[10:13], d_tail, d_feed, table, 4 * unit, "dec_feed"
+    )
+    gradient, d_gu, d_sums_f, d_bias, keep, send = feed_back_out(
+        [dec_cot], d_hid_f, d_rows[11:12], d_act, d_slope, d_feed, table, 4 * unit, "dec_feed_back_out"
+    )
+    grad_d_w2 = reduce_blocks(keep, send)
+    gradient, keep, send = feed_back_in(
+        gradient, d_gu, d_second, d_feed, table, 4 * unit, "dec_feed_back_in"
+    )
+    grad_d_w1 = reduce_blocks(keep, send)
+    gradient, grad_encoded, d_sums_c, keep, send = attn_back(
+        gradient, d_hid_c, d_rows[8:9], d_first, encoded, c_saved, d_attn, table, 4, 4 * unit, "cross_back"
+    )
+    grad_d_cross = reduce_blocks(keep, send)
+    e_gradient, e_gu, e_sums_f, e_bias, keep, send = feed_back_out(
+        [enc_cot, grad_encoded], e_hid_f, e_rows[6:7], e_act, e_slope, e_feed, table, 4 * unit, "enc_feed_back_out"
+    )
+    grad_e_w2 = reduce_blocks(keep, send)
+    e_gradient, keep, send = feed_back_in(
+        e_gradient, e_gu, e_first, e_feed, table, 4 * unit, "enc_feed_back_in"
+    )
+    grad_e_w1 = reduce_blocks(keep, send)
+    dec_in_grad, d_sums_s, keep, send = attn_back(
+        gradient, d_hid_s, d_rows[3:4], dec_in, None, s_saved, d_attn, table, 0, 4 * unit, "self_back"
+    )
+    grad_d_self = reduce_blocks(
+        keep, send, vec_blocks([d_sums_s, d_sums_c, d_sums_f], d_bias, table, feature)
+    )
+    enc_in_grad, e_sums_a, keep, send = attn_back(
+        e_gradient, e_hid_a, e_rows[3:4], enc_in, None, e_saved, e_attn, table, 0, 2 * unit, "enc_attn_back"
+    )
+    grad_e_attn = reduce_blocks(
+        keep, send, vec_blocks([e_sums_a, e_sums_f], e_bias, table, feature)
+    )
+    d_wide = jnp.concatenate([wide_out(grad_d_self, feature), wide_out(grad_d_cross, feature)], axis=1)
+    return (
+        encoded,
+        decoded,
+        enc_in_grad,
+        dec_in_grad,
+        wide_out(grad_e_attn, feature),
+        grad_e_attn[4 * unit :].reshape(-1)[: enc_vec.shape[0]].astype(jnp.float32),
+        wide_out(grad_e_w1, feature),
+        grad_e_w2.astype(jnp.float32),
+        d_wide,
+        grad_d_self[4 * unit :].reshape(-1)[: dec_vec.shape[0]].astype(jnp.float32),
+        wide_out(grad_d_w1, feature),
+        grad_d_w2.astype(jnp.float32),
+    )
+
+
 def solution(mesh):
     in_specs = (
         P(("rep", "fsdp"), None),
@@ -343,6 +982,7 @@
         P("fsdp", None),
         P("fsdp", None),
     )
+    small = mesh.shape["fsdp"] == 8 and mesh.shape["rep"] == 4
     return jax.shard_map(
-        per_device, mesh=mesh, in_specs=in_specs, out_specs=out_specs, check_vma=False
-    )
+        per_device if small else per_device_any, mesh=mesh, in_specs=in_specs, out_specs=out_specs, check_vma=False
+    )

time: 926 us -> 627 us (0.68)
  waiting for transfers between devices: 551 us -> 334 us
  matrix products: 199 us -> 0.9 us
  Pallas kernels: 0 us -> 121 us
  starting transfers between devices: 0.98 us -> 87.9 us
  blocking collectives: 72.6 us -> 0 us
  between operations: 18.4 us -> 3.5 us
  local copies, waits for them, and re-layouts: 55.4 us -> 43.5 us
    ppermute x0 -> x94, waiting for transfers between devices: none -> 334 us  [the longest x73 199 us: swap(): return lax.ppermute(value, 'fsdp', [(i, i ^ bit) for i in range(8)])]
    reduce_scatter x4 -> x0, waiting for transfers between devices: 227 us -> none  [the longest x2 114 us: reduce_grads(): lax.psum_scatter(grad_out.astype(jnp.bfloat16), 'fsdp', scatter_dimension...]
    all_gather x6 -> x0, waiting for transfers between devices: 154 us -> none  [the longest x2 57.9 us: fetch(): lax.all_gather(w_out, 'fsdp', axis=0, tiled=True)]
    pallas_call x0 -> x12, Pallas kernels: none -> 121 us  [the longest x3 40.3 us: attn_back(): pl.pallas_call(functools.partial(attn_back_body, cross, first_unit, cut),...]
    psum x1 -> x0, waiting for transfers between devices: 115 us -> none  [reduce_grads(): lax.psum(shard[0].astype(jnp.bfloat16), 'rep').astype(jnp.float32)]
    dot_general x26 -> x0, matrix products: 104 us -> none  [the longest x11 36.2 us: dot_right(): lax.dot_general(first_op, second_op, (((1,), (1,)), ((), ())), preferred_...]
    ppermute x0 -> x94, starting transfers between devices: none -> 87.9 us  [the longest x73 56.4 us: swap(): return lax.ppermute(value, 'fsdp', [(i, i ^ bit) for i in range(8)])]
    unnamed x15 -> x0, waiting for transfers between devices: 54 us -> none
  transfers between devices with their start and end apart: 13 -> 94, of which waited for: 12 -> 37; matrix products, arithmetic and copies ran while one was open for 19% -> 9% of each run, Pallas kernels for 0% -> 17%
where the time goes in v2:
time: 627 us; the launch traced here: 617 us
  waiting for transfers between devices  334 us (53%)
  Pallas kernels  121 us (19%)
  starting transfers between devices  87.9 us (14%)
  local copies, waits for them, and re-layouts  43.5 us (7%)
  other arithmetic  26.3 us (4%)
    ppermute x73, waiting for transfers between devices, swap(): return lax.ppermute(value, 'fsdp', [(i, i ^ bit) for i in range(8)])  199 us
    ppermute x7, waiting for transfers between devices, line_sum(): return jnp.where(inner, total, lax.ppermute(total, 'rep', [(1, 0), (2, 3)]))  82.2 us
    ppermute x73, starting transfers between devices, swap(): return lax.ppermute(value, 'fsdp', [(i, i ^ bit) for i in range(8)])  56.4 us
    ppermute x7, waiting for transfers between devices, line_sum(): half = add_low(value, lax.ppermute(value, 'rep', [(0, 1), (3, 2)]))  52.6 us
    pallas_call x3, Pallas kernels, attn_back(): pl.pallas_call(functools.partial(attn_back_body, cross, first_unit, cut),...  40.3 us
    pallas_call x3, Pallas kernels, attn_forward(): pl.pallas_call(functools.partial(attn_body, cross, causal, first_unit, cu...  25.5 us
    unnamed x153, local copies, waits for them, and re-layouts  24.2 us
    pallas_call x2, Pallas kernels, feed_forward(): pl.pallas_call(functools.partial(feed_body, cut), out_shape=[jax.ShapeDty...  18.9 us
  transfers between devices with their start and end apart: 94, of which 37 were waited for; matrix products, arithmetic and copies ran while one was open for 9% of the time, Pallas kernels for 17%

profile of v2, /device:TPU:0, one launch (start us, length us, event | category | flops | bytes accessed | tf_op | source)
XLA Modules:
  0.0 616.7 jit_solution(704327942731669390)
XLA Ops:
  32.6 22.1 %collective-permute-done.7.refs_5_.refs_11_ = bf16[192,768]{1,0:T(8,128)(2,1)} collective-permute-done((bf16[192,768]{1,0:T(8,128)(2,1)S(1)}, bf16[192,768]{1,0:T(8,128)(2,1)}, u32[]{:S(2)}, u32[]{:S(2)}) %collective-permute-start.7) | collective-permute-done | bytes 294944 | tf_op jit(solution)/shard_map/ppermute | solution.py:325
  58.1 23.0 %collective-permute-done.5.refs_6_.refs_12_ = bf16[208,768]{1,0:T(8,128)(2,1)S(1)} collective-permute-done((bf16[208,768]{1,0:T(8,128)(2,1)S(1)}, bf16[208,768]{1,0:T(8,128)(2,1)S(1)}, u32[]{:S(2)}, u32[]{:S(2)}) %collective-permute-start.5) | collective-permute-done | bytes 319520 | tf_op jit(solution)/shard_map/ppermute | solution.py:325
  92.8 15.5 %collective-permute-done.21.refs_4_.refs_5_.refs_11_.refs_10_ = bf16[784,768]{1,0:T(8,128)(2,1)S(1)} collective-permute-done((bf16[784,768]{1,0:T(8,128)(2,1)}, bf16[784,768]{1,0:T(8,128)(2,1)S(1)}, u32[]{:S(2)}, u32[]{:S(2)}) %collective-permute-start.21) | collective-permute-done | bytes 1204256 | tf_op jit(solution)/shard_map/ppermute | solution.py:325
  113.9 10.2 %collective-permute-done.11.refs_3_.refs_9_ = bf16[384,768]{1,0:T(8,128)(2,1)} collective-permute-done((bf16[384,768]{1,0:T(8,128)(2,1)S(1)}, bf16[384,768]{1,0:T(8,128)(2,1)}, u32[]{:S(2)}, u32[]{:S(2)}) %collective-permute-start.11) | collective-permute-done | bytes 589856 | tf_op jit(solution)/shard_map/ppermute | solution.py:325
  126.7 12.6 %collective-permute-done.23.refs_6_.refs_7_.refs_13_.refs_12_ = bf16[400,768]{1,0:T(8,128)(2,1)S(1)} collective-permute-done((bf16[400,768]{1,0:T(8,128)(2,1)S(1)}, bf16[400,768]{1,0:T(8,128)(2,1)S(1)}, u32[]{:S(2)}, u32[]{:S(2)}) %collective-permute-start.23) | collective-permute-done | bytes 614432 | tf_op jit(solution)/shard_map/ppermute | solution.py:325
  154.1 9.5 %enc_feed.1 = (f32[256,768]{1,0:T(8,128)}, bf16[256,768]{1,0:T(8,128)(2,1)}, bf16[256,3072]{1,0:T(8,128)(2,1)}, bf16[256,3072]{1,0:T(8,128)(2,1)}) custom-call(s32[8]{0:T(128)} %copy-done.35, bf16[256,768]{1,0:T(8,128)(2,1)} %get-tuple-element.72.rows_in, f32[3,768]{1,0:T(4,128)} %slice.659.vec, f32[1,3072]{1,0:T(1,128)} %bitcast.268, ...), custom_call_target="tpu_custom_call" | custom-call | flops 2415919104 | bytes 18874368 | tf_op jit(solution)/shard_map/enc_feed/pallas_call | solution.py:612
  169.7 10.3 %collective-permute-done.25.refs_5_.refs_6_.refs_12_.refs_11_ = bf16[384,768]{1,0:T(8,128)(2,1)} collective-permute-done((bf16[384,768]{1,0:T(8,128)(2,1)S(1)}, bf16[384,768]{1,0:T(8,128)(2,1)}, u32[]{:S(2)}, u32[]{:S(2)}) %collective-permute-start.25) | collective-permute-done | bytes 589856 | tf_op jit(solution)/shard_map/ppermute | solution.py:325
  205.8 9.4 %dec_feed.1 = (f32[256,768]{1,0:T(8,128)}, bf16[256,768]{1,0:T(8,128)(2,1)}, bf16[256,3072]{1,0:T(8,128)(2,1)}, bf16[256,3072]{1,0:T(8,128)(2,1)}) custom-call(s32[8]{0:T(128)} %copy-done.35, bf16[256,768]{1,0:T(8,128)(2,1)} %get-tuple-element.75.rows_in, f32[3,768]{1,0:T(4,128)} %slice.682.vec, f32[1,3072]{1,0:T(1,128)} %bitcast.267, ...), custom_call_target="tpu_custom_call" | custom-call | flops 2415919104 | bytes 18874368 | tf_op jit(solution)/shard_map/dec_feed/pallas_call | solution.py:612
  215.2 8.7 %dec_feed_back_out.1 = (f32[256,768]{1,0:T(8,128)}, bf16[256,3072]{1,0:T(8,128)(2,1)}, f32[3,768]{1,0:T(4,128)}, f32[1,3072]{1,0:T(1,128)}, bf16[4,384,768]{2,1,0:T(8,128)(2,1)}, /*index=5*/bf16[4,384,768]{2,1,0:T(8,128)(2,1)}) custom-call(s32[8]{0:T(128)} %copy-done.35, bf16[256,768]{1,0:T(8,128)(2,1)} %refs_0_.6, f32[256,768]{1,0:T(8,128)} %get-tuple-element.77.refs_1_, ...), custom_call_target="tpu_custom_call" | custom-call | flops 2415919104 | bytes 14155776 | tf_op jit(solution)/shard_map/dec_feed_back_out/pallas_call | solution.py:667
  225.0 9.1 %dec_feed_back_in.1 = (f32[256,768]{1,0:T(8,128)}, bf16[4,384,768]{2,1,0:T(8,128)(2,1)}, bf16[4,384,768]{2,1,0:T(8,128)(2,1)}) custom-call(s32[8]{0:T(128)} %copy-done.35, f32[256,768]{1,0:T(8,128)} %get-tuple-element.80.gradient, bf16[256,3072]{1,0:T(8,128)(2,1)} %get-tuple-element.81.grad_hidden, bf16[256,768]{1,0:T(8,128)(2,1)} %get-tuple-element.75.rows_in, ...), custom_call_target="tpu_custom_call" | custom-call | flops 2415919104 | bytes 14155776 | tf_op jit(solution)/shard_map/dec_feed_back_in/pallas_call | solution.py:714
  234.1 13.3 %cross_back.1 = (f32[256,768]{1,0:T(8,128)}, f32[256,768]{1,0:T(8,128)}, f32[5,768]{1,0:T(8,128)}, bf16[4,384,768]{2,1,0:T(8,128)(2,1)}, bf16[4,384,768]{2,1,0:T(8,128)(2,1)}) custom-call(s32[8]{0:T(128)} %copy-done.35, f32[256,768]{1,0:T(8,128)} %get-tuple-element.82.gradient, f32[256,768]{1,0:T(8,128)} %get-tuple-element.83.refs_0_, ...), custom_call_target="tpu_custom_call" | custom-call | flops 2415919104 | bytes 11796480 | tf_op jit(solution)/shard_map/cross_back/pallas_call | solution.py:806
  247.4 8.9 %enc_feed_back_out.1 = (f32[256,768]{1,0:T(8,128)}, bf16[256,3072]{1,0:T(8,128)(2,1)}, f32[3,768]{1,0:T(4,128)}, f32[1,3072]{1,0:T(1,128)}, bf16[4,384,768]{2,1,0:T(8,128)(2,1)}, /*index=5*/bf16[4,384,768]{2,1,0:T(8,128)(2,1)}) custom-call(s32[8]{0:T(128)} %copy-done.35, bf16[256,768]{1,0:T(8,128)(2,1)} %refs_0_.7, f32[256,768]{1,0:T(8,128)} %get-tuple-element.89.refs_1_, ...), custom_call_target="tpu_custom_call" | custom-call | flops 2415919104 | bytes 14155776 | tf_op jit(solution)/shard_map/enc_feed_back_out/pallas_call | solution.py:667
  256.4 9.1 %enc_feed_back_in.1 = (f32[256,768]{1,0:T(8,128)}, bf16[4,384,768]{2,1,0:T(8,128)(2,1)}, bf16[4,384,768]{2,1,0:T(8,128)(2,1)}) custom-call(s32[8]{0:T(128)} %copy-done.35, f32[256,768]{1,0:T(8,128)} %get-tuple-element.93.gradient, bf16[256,3072]{1,0:T(8,128)(2,1)} %get-tuple-element.94.grad_hidden, bf16[256,768]{1,0:T(8,128)(2,1)} %get-tuple-element.72.rows_in, ...), custom_call_target="tpu_custom_call" | custom-call | flops 2415919104 | bytes 14155776 | tf_op jit(solution)/shard_map/enc_feed_back_in/pallas_call | solution.py:714
  266.6 13.5 %self_back.1 = (f32[256,768]{1,0:T(8,128)}, f32[5,768]{1,0:T(8,128)}, bf16[4,384,768]{2,1,0:T(8,128)(2,1)}, bf16[4,384,768]{2,1,0:T(8,128)(2,1)}) custom-call(s32[8]{0:T(128)} %copy-done.35, f32[256,768]{1,0:T(8,128)} %get-tuple-element.103.gradient, f32[256,768]{1,0:T(8,128)} %get-tuple-element.104.refs_0_, f32[1,768]{1,0:T(1,128)} %slice.563.refs_1_, ...), custom_call_target="tpu_custom_call" | custom-call | flops 2415919104 | bytes 11796480 | tf_op jit(solution)/shard_map/self_back/pallas_call | solution.py:806
  282.2 13.4 %enc_attn_back.1 = (f32[256,768]{1,0:T(8,128)}, f32[5,768]{1,0:T(8,128)}, bf16[4,384,768]{2,1,0:T(8,128)(2,1)}, bf16[4,384,768]{2,1,0:T(8,128)(2,1)}) custom-call(s32[8]{0:T(128)} %copy-done.35, f32[256,768]{1,0:T(8,128)} %get-tuple-element.95.gradient, f32[256,768]{1,0:T(8,128)} %get-tuple-element.96.refs_0_, f32[1,768]{1,0:T(1,128)} %slice.561.refs_1_, ...), custom_call_target="tpu_custom_call" | custom-call | flops 2415919104 | bytes 11796480 | tf_op jit(solution)/shard_map/enc_attn_back/pallas_call | solution.py:806
  331.6 9.4 %collective-permute-done.63 = bf16[192,768]{1,0:T(8,128)(2,1)S(1)} collective-permute-done((bf16[192,768]{1,0:T(8,128)(2,1)S(1)}, bf16[192,768]{1,0:T(8,128)(2,1)S(1)}, u32[]{:S(2)}, u32[]{:S(2)}) %collective-permute-start.63) | collective-permute-done | bytes 294944 | tf_op jit(solution)/shard_map/ppermute | solution.py:325
  344.2 8.6 %collective-permute-done.38 = bf16[192,768]{1,0:T(8,128)(2,1)S(1)} collective-permute-done((bf16[192,768]{1,0:T(8,128)(2,1)S(1)}, bf16[192,768]{1,0:T(8,128)(2,1)S(1)}, u32[]{:S(2)}, u32[]{:S(2)}) %collective-permute-start.38) | collective-permute-done | bytes 294944 | tf_op jit(solution)/shard_map/ppermute | solution.py:325
  359.3 11.0 %collective-permute-done.88 = bf16[384,768]{1,0:T(8,128)(2,1)S(1)} collective-permute-done((bf16[384,768]{1,0:T(8,128)(2,1)S(1)}, bf16[384,768]{1,0:T(8,128)(2,1)S(1)}, u32[]{:S(2)}, u32[]{:S(2)}) %collective-permute-start.88) | collective-permute-done | bytes 589856 | tf_op jit(solution)/shard_map/ppermute | solution.py:325
  372.5 10.5 %collective-permute-done.47 = bf16[384,768]{1,0:T(8,128)(2,1)S(1)} collective-permute-done((bf16[384,768]{1,0:T(8,128)(2,1)S(1)}, bf16[384,768]{1,0:T(8,128)(2,1)S(1)}, u32[]{:S(2)}, u32[]{:S(2)}) %collective-permute-start.47) | collective-permute-done | bytes 589856 | tf_op jit(solution)/shard_map/ppermute | solution.py:325
  385.3 10.3 %collective-permute-done.80 = bf16[384,768]{1,0:T(8,128)(2,1)S(1)} collective-permute-done((bf16[384,768]{1,0:T(8,128)(2,1)S(1)}, bf16[384,768]{1,0:T(8,128)(2,1)S(1)}, u32[]{:S(2)}, u32[]{:S(2)}) %collective-permute-start.80) | collective-permute-done | bytes 589856 | tf_op jit(solution)/shard_map/ppermute | solution.py:325
  398.0 10.3 %collective-permute-done.72 = bf16[384,768]{1,0:T(8,128)(2,1)S(1)} collective-permute-done((bf16[384,768]{1,0:T(8,128)(2,1)S(1)}, bf16[384,768]{1,0:T(8,128)(2,1)S(1)}, u32[]{:S(2)}, u32[]{:S(2)}) %collective-permute-start.72) | collective-permute-done | bytes 589856 | tf_op jit(solution)/shard_map/ppermute | solution.py:325
  410.7 10.3 %collective-permute-done.55 = bf16[384,768]{1,0:T(8,128)(2,1)S(1)} collective-permute-done((bf16[384,768]{1,0:T(8,128)(2,1)S(1)}, bf16[384,768]{1,0:T(8,128)(2,1)S(1)}, u32[]{:S(2)}, u32[]{:S(2)}) %collective-permute-start.55) | collective-permute-done | bytes 589856 | tf_op jit(solution)/shard_map/ppermute | solution.py:325
  425.5 8.6 %collective-permute-done.64 = bf16[400,768]{1,0:T(8,128)(2,1)S(1)} collective-permute-done((bf16[400,768]{1,0:T(8,128)(2,1)S(1)}, bf16[400,768]{1,0:T(8,128)(2,1)S(1)}, u32[]{:S(2)}, u32[]{:S(2)}) %collective-permute-start.64) | collective-permute-done | bytes 614432 | tf_op jit(solution)/shard_map/ppermute | solution.py:325
  464.8 11.8 %collective-permute-done.75 = bf16[384,768]{1,0:T(8,128)(2,1)S(1)} collective-permute-done((bf16[384,768]{1,0:T(8,128)(2,1)S(1)}, bf16[384,768]{1,0:T(8,128)(2,1)S(1)}, u32[]{:S(2)}, u32[]{:S(2)}) %collective-permute-start.75) | collective-permute-done | bytes 589856 | tf_op jit(solution)/shard_map/ppermute | solution.py:824
  477.5 11.8 %collective-permute-done.58 = bf16[384,768]{1,0:T(8,128)(2,1)S(1)} collective-permute-done((bf16[384,768]{1,0:T(8,128)(2,1)S(1)}, bf16[384,768]{1,0:T(8,128)(2,1)S(1)}, u32[]{:S(2)}, u32[]{:S(2)}) %collective-permute-start.58) | collective-permute-done | bytes 589856 | tf_op jit(solution)/shard_map/ppermute | solution.py:824
  490.1 12.3 %collective-permute-done.67 = bf16[400,768]{1,0:T(8,128)(2,1)S(1)} collective-permute-done((bf16[400,768]{1,0:T(8,128)(2,1)S(1)}, bf16[400,768]{1,0:T(8,128)(2,1)S(1)}, u32[]{:S(2)}, u32[]{:S(2)}) %collective-permute-start.67) | collective-permute-done | bytes 614432 | tf_op jit(solution)/shard_map/ppermute | solution.py:824
  503.3 8.6 %collective-permute-done.42 = bf16[400,768]{1,0:T(8,128)(2,1)S(1)} collective-permute-done((bf16[400,768]{1,0:T(8,128)(2,1)S(1)}, bf16[400,768]{1,0:T(8,128)(2,1)S(1)}, u32[]{:S(2)}, u32[]{:S(2)}) %collective-permute-start.42) | collective-permute-done | bytes 614432 | tf_op jit(solution)/shard_map/ppermute | solution.py:824
  521.9 17.9 %collective-permute-done.93 = bf16[384,768]{1,0:T(8,128)(2,1)S(1)} collective-permute-done((bf16[384,768]{1,0:T(8,128)(2,1)S(1)}, bf16[384,768]{1,0:T(8,128)(2,1)S(1)}, u32[]{:S(2)}, u32[]{:S(2)}) %collective-permute-start.93) | collective-permute-done | bytes 589856 | tf_op jit(solution)/shard_map/ppermute | solution.py:826
  542.1 10.2 %collective-permute-done.52 = bf16[384,768]{1,0:T(8,128)(2,1)S(1)} collective-permute-done((bf16[384,768]{1,0:T(8,128)(2,1)S(1)}, bf16[384,768]{1,0:T(8,128)(2,1)S(1)}, u32[]{:S(2)}, u32[]{:S(2)}) %collective-permute-start.52) | collective-permute-done | bytes 589856 | tf_op jit(solution)/shard_map/ppermute | solution.py:826
  553.7 11.4 %collective-permute-done.85 = bf16[384,768]{1,0:T(8,128)(2,1)S(1)} collective-permute-done((bf16[384,768]{1,0:T(8,128)(2,1)S(1)}, bf16[384,768]{1,0:T(8,128)(2,1)S(1)}, u32[]{:S(2)}, u32[]{:S(2)}) %collective-permute-start.85) | collective-permute-done | bytes 589856 | tf_op jit(solution)/shard_map/ppermute | solution.py:826
  566.3 24.0 %collective-permute-done.60 = bf16[384,768]{1,0:T(8,128)(2,1)S(1)} collective-permute-done((bf16[384,768]{1,0:T(8,128)(2,1)S(1)}, bf16[384,768]{1,0:T(8,128)(2,1)S(1)}, u32[]{:S(2)}, u32[]{:S(2)}) %collective-permute-start.60) | collective-permute-done | bytes 589856 | tf_op jit(solution)/shard_map/ppermute | solution.py:826
  592.6 10.8 %collective-permute-done.69 = bf16[400,768]{1,0:T(8,128)(2,1)S(1)} collective-permute-done((bf16[400,768]{1,0:T(8,128)(2,1)S(1)}, bf16[400,768]{1,0:T(8,128)(2,1)S(1)}, u32[]{:S(2)}, u32[]{:S(2)}) %collective-permute-start.69) | collective-permute-done | bytes 614432 | tf_op jit(solution)/shard_map/ppermute | solution.py:826
  (485 shorter events, 226.4 us)
Async XLA Ops:
  13.4 68.0 %collective-permute-start.9 = (bf16[768,768]{1,0:T(8,128)(2,1)}, bf16[768,768]{1,0:T(8,128)(2,1)}, u32[]{:S(2)}, u32[]{:S(2)}) collective-permute-start(bf16[768,768]{1,0:T(8,128)(2,1)} %constant_dynamic-update-slice_fusion.1.refs_0_.refs_6_), channel_id=1, source_target_pairs={{0,2},{1,3},{2,0},{3,1},{4,6},{5,7},{6,4},{7,5},{8,10},{9,11},{10,... | collective-permute-start | bytes 3538952 | tf_op jit(solution)/shard_map/ppermute | solution.py:325
  13.9 69.1 %collective-permute-start.10 = (bf16[768,768]{1,0:T(8,128)(2,1)}, bf16[768,768]{1,0:T(8,128)(2,1)}, u32[]{:S(2)}, u32[]{:S(2)}) collective-permute-start(bf16[768,768]{1,0:T(8,128)(2,1)} %constant_dynamic-update-slice_fusion.1.refs_0_.refs_6_), channel_id=1, source_target_pairs={{0,4},{1,5},{2,6},{3,7},{4,0},{5,1},{6,2},{7,3},{8,12},{9,13},{10,... | collective-permute-start | bytes 3538952 | tf_op jit(solution)/shard_map/ppermute | solution.py:325
  25.1 58.7 %collective-permute-start.27 = (bf16[768,768]{1,0:T(8,128)(2,1)}, bf16[768,768]{1,0:T(8,128)(2,1)}, u32[]{:S(2)}, u32[]{:S(2)}) collective-permute-start(bf16[768,768]{1,0:T(8,128)(2,1)} %constant_dynamic-update-slice_fusion.3.refs_0_.refs_5_), channel_id=1, source_target_pairs={{0,2},{1,3},{2,0},{3,1},{4,6},{5,7},{6,4},{7,5},{8,10},{9,11},{10,... | collective-permute-start | bytes 3538952 | tf_op jit(solution)/shard_map/ppermute | solution.py:325
  31.0 55.0 %collective-permute-start.28 = (bf16[768,768]{1,0:T(8,128)(2,1)}, bf16[768,768]{1,0:T(8,128)(2,1)}, u32[]{:S(2)}, u32[]{:S(2)}) collective-permute-start(bf16[768,768]{1,0:T(8,128)(2,1)} %constant_dynamic-update-slice_fusion.3.refs_0_.refs_5_), channel_id=1, source_target_pairs={{0,4},{1,5},{2,6},{3,7},{4,0},{5,1},{6,2},{7,3},{8,12},{9,13},{10,... | collective-permute-start | bytes 3538952 | tf_op jit(solution)/shard_map/ppermute | solution.py:325
  113.4 39.4 %collective-permute-start.14 = (bf16[768,768]{1,0:T(8,128)(2,1)}, bf16[768,768]{1,0:T(8,128)(2,1)}, u32[]{:S(2)}, u32[]{:S(2)}) collective-permute-start(bf16[768,768]{1,0:T(8,128)(2,1)} %collective-permute-done.9.refs_1_.refs_7_), channel_id=1, source_target_pairs={{0,1},{1,0},{2,3},{3,2},{4,5},{5,4},{6,7},{7,6},{8,9},{9,8},{10,11... | collective-permute-start | bytes 3538952 | tf_op jit(solution)/shard_map/ppermute | solution.py:325
  113.4 40.6 %collective-permute-start.15 = (bf16[768,768]{1,0:T(8,128)(2,1)}, bf16[768,768]{1,0:T(8,128)(2,1)}, u32[]{:S(2)}, u32[]{:S(2)}) collective-permute-start(bf16[768,768]{1,0:T(8,128)(2,1)} %collective-permute-done.10.refs_2_.refs_8_), channel_id=1, source_target_pairs={{0,1},{1,0},{2,3},{3,2},{4,5},{5,4},{6,7},{7,6},{8,9},{9,8},{10,11... | collective-permute-start | bytes 3538952 | tf_op jit(solution)/shard_map/ppermute | solution.py:325
  126.7 37.0 %collective-permute-start.20 = (bf16[784,768]{1,0:T(8,128)(2,1)S(1)}, bf16[784,768]{1,0:T(8,128)(2,1)}, u32[]{:S(2)}, u32[]{:S(2)}) collective-permute-start(bf16[784,768]{1,0:T(8,128)(2,1)S(1)} %collective-permute-done.19.refs_3_.refs_4_.refs_10_.refs_9_), channel_id=1, source_target_pairs={{0,1},{1,0},{2,3},{3,2},{4,5},{5,4},{6,7},{7,6},{8,9},{9,8},{10,11... | collective-permute-start | bytes 3612680 | tf_op jit(solution)/shard_map/ppermute | solution.py:325
  139.5 40.5 %collective-permute-start.22 = (bf16[784,768]{1,0:T(8,128)(2,1)S(1)}, bf16[784,768]{1,0:T(8,128)(2,1)}, u32[]{:S(2)}, u32[]{:S(2)}) collective-permute-start(bf16[784,768]{1,0:T(8,128)(2,1)S(1)} %collective-permute-done.21.refs_4_.refs_5_.refs_11_.refs_10_), channel_id=1, source_target_pairs={{0,1},{1,0},{2,3},{3,2},{4,5},{5,4},{6,7},{7,6},{8,9},{9,8},{10,11... | collective-permute-start | bytes 3612680 | tf_op jit(solution)/shard_map/ppermute | solution.py:325
  163.7 40.3 %collective-permute-start.31 = (bf16[768,768]{1,0:T(8,128)(2,1)}, bf16[768,768]{1,0:T(8,128)(2,1)S(1)}, u32[]{:S(2)}, u32[]{:S(2)}) collective-permute-start(bf16[768,768]{1,0:T(8,128)(2,1)} %constant_dynamic-update-slice_fusion.3.refs_0_.refs_5_), channel_id=1, source_target_pairs={{0,1},{1,0},{2,3},{3,2},{4,5},{5,4},{6,7},{7,6},{8,9},{9,8},{10,11... | collective-permute-start | bytes 3538952 | tf_op jit(solution)/shard_map/ppermute | solution.py:325
  224.0 74.5 %collective-permute-start.86 = (bf16[4,384,768]{2,1,0:T(8,128)(2,1)}, bf16[4,384,768]{2,1,0:T(8,128)(2,1)}, u32[]{:S(2)}, u32[]{:S(2)}) collective-permute-start(bf16[4,384,768]{2,1,0:T(8,128)(2,1)} %get-tuple-element.131), channel_id=1, source_target_pairs={{0,1},{1,0},{2,3},{3,2},{4,5},{5,4},{6,7},{7,6},{8,9},{9,8},{10,11... | collective-permute-start | bytes 7077896 | tf_op jit(solution)/shard_map/ppermute | solution.py:325
  265.5 35.7 %collective-permute-start.45 = (bf16[4,384,768]{2,1,0:T(8,128)(2,1)}, bf16[4,384,768]{2,1,0:T(8,128)(2,1)}, u32[]{:S(2)}, u32[]{:S(2)}) collective-permute-start(bf16[4,384,768]{2,1,0:T(8,128)(2,1)} %get-tuple-element.117), channel_id=1, source_target_pairs={{0,1},{1,0},{2,3},{3,2},{4,5},{5,4},{6,7},{7,6},{8,9},{9,8},{10,11... | collective-permute-start | bytes 7077896 | tf_op jit(solution)/shard_map/ppermute | solution.py:325
  265.7 42.4 %collective-permute-start.78 = (bf16[4,384,768]{2,1,0:T(8,128)(2,1)}, bf16[4,384,768]{2,1,0:T(8,128)(2,1)}, u32[]{:S(2)}, u32[]{:S(2)}) collective-permute-start(bf16[4,384,768]{2,1,0:T(8,128)(2,1)} %get-tuple-element.129), channel_id=1, source_target_pairs={{0,1},{1,0},{2,3},{3,2},{4,5},{5,4},{6,7},{7,6},{8,9},{9,8},{10,11... | collective-permute-start | bytes 7077896 | tf_op jit(solution)/shard_map/ppermute | solution.py:325
  357.7 37.9 %collective-permute-start.80 = (bf16[384,768]{1,0:T(8,128)(2,1)S(1)}, bf16[384,768]{1,0:T(8,128)(2,1)S(1)}, u32[]{:S(2)}, u32[]{:S(2)}) collective-permute-start(bf16[384,768]{1,0:T(8,128)(2,1)S(1)} %pad_maximum_fusion.10), channel_id=1, source_target_pairs={{0,2},{1,3},{2,0},{3,1},{4,6},{5,7},{6,4},{7,5},{8,10},{9,11},{10,... | collective-permute-start | bytes 1769480 | tf_op jit(solution)/shard_map/ppermute | solution.py:325
  371.1 37.2 %collective-permute-start.72 = (bf16[384,768]{1,0:T(8,128)(2,1)S(1)}, bf16[384,768]{1,0:T(8,128)(2,1)S(1)}, u32[]{:S(2)}, u32[]{:S(2)}) collective-permute-start(bf16[384,768]{1,0:T(8,128)(2,1)S(1)} %pad_maximum_fusion.8), channel_id=1, source_target_pairs={{0,2},{1,3},{2,0},{3,1},{4,6},{5,7},{6,4},{7,5},{8,10},{9,11},{10,... | collective-permute-start | bytes 1769480 | tf_op jit(solution)/shard_map/ppermute | solution.py:325
  383.8 37.2 %collective-permute-start.55 = (bf16[384,768]{1,0:T(8,128)(2,1)S(1)}, bf16[384,768]{1,0:T(8,128)(2,1)S(1)}, u32[]{:S(2)}, u32[]{:S(2)}) collective-permute-start(bf16[384,768]{1,0:T(8,128)(2,1)S(1)} %pad_maximum_fusion.6), channel_id=1, source_target_pairs={{0,2},{1,3},{2,0},{3,1},{4,6},{5,7},{6,4},{7,5},{8,10},{9,11},{10,... | collective-permute-start | bytes 1769480 | tf_op jit(solution)/shard_map/ppermute | solution.py:325
  396.6 37.5 %collective-permute-start.64 = (bf16[400,768]{1,0:T(8,128)(2,1)S(1)}, bf16[400,768]{1,0:T(8,128)(2,1)S(1)}, u32[]{:S(2)}, u32[]{:S(2)}) collective-permute-start(bf16[400,768]{1,0:T(8,128)(2,1)S(1)} %pad_maximum_fusion.2), channel_id=1, source_target_pairs={{0,2},{1,3},{2,0},{3,1},{4,6},{5,7},{6,4},{7,5},{8,10},{9,11},{10,... | collective-permute-start | bytes 1843208 | tf_op jit(solution)/shard_map/ppermute | solution.py:325
  408.3 29.3 %collective-permute-start.66 = (bf16[400,768]{1,0:T(8,128)(2,1)S(1)}, bf16[400,768]{1,0:T(8,128)(2,1)S(1)}, u32[]{:S(2)}, u32[]{:S(2)}) collective-permute-start(bf16[400,768]{1,0:T(8,128)(2,1)S(1)} %pad_maximum_fusion.3), channel_id=1, source_target_pairs={{0,4},{1,5},{2,6},{3,7},{4,0},{5,1},{6,2},{7,3},{8,12},{9,13},{10,... | collective-permute-start | bytes 1843208 | tf_op jit(solution)/shard_map/ppermute | solution.py:325
  409.3 36.6 %collective-permute-start.39 = (bf16[400,768]{1,0:T(8,128)(2,1)S(1)}, bf16[400,768]{1,0:T(8,128)(2,1)S(1)}, u32[]{:S(2)}, u32[]{:S(2)}) collective-permute-start(bf16[400,768]{1,0:T(8,128)(2,1)S(1)} %pad_maximum_fusion), channel_id=1, source_target_pairs={{0,2},{1,3},{2,0},{3,1},{4,6},{5,7},{6,4},{7,5},{8,10},{9,11},{10,... | collective-permute-start | bytes 1843208 | tf_op jit(solution)/shard_map/ppermute | solution.py:325
  420.9 28.4 %collective-permute-start.41 = (bf16[400,768]{1,0:T(8,128)(2,1)S(1)}, bf16[400,768]{1,0:T(8,128)(2,1)S(1)}, u32[]{:S(2)}, u32[]{:S(2)}) collective-permute-start(bf16[400,768]{1,0:T(8,128)(2,1)S(1)} %pad_maximum_fusion.1), channel_id=1, source_target_pairs={{0,4},{1,5},{2,6},{3,7},{4,0},{5,1},{6,2},{7,3},{8,12},{9,13},{10,... | collective-permute-start | bytes 1843208 | tf_op jit(solution)/shard_map/ppermute | solution.py:325
  421.9 29.0 %collective-permute-start.91 = (bf16[384,768]{1,0:T(8,128)(2,1)S(1)}, bf16[384,768]{1,0:T(8,128)(2,1)S(1)}, u32[]{:S(2)}, u32[]{:S(2)}) collective-permute-start(bf16[384,768]{1,0:T(8,128)(2,1)S(1)} %fusion.5), channel_id=1, source_target_pairs={{0,8},{24,16},{1,9},{25,17},{2,10},{26,18},{3,11},{27,19},{4,12},{... | collective-permute-start | bytes 1769480 | tf_op jit(solution)/shard_map/ppermute | solution.py:824
  445.9 30.8 %collective-permute-start.75 = (bf16[384,768]{1,0:T(8,128)(2,1)S(1)}, bf16[384,768]{1,0:T(8,128)(2,1)S(1)}, u32[]{:S(2)}, u32[]{:S(2)}) collective-permute-start(bf16[384,768]{1,0:T(8,128)(2,1)S(1)} %fusion.9), channel_id=1, source_target_pairs={{0,8},{24,16},{1,9},{25,17},{2,10},{26,18},{3,11},{27,19},{4,12},{... | collective-permute-start | bytes 1769480 | tf_op jit(solution)/shard_map/ppermute | solution.py:824
  449.4 39.9 %collective-permute-start.58 = (bf16[384,768]{1,0:T(8,128)(2,1)S(1)}, bf16[384,768]{1,0:T(8,128)(2,1)S(1)}, u32[]{:S(2)}, u32[]{:S(2)}) collective-permute-start(bf16[384,768]{1,0:T(8,128)(2,1)S(1)} %fusion.11), channel_id=1, source_target_pairs={{0,8},{24,16},{1,9},{25,17},{2,10},{26,18},{3,11},{27,19},{4,12},{... | collective-permute-start | bytes 1769480 | tf_op jit(solution)/shard_map/ppermute | solution.py:824
  451.0 51.5 %collective-permute-start.67 = (bf16[400,768]{1,0:T(8,128)(2,1)S(1)}, bf16[400,768]{1,0:T(8,128)(2,1)S(1)}, u32[]{:S(2)}, u32[]{:S(2)}) collective-permute-start(bf16[400,768]{1,0:T(8,128)(2,1)S(1)} %fusion.1), channel_id=1, source_target_pairs={{0,8},{24,16},{1,9},{25,17},{2,10},{26,18},{3,11},{27,19},{4,12},{... | collective-permute-start | bytes 1843208 | tf_op jit(solution)/shard_map/ppermute | solution.py:824
  452.7 59.2 %collective-permute-start.42 = (bf16[400,768]{1,0:T(8,128)(2,1)S(1)}, bf16[400,768]{1,0:T(8,128)(2,1)S(1)}, u32[]{:S(2)}, u32[]{:S(2)}) collective-permute-start(bf16[400,768]{1,0:T(8,128)(2,1)S(1)} %fusion.3), channel_id=1, source_target_pairs={{0,8},{24,16},{1,9},{25,17},{2,10},{26,18},{3,11},{27,19},{4,12},{... | collective-permute-start | bytes 1843208 | tf_op jit(solution)/shard_map/ppermute | solution.py:824
  464.0 48.8 %collective-permute-start.92 = (bf16[384,768]{1,0:T(8,128)(2,1)S(1)}, bf16[384,768]{1,0:T(8,128)(2,1)S(1)}, u32[]{:S(2)}, u32[]{:S(2)}) collective-permute-start(bf16[384,768]{1,0:T(8,128)(2,1)S(1)} %add_convert_fusion.12), channel_id=1, source_target_pairs={{8,16},{16,8},{9,17},{17,9},{10,18},{18,10},{11,19},{19,11},{12,20... | collective-permute-start | bytes 1769480 | tf_op jit(solution)/shard_map/ppermute | solution.py:825
  476.6 37.0 %collective-permute-start.51 = (bf16[384,768]{1,0:T(8,128)(2,1)S(1)}, bf16[384,768]{1,0:T(8,128)(2,1)S(1)}, u32[]{:S(2)}, u32[]{:S(2)}) collective-permute-start(bf16[384,768]{1,0:T(8,128)(2,1)S(1)} %add_convert_fusion.20), channel_id=1, source_target_pairs={{8,16},{16,8},{9,17},{17,9},{10,18},{18,10},{11,19},{19,11},{12,20... | collective-permute-start | bytes 1769480 | tf_op jit(solution)/shard_map/ppermute | solution.py:825
  516.0 36.4 %collective-permute-start.52 = (bf16[384,768]{1,0:T(8,128)(2,1)S(1)}, bf16[384,768]{1,0:T(8,128)(2,1)S(1)}, u32[]{:S(2)}, u32[]{:S(2)}) collective-permute-start(bf16[384,768]{1,0:T(8,128)(2,1)S(1)} %add_convert_fusion.19), channel_id=1, source_target_pairs={{8,0},{16,24},{9,1},{17,25},{10,2},{18,26},{11,3},{19,27},{12,4},{... | collective-permute-start | bytes 1769480 | tf_op jit(solution)/shard_map/ppermute | solution.py:826
  517.5 47.6 %collective-permute-start.85 = (bf16[384,768]{1,0:T(8,128)(2,1)S(1)}, bf16[384,768]{1,0:T(8,128)(2,1)S(1)}, u32[]{:S(2)}, u32[]{:S(2)}) collective-permute-start(bf16[384,768]{1,0:T(8,128)(2,1)S(1)} %add_convert_fusion.13), channel_id=1, source_target_pairs={{8,0},{16,24},{9,1},{17,25},{10,2},{18,26},{11,3},{19,27},{12,4},{... | collective-permute-start | bytes 1769480 | tf_op jit(solution)/shard_map/ppermute | solution.py:826
  518.9 73.6 %collective-permute-start.77 = (bf16[384,768]{1,0:T(8,128)(2,1)S(1)}, bf16[384,768]{1,0:T(8,128)(2,1)S(1)}, u32[]{:S(2)}, u32[]{:S(2)}) collective-permute-start(bf16[384,768]{1,0:T(8,128)(2,1)S(1)} %add_convert_fusion.15), channel_id=1, source_target_pairs={{8,0},{16,24},{9,1},{17,25},{10,2},{18,26},{11,3},{19,27},{12,4},{... | collective-permute-start | bytes 1769480 | tf_op jit(solution)/shard_map/ppermute | solution.py:826
  520.4 69.9 %collective-permute-start.60 = (bf16[384,768]{1,0:T(8,128)(2,1)S(1)}, bf16[384,768]{1,0:T(8,128)(2,1)S(1)}, u32[]{:S(2)}, u32[]{:S(2)}) collective-permute-start(bf16[384,768]{1,0:T(8,128)(2,1)S(1)} %add_convert_fusion.17), channel_id=1, source_target_pairs={{8,0},{16,24},{9,1},{17,25},{10,2},{18,26},{11,3},{19,27},{12,4},{... | collective-permute-start | bytes 1769480 | tf_op jit(solution)/shard_map/ppermute | solution.py:826
  539.7 63.7 %collective-permute-start.69 = (bf16[400,768]{1,0:T(8,128)(2,1)S(1)}, bf16[400,768]{1,0:T(8,128)(2,1)S(1)}, u32[]{:S(2)}, u32[]{:S(2)}) collective-permute-start(bf16[400,768]{1,0:T(8,128)(2,1)S(1)} %add_convert_fusion.7), channel_id=1, source_target_pairs={{8,0},{16,24},{9,1},{17,25},{10,2},{18,26},{11,3},{19,27},{12,4},{... | collective-permute-start | bytes 1843208 | tf_op jit(solution)/shard_map/ppermute | solution.py:826
  552.4 59.1 %collective-permute-start.44 = (bf16[400,768]{1,0:T(8,128)(2,1)S(1)}, bf16[400,768]{1,0:T(8,128)(2,1)S(1)}, u32[]{:S(2)}, u32[]{:S(2)}) collective-permute-start(bf16[400,768]{1,0:T(8,128)(2,1)S(1)} %add_convert_fusion.9), channel_id=1, source_target_pairs={{8,0},{16,24},{9,1},{17,25},{10,2},{18,26},{11,3},{19,27},{12,4},{... | collective-permute-start | bytes 1843208 | tf_op jit(solution)/shard_map/ppermute | solution.py:826
  (114 other events, 1822.1 us)

commit v3 on v2

--- a/solution.py
+++ b/solution.py
@@ -336,17 +336,59 @@
     return -(-rows // ROW_TILE) * ROW_TILE
 
 
-def pack_units(shards, feature):
-    unit_rows = feature // 8
-    parts = []
+def size_of(shape):
+    total = 1
+    for extent in shape:
+        total *= extent
+    return total
+
+
+class Order:
+    def __init__(self):
+        self.token = None
+        self.waits = []
+
+    def mark(self, *values):
+        self.waits += values
+
+    def tie(self, value):
+        if self.token is None:
+            return value
+        value, self.token = lax.optimization_barrier((value, self.token))
+        return value
+
+    def kernel(self, body, operands, specs, outs, scratch, name, flops=0, moved=0):
+        extra = self.waits + ([] if self.token is None else [self.token])
+        self.waits = []
+        count, skip = len(operands), len(extra)
+        results = pl.pallas_call(
+            lambda *refs: body(*refs[:count], *refs[count + skip :]),
+            out_shape=[jax.ShapeDtypeStruct(shape, dtype) for shape, dtype, spec in outs],
+            in_specs=list(specs) + [ANY] * skip,
+            out_specs=[spec for shape, dtype, spec in outs],
+            scratch_shapes=scratch,
+            compiler_params=pltpu.CompilerParams(vmem_limit_bytes=VMEM_BYTES),
+            cost_estimate=pl.CostEstimate(flops=flops, bytes_accessed=moved, transcendentals=0),
+            name=name,
+        )(*operands, *extra)
+        self.token = min(results, key=lambda result: result.size)
+        return results
+
+
+def pack_body(count, *refs):
+    shards, out = refs[:count], refs[-1]
+    feature = out.shape[1]
+    offset = 0
     for shard in shards:
         rows, columns = shard.shape
-        if rows == unit_rows:
-            for block in range(columns // feature):
-                parts.append(shard[:, block * feature : (block + 1) * feature])
-        else:
-            parts.append(shard)
-    return jnp.concatenate(parts, axis=0)
+        for block in range(columns // feature):
+            out[offset : offset + rows, :] = shard[:, block * feature : (block + 1) * feature]
+            offset += rows
+
+
+def split_body(cut, from_x, from_y, top, lower):
+    top[...] = from_x[:cut, :]
+    lower[...] = from_y[cut:, :]
 
 
 def vec_rows(vec_part, feature):
@@ -355,54 +397,129 @@
     return padded.reshape(rows, feature)
 
 
-def gather_piece(packed, cut):
-    from_x = swap(packed, 2)
-    from_y = swap(packed, 4)
-    corner_top = swap(from_x[:cut], 4)
-    corner_low = swap(from_y[cut:], 2)
-    mine = [packed, from_x, from_y, corner_top, corner_low]
-    return mine + [swap(value, 1) for value in mine]
-
-
-def gathered_vec(buffers, cut, offset, table, length, feature):
-    rows = tile_up(-(-length // feature))
-    parts = []
+class Gather:
+    def __init__(self, order, feature, name):
+        self.order = order
+        self.feature = feature
+        self.name = name
+        self.mine = []
+
+    def sides(self, *shards):
+        feature = self.feature
+        rows = sum(shard.size for shard in shards) // feature
+        (packed,) = self.order.kernel(
+            functools.partial(pack_body, len(shards)),
+            shards,
+            [VMEM] * len(shards),
+            [((rows, feature), jnp.bfloat16, VMEM)],
+            [],
+            self.name + "_pack",
+            moved=4 * rows * feature,
+        )
+        self.mine = [packed, swap(packed, 2), swap(packed, 4)]
+
+    def corners(self):
+        rows, feature = self.mine[0].shape
+        cut = rows // (2 * ROW_TILE) * ROW_TILE
+        top, lower = self.order.kernel(
+            functools.partial(split_body, cut),
+            self.mine[1:3],
+            [VMEM] * 2,
+            [
+                ((cut, feature), jnp.bfloat16, VMEM),
+                ((rows - cut, feature), jnp.bfloat16, VMEM),
+            ],
+            [],
+            self.name + "_split",
+            moved=4 * rows * feature,
+        )
+        self.mine += [swap(top, 4), swap(lower, 2)]
+
+    def join(self, *parts):
+        rows, feature = self.mine[0].shape
+        joined = self.order.kernel(
+            functools.partial(join_body, parts),
+            self.mine,
+            [ANY] * 5,
+            [((4 * count, feature), jnp.bfloat16, ANY) for first, count in parts],
+            [pltpu.VMEM((4 * rows, feature), jnp.bfloat16), pltpu.SemaphoreType.DMA((5 + 4 * len(parts),))],
+            self.name + "_join",
+        )
+        return [(part, swap(part, 1)) for part in joined]
+
+
+def join_body(parts, own, from_x, from_y, top, lower, *refs):
+    outs, stage, sems = refs[:-2], refs[-2], refs[-1]
+    copies = []
+    place = 0
+    for index, source in enumerate((own, from_x, from_y, top, lower)):
+        rows = source.shape[0]
+        copy = pltpu.make_async_copy(source, stage.at[pl.ds(place, rows), :], sems.at[index])
+        copy.start()
+        copies.append(copy)
+        place += rows
+    block = own.shape[0]
+    stores = []
     for chip in range(4):
-        for core in range(2):
-            group = buffers[5 * core : 5 * core + 5]
-            source = group[chip] if chip < 3 else group[4]
-            first = offset if chip < 3 else offset - cut
-            parts.append(source[first : first + rows].reshape(1, rows * feature)[:, :length])
-    stacked = jnp.concatenate(parts, axis=0)
-    chosen = (table[:, None] == jnp.arange(8, dtype=jnp.int32)[None, :]).astype(jnp.bfloat16)
-    return dot_left(chosen, stacked).reshape(-1)
+        wait_all(copies[chip : chip + 1] if chip < 3 else copies[3:])
+        for (first, count), out in zip(parts, outs):
+            copy = pltpu.make_async_copy(
+                stage.at[pl.ds(chip * block + first, count), :],
+                out.at[pl.ds(chip * count, count), :],
+                sems.at[5 + len(stores)],
+            )
+            copy.start()
+            stores.append(copy)
+    wait_all(stores)
+
+
+def vec_body(table, mine, theirs, out, sems):
+    rows = out.shape[0] // 8
+    block = mine.shape[0] // 4
+    copies = []
+    for chip in range(4):
+        for core, source in enumerate((mine, theirs)):
+            copies.append(
+                pltpu.make_async_copy(
+                    source.at[pl.ds((chip + 1) * block - rows, rows), :],
+                    out.at[pl.ds(pl.multiple_of(table[2 * chip + core] * rows, ROW_TILE), rows), :],
+                    sems.at[len(copies)],
+                )
+            )
+    for copy in copies:
+        copy.start()
+    wait_all(copies)
+
+
+def gathered_vec(order, buffers, table, rows, feature):
+    (out,) = order.kernel(
+        vec_body,
+        [table, *buffers],
+        [SMEM] + [ANY] * 2,
+        [((8 * rows, feature), jnp.bfloat16, VMEM)],
+        [pltpu.SemaphoreType.DMA((8,))],
+        "vectors",
+    )
+    return out.reshape(8, rows * feature)
 
 
 class Loader:
-    def __init__(self, buffers, table, cut, sems):
+    def __init__(self, buffers, table, sems, used=0):
         self.buffers = buffers
+        self.block = buffers[0].shape[0] // 4
         self.table = table
-        self.cut = cut
         self.sems = sems
-        self.used = 0
+        self.used = used
 
     def unit(self, number, target, stride, first):
         rows = target.shape[1] // 8
         copies = []
         for chip in range(4):
             for core in range(2):
-                group = self.buffers[5 * core : 5 * core + 5]
-                offset = number * rows
-                if chip < 3:
-                    source = group[chip]
-                elif offset < self.cut:
-                    source = group[3]
-                else:
-                    source = group[4]
-                    offset -= self.cut
+                offset = chip * self.block + number * rows
                 place = pl.multiple_of(self.table[2 * chip + core] * stride + first, ROW_TILE)
                 copy = pltpu.make_async_copy(
-                    source.at[pl.ds(offset, rows), :],
+                    self.buffers[core].at[pl.ds(offset, rows), :],
                     target.at[pl.ds(place, rows), :],
                     self.sems.at[self.used],
                 )
@@ -428,27 +545,46 @@
 
 
 class Storer:
-    def __init__(self, keep, send, table, sems):
-        self.keep = keep
-        self.send = send
+    def __init__(self, outs, table, slots, sems):
+        self.keep, self.upper, self.lower = outs if len(outs) == 3 else (outs[0], None, outs[1])
         self.table = table
+        self.slots = slots
+        self.block = self.keep.shape[1] // 2
         self.sems = sems
         self.copies = []
 
-    def rows(self, source, stride, count, offset, chips_of=None):
-        for core, out in ((1, self.send), (0, self.keep)):
-            for chip in range(4):
-                place = pl.multiple_of(self.table[2 * chip + core] * stride, ROW_TILE)
-                copy = pltpu.make_async_copy(
-                    source.at[pl.ds(place, count), :],
-                    out.at[chip, pl.ds(offset, count), :],
-                    self.sems.at[len(self.copies)],
-                )
-                copy.start()
-                self.copies.append(copy)
+    def add(self, source, out, row):
+        copy = pltpu.make_async_copy(
+            source, out.at[pl.ds(row, source.shape[0]), :], self.sems.at[len(self.copies)]
+        )
+        copy.start()
+        self.copies.append(copy)
+
+    def rows(self, source, stride, count, offset):
+        for core in (1, 0):
+            for slot in (2, 3, 0, 1):
+                place = self.table[2 * self.slots[slot] + core] * stride
+                block = source.at[pl.ds(pl.multiple_of(place, ROW_TILE), count), :]
+                if core == 0:
+                    self.add(block, self.keep, slot * self.block + offset)
+                elif slot < 2 or self.upper is None:
+                    self.add(block, self.lower, slot * self.block + offset)
+                else:
+                    self.add(block, self.upper, (slot - 2) * self.block + offset)
+
+    def tail(self, source):
+        self.add(source, self.lower, (4 if self.upper is None else 2) * self.block)
+        self.add(source, self.keep, 4 * self.block)
 
     def finish(self):
         wait_all(self.copies)
+
+
+def gradient_outs(feature, extra=0, single=False):
+    rows = feature // 2
+    if single:
+        return [((4 * rows + extra, feature), jnp.bfloat16, ANY)] * 2
+    return [((count, feature), jnp.bfloat16, ANY) for count in (4 * rows + extra, 2 * rows, 2 * rows + extra)]
 
 
 def low(value):
@@ -505,17 +641,17 @@
 
 
 def attn_body(
-    cross, causal, first_unit, cut, segs, table, bucket, lengths, *refs
+    cross, causal, first_unit, segs, table, bucket, lengths, *refs
 ):
     refs = list(refs)
     q_in = refs.pop(0)
     kv_in = refs.pop(0) if cross else q_in
     vec = refs.pop(0)
-    buffers = [refs.pop(0) for _ in range(10)]
+    buffers = [refs.pop(0) for _ in range(2)]
     hidden_out, norm_out, q_out, k_out, v_out, o_out, p_out = refs[:7]
     w_q, w_k, w_v, w_o, sems = refs[7:]
     rows, feature = q_in.shape
-    load = Loader(buffers, table, cut, sems)
+    load = Loader(buffers, table, sems)
     waits = [load.wide(first_unit + i, w) for i, w in enumerate((w_q, w_k, w_v, w_o))]
     mask = key_mask(bucket, lengths, rows, segs, causal)
     lanes = head_lanes(rows)
@@ -544,38 +680,22 @@
     norm_out[...] = low(layer_norm(hidden, vec[3:4, :], vec[4:5, :]))
 
 
-def params(flops, moved):
-    return dict(
-        compiler_params=pltpu.CompilerParams(vmem_limit_bytes=VMEM_BYTES),
-        cost_estimate=pl.CostEstimate(flops=flops, bytes_accessed=moved, transcendentals=0),
-    )
-
-
-def attn_forward(q_in, kv_in, vec, buffers, ids, lengths, first_unit, cut, causal, name):
-    table, bucket = ids
+def attn_forward(order, q_in, kv_in, vec, weights, ids, lengths, causal, name):
     rows, feature = q_in.shape
-    heads = feature // HEAD
-    cross = kv_in is not None
-    wide = jax.ShapeDtypeStruct((rows, feature), jnp.bfloat16)
-    sources = [q_in] + ([kv_in] if cross else []) + [vec]
-    square = pltpu.VMEM((feature, feature), jnp.bfloat16)
-    return pl.pallas_call(
-        functools.partial(attn_body, cross, causal, first_unit, cut, lengths.shape[1]),
-        out_shape=[
-            jax.ShapeDtypeStruct((rows, feature), jnp.float32),
-            wide,
-            wide,
-            wide,
-            wide,
-            wide,
-            jax.ShapeDtypeStruct((heads, rows, rows), jnp.bfloat16),
-        ],
-        in_specs=[SMEM] * 3 + [VMEM] * len(sources) + [ANY] * 10,
-        out_specs=[VMEM] * 7,
-        scratch_shapes=[square] * 4 + [pltpu.SemaphoreType.DMA((32,))],
-        name=name,
-        **params(8 * rows * feature * feature, 10 * feature * feature),
-    )(table, bucket, lengths, *sources, *buffers)
+    sources = [q_in] + ([] if kv_in is None else [kv_in]) + [vec]
+    wide = ((rows, feature), jnp.bfloat16, VMEM)
+    return order.kernel(
+        functools.partial(attn_body, kv_in is not None, causal, weights[1], lengths.shape[1]),
+        [*ids, lengths, *sources, *weights[0]],
+        [SMEM] * 3 + [VMEM] * len(sources) + [ANY] * 2,
+        [((rows, feature), jnp.float32, VMEM)]
+        + [wide] * 5
+        + [((feature // HEAD, rows, rows), jnp.bfloat16, VMEM)],
+        [pltpu.VMEM((feature, feature), jnp.bfloat16)] * 4 + [pltpu.SemaphoreType.DMA((32,))],
+        name,
+        8 * rows * feature * feature,
+        10 * feature * feature,
+    )
 
 
 def gelu_parts(hidden):
@@ -584,13 +704,12 @@
     return (hidden * phi, slope)
 
 
-def feed_body(cut, table, rows_in, vec, b_in, *refs):
-    buffers = refs[:10]
-    hidden_out, norm_out, r_out, slope_out, w_in, w_out, sems = refs[10:]
+def feed_body(units, table, rows_in, vec, b_in, *refs):
+    hidden_out, norm_out, r_out, slope_out, w_in, w_out, sems = refs[4:]
     feature = rows_in.shape[1]
-    load = Loader(buffers, table, cut, sems)
-    waits = [load.wide(j, w_in.at[j]) for j in range(4)]
-    tail = load.tall(4, w_out)
+    load = Loader(refs[:2], table, sems)
+    waits = [load.wide(units[0] + j, w_in.at[j]) for j in range(4)]
+    tail = Loader(refs[2:4], table, sems, load.used).tall(units[1], w_out)
     total = None
     for j in range(4):
         columns = slice(j * feature, (j + 1) * feature)
@@ -606,41 +725,38 @@
     norm_out[...] = low(layer_norm(hidden, vec[1:2, :], vec[2:3, :]))
 
 
-def feed_forward(rows_in, vec, b_in, buffers, table, cut, name):
+def feed_forward(order, rows_in, vec, b_in, w_in, w_out, table, name):
     rows, feature = rows_in.shape
     width = b_in.shape[1]
-    return pl.pallas_call(
-        functools.partial(feed_body, cut),
-        out_shape=[
-            jax.ShapeDtypeStruct((rows, feature), jnp.float32),
-            jax.ShapeDtypeStruct((rows, feature), jnp.bfloat16),
-            jax.ShapeDtypeStruct((rows, width), jnp.bfloat16),
-            jax.ShapeDtypeStruct((rows, width), jnp.bfloat16),
+    return order.kernel(
+        functools.partial(feed_body, (w_in[1], w_out[1])),
+        [table, rows_in, vec, b_in, *w_in[0], *w_out[0]],
+        [SMEM] + [VMEM] * 3 + [ANY] * 4,
+        [
+            ((rows, feature), jnp.float32, VMEM),
+            ((rows, feature), jnp.bfloat16, VMEM),
+            ((rows, width), jnp.bfloat16, VMEM),
+            ((rows, width), jnp.bfloat16, VMEM),
         ],
-        in_specs=[SMEM] + [VMEM] * 3 + [ANY] * 10,
-        out_specs=[VMEM] * 4,
-        scratch_shapes=[
+        [
             pltpu.VMEM((4, feature, feature), jnp.bfloat16),
             pltpu.VMEM((width, feature), jnp.bfloat16),
             pltpu.SemaphoreType.DMA((64,)),
         ],
-        name=name,
-        **params(4 * rows * feature * width, 8 * feature * width),
-    )(table, rows_in, vec, b_in, *buffers)
-
-
-def feed_back_out_body(cut, extra, table, *refs):
+        name,
+        4 * rows * feature * width,
+        8 * feature * width,
+    )
+
+
+def feed_back_out_body(extra, slots, table, *refs):
     refs = list(refs)
     gradient = refs.pop(0)[...].astype(jnp.float32)
     if extra:
         gradient = gradient + refs.pop(0)[...].astype(jnp.float32)
-    hidden, gain, active, slope = refs[:4]
-    buffers = refs[4:14]
-    g_out, gu_out, sums, bias_in, keep, send, w_out, stage, sems, out_sems = refs[14:]
+    hidden, gain, active, g_out, sums, keep, upper, lower, stage, out_sems = refs
     feature = hidden.shape[1]
-    load = Loader(buffers, table, cut, sems)
-    tail = load.tall(4, w_out)
-    store = Storer(keep, send, table, out_sems)
+    store = Storer((keep, upper, lower), table, slots, out_sems)
     gradient, grad_gain, grad_shift = layer_norm_back(hidden[...], gain[...], gradient)
     sums[0:1, :] = jnp.sum(gradient, axis=0, keepdims=True)
     sums[1:2, :] = grad_gain
@@ -651,52 +767,39 @@
         columns = slice(j * feature, (j + 1) * feature)
         stage[columns, :] = low(dot_left(active[:, columns], grad_low))
     store.rows(stage, feature // 2, feature // 2, 0)
+    store.finish()
+
+
+def feed_back_out(order, gradients, hidden, gain, active, table, slots, name):
+    rows, feature = hidden.shape
+    width = active.shape[1]
+    return order.kernel(
+        functools.partial(feed_back_out_body, len(gradients) == 2, slots),
+        [table, *gradients, hidden, gain, active],
+        [SMEM] + [VMEM] * (len(gradients) + 3),
+        [((rows, feature), jnp.float32, VMEM), ((3, feature), jnp.float32, VMEM), *gradient_outs(feature)],
+        [pltpu.VMEM((width, feature), jnp.bfloat16), pltpu.SemaphoreType.DMA((8,))],
+        name,
+        2 * rows * feature * width,
+        4 * feature * width,
+    )
+
+
+def feed_back_in_body(slots, units, table, gradient, slope, rows_in, *refs):
+    total_out, bias_in, keep, upper, lower, w_in, w_out, grad_hidden, stage, sems, out_sems = refs[4:]
+    feature = rows_in.shape[1]
+    tail = Loader(refs[2:4], table, sems).tall(units[1], w_out)
+    load = Loader(refs[:2], table, sems, len(tail))
+    waits = [load.wide(units[0] + j, w_in.at[j]) for j in range(4)]
+    store = Storer((keep, upper, lower), table, slots, out_sems)
+    total = gradient[...]
+    grad_low = low(total)
     wait_all(tail)
     for j in range(4):
         columns = slice(j * feature, (j + 1) * feature)
-        grad_hidden = dot_right(grad_low, w_out[columns, :]) * slope[:, columns].astype(jnp.float32)
-        bias_in[0:1, columns] = jnp.sum(grad_hidden, axis=0, keepdims=True)
-        gu_out[:, columns] = low(grad_hidden)
-    store.finish()
-
-
-def feed_back_out(gradients, hidden, gain, active, slope, buffers, table, cut, name):
-    rows, feature = hidden.shape
-    width = active.shape[1]
-    block = jax.ShapeDtypeStruct((4, feature // 2, feature), jnp.bfloat16)
-    return pl.pallas_call(
-        functools.partial(feed_back_out_body, cut, len(gradients) == 2),
-        out_shape=[
-            jax.ShapeDtypeStruct((rows, feature), jnp.float32),
-            jax.ShapeDtypeStruct((rows, width), jnp.bfloat16),
-            jax.ShapeDtypeStruct((3, feature), jnp.float32),
-            jax.ShapeDtypeStruct((1, width), jnp.float32),
-            block,
-            block,
-        ],
-        in_specs=[SMEM] + [VMEM] * (len(gradients) + 4) + [ANY] * 10,
-        out_specs=[VMEM] * 4 + [ANY] * 2,
-        scratch_shapes=[
-            pltpu.VMEM((width, feature), jnp.bfloat16),
-            pltpu.VMEM((width, feature), jnp.bfloat16),
-            pltpu.SemaphoreType.DMA((32,)),
-            pltpu.SemaphoreType.DMA((8,)),
-        ],
-        name=name,
-        **params(4 * rows * feature * width, 6 * feature * width),
-    )(table, *gradients, hidden, gain, active, slope, *buffers)
-
-
-def feed_back_in_body(cut, table, gradient, grad_hidden, rows_in, *refs):
-    buffers = refs[:10]
-    total_out, keep, send, w_in, stage, sems, out_sems = refs[10:]
-    feature = rows_in.shape[1]
-    load = Loader(buffers, table, cut, sems)
-    waits = [load.wide(j, w_in.at[j]) for j in range(4)]
-    store = Storer(keep, send, table, out_sems)
-    total = gradient[...]
-    for j in range(4):
-        columns = slice(j * feature, (j + 1) * feature)
+        hidden = dot_right(grad_low, w_out[columns, :]) * slope[:, columns].astype(jnp.float32)
+        bias_in[j : j + 1, :] = jnp.sum(hidden, axis=0, keepdims=True)
+        grad_hidden[:, columns] = low(hidden)
         stage[j] = low(dot_left(rows_in[...], grad_hidden[:, columns]))
         store.rows(stage.at[j], feature // 8, feature // 8, j * (feature // 8))
     for j in range(4):
@@ -707,43 +810,49 @@
     store.finish()
 
 
-def feed_back_in(gradient, grad_hidden, rows_in, buffers, table, cut, name):
+def feed_back_in(order, gradient, slope, rows_in, w_in, w_out, table, slots, name):
     rows, feature = rows_in.shape
-    width = grad_hidden.shape[1]
-    block = jax.ShapeDtypeStruct((4, feature // 2, feature), jnp.bfloat16)
-    return pl.pallas_call(
-        functools.partial(feed_back_in_body, cut),
-        out_shape=[jax.ShapeDtypeStruct((rows, feature), jnp.float32), block, block],
-        in_specs=[SMEM] + [VMEM] * 3 + [ANY] * 10,
-        out_specs=[VMEM] + [ANY] * 2,
-        scratch_shapes=[
-            pltpu.VMEM((4, feature, feature), jnp.bfloat16),
-            pltpu.VMEM((4, feature, feature), jnp.bfloat16),
-            pltpu.SemaphoreType.DMA((32,)),
+    width = slope.shape[1]
+    square = pltpu.VMEM((4, feature, feature), jnp.bfloat16)
+    return order.kernel(
+        functools.partial(feed_back_in_body, slots, (w_in[1], w_out[1])),
+        [table, gradient, slope, rows_in, *w_in[0], *w_out[0]],
+        [SMEM] + [VMEM] * 3 + [ANY] * 4,
+        [((rows, feature), jnp.float32, VMEM), ((4, feature), jnp.float32, VMEM), *gradient_outs(feature)],
+        [
+            square,
+            pltpu.VMEM((width, feature), jnp.bfloat16),
+            pltpu.VMEM((rows, width), jnp.bfloat16),
+            square,
+            pltpu.SemaphoreType.DMA((64,)),
             pltpu.SemaphoreType.DMA((32,)),
         ],
-        name=name,
-        **params(4 * rows * feature * width, 6 * feature * width),
-    )(table, gradient, grad_hidden, rows_in, *buffers)
-
-
-def attn_back_body(cross, first_unit, cut, table, gradient, *refs):
+        name,
+        6 * rows * feature * width,
+        6 * feature * width,
+    )
+
+
+def attn_back_body(cross, first_unit, others, slots, out_count, table, gradient, *refs):
     refs = list(refs)
+    other_sums = [refs.pop(0) for _ in range(others)]
     hidden, gain, q_in = refs[:3]
     refs = refs[3:]
     kv_in = refs.pop(0) if cross else q_in
     queries, keys, values, mixed, probs_in = refs[:5]
-    buffers = refs[5:15]
-    refs = refs[15:]
+    buffers = refs[5:7]
+    refs = refs[7:]
     q_grad_out = refs.pop(0)
     kv_grad_out = refs.pop(0) if cross else None
-    sums, keep, send, w_q, w_k, w_v, w_o, stage, go, gq, gk, gv, sems, out_sems = refs
+    sums = refs.pop(0)
+    grads = [refs.pop(0) for _ in range(out_count)]
+    w_q, w_k, w_v, w_o, stage, go, gq, gk, gv, vec_low, sems, out_sems = refs
     rows, feature = hidden.shape
     unit = feature // 8
-    load = Loader(buffers, table, cut, sems)
+    load = Loader(buffers, table, sems)
     wait_o = load.wide(first_unit + 3, w_o)
     waits = [load.wide(first_unit + i, w) for i, w in enumerate((w_q, w_k, w_v))]
-    store = Storer(keep, send, table, out_sems)
+    store = Storer(grads, table, slots, out_sems)
     lanes = head_lanes(rows)
     total, grad_gain, grad_shift = layer_norm_back(hidden[...], gain[...], gradient[...])
     sums[2:3, :] = jnp.sum(total, axis=0, keepdims=True)
@@ -780,6 +889,12 @@
         gq[:, columns] = low(grad_q)
         gk[:, columns] = low(grad_k)
         gv[:, columns] = low(grad_v)
+    if others:
+        parts = [sums[...]] + [other[...] for other in other_sums]
+        count = sum(part.shape[0] for part in parts)
+        parts.append(jnp.zeros((vec_low.shape[0] - count, feature), jnp.float32))
+        vec_low[...] = low(jnp.concatenate(parts, axis=0))
+        store.tail(vec_low)
     for index, (source, grad) in enumerate(((q_in, gq), (kv_in, gk), (kv_in, gv))):
         stage[index] = low(dot_left(source[...], grad[...]))
         store.rows(stage.at[index], unit, unit, index * unit)
@@ -795,64 +910,260 @@
     store.finish()
 
 
-def attn_back(gradient, hidden, gain, q_in, kv_in, saved, buffers, table, first_unit, cut, name):
+def attn_back(
+    order, gradient, hidden, gain, q_in, kv_in, saved, weights, table, others, slots, name, single=False
+):
     rows, feature = hidden.shape
     cross = kv_in is not None
-    wide = jax.ShapeDtypeStruct((rows, feature), jnp.float32)
-    block = jax.ShapeDtypeStruct((4, feature // 2, feature), jnp.bfloat16)
-    sources = [gradient, hidden, gain, q_in] + ([kv_in] if cross else []) + list(saved)
-    square = pltpu.VMEM((feature, feature), jnp.bfloat16)
-    low_rows = pltpu.VMEM((rows, feature), jnp.bfloat16)
-    return pl.pallas_call(
-        functools.partial(attn_back_body, cross, first_unit, cut),
-        out_shape=[wide] * (1 + cross)
-        + [jax.ShapeDtypeStruct((5, feature), jnp.float32), block, block],
-        in_specs=[SMEM] + [VMEM] * len(sources) + [ANY] * 10,
-        out_specs=[VMEM] * (2 + cross) + [ANY] * 2,
-        scratch_shapes=[square] * 4
+    sources = [gradient, *others, hidden, gain, q_in] + ([kv_in] if cross else []) + list(saved)
+    count = tile_up(5 + sum(other.shape[0] for other in others)) if others else 0
+    return order.kernel(
+        functools.partial(attn_back_body, cross, weights[1], len(others), slots, 2 if single else 3),
+        [table, *sources, *weights[0]],
+        [SMEM] + [VMEM] * len(sources) + [ANY] * 2,
+        [((rows, feature), jnp.float32, VMEM)] * (1 + cross)
+        + [((5, feature), jnp.float32, VMEM), *gradient_outs(feature, count, single)],
+        [pltpu.VMEM((feature, feature), jnp.bfloat16)] * 4
         + [pltpu.VMEM((4, feature, feature), jnp.bfloat16)]
-        + [low_rows] * 4
-        + [pltpu.SemaphoreType.DMA((32,)), pltpu.SemaphoreType.DMA((32,))],
-        name=name,
-        **params(16 * rows * feature * feature, 20 * feature * feature),
-    )(table, *sources, *buffers)
-
-
-def line_sum(value):
-    place = lax.axis_index("rep")
-    inner = (place == 1) | (place == 2)
-    half = add_low(value, lax.ppermute(value, "rep", [(0, 1), (3, 2)]))
-    total = add_low(half, lax.ppermute(half, "rep", [(1, 2), (2, 1)]))
-    return jnp.where(inner, total, lax.ppermute(total, "rep", [(1, 0), (2, 3)]))
-
-
-def reduce_blocks(keep, send, vec_blocks=None):
-    full = add_low(keep, swap(send, 1))
-    if vec_blocks is not None:
-        full = jnp.concatenate([full, add_low(vec_blocks[0], swap(vec_blocks[1], 1))], axis=1)
-    cut = tile_up(full.shape[1] // 2)
-    low_x = swap(full[3, :cut], 2)
-    low_y = swap(full[3, cut:], 4)
-    to_x = jnp.concatenate([full[1, :cut], add_low(full[1, cut:], low_y)], axis=0)
-    to_y = jnp.concatenate([add_low(full[2, :cut], low_x), full[2, cut:]], axis=0)
-    return line_sum(add_low(full[0], swap(to_x, 2), swap(to_y, 4)))
-
-
-def vec_blocks(rows_list, tail, table, feature):
-    flat = jnp.concatenate([rows.reshape(-1) for rows in rows_list] + [tail.reshape(-1)])
-    parts = flat.astype(jnp.bfloat16).reshape(8, -1)
-    chosen = (table[:, None] == jnp.arange(8, dtype=jnp.int32)[None, :]).astype(jnp.bfloat16)
-    placed = dot_plain(chosen, parts).astype(jnp.bfloat16)
-    count = tile_up(-(-parts.shape[1] // feature))
-    placed = jnp.pad(placed, ((0, 0), (0, count * feature - parts.shape[1])))
-    placed = placed.reshape(4, 2, count, feature)
-    return (placed[:, 0], placed[:, 1])
-
-
-def wide_out(block, feature):
+        + [pltpu.VMEM((rows, feature), jnp.bfloat16)] * 4
+        + [pltpu.VMEM((max(count, ROW_TILE), feature), jnp.bfloat16)]
+        + [pltpu.SemaphoreType.DMA((32,)), pltpu.SemaphoreType.DMA((34,))],
+        name,
+        16 * rows * feature * feature,
+        20 * feature * feature,
+    )
+
+
+def combine_body(plan, count, *refs):
+    inputs = refs[:count]
+    outs = refs[count:-4]
+    landed, summed, in_sems, out_sems = refs[-4:]
+    loads = []
+    place = 0
+    for out, first, rows, terms in plan:
+        parts = []
+        for source, row in terms:
+            copy = pltpu.make_async_copy(
+                inputs[source].at[pl.ds(row, rows), :],
+                landed.at[pl.ds(place, rows), :],
+                in_sems.at[sum(len(other) for other in loads) + len(parts)],
+            )
+            copy.start()
+            parts.append((copy, place))
+            place += rows
+        loads.append(parts)
+    stores = []
+    place = 0
+    for (out, first, rows, terms), parts in zip(plan, loads):
+        total = None
+        for copy, start in parts:
+            copy.wait()
+            term = landed[start : start + rows, :].astype(jnp.float32)
+            total = term if total is None else total + term
+        summed[place : place + rows, :] = low(total)
+        copy = pltpu.make_async_copy(
+            summed.at[pl.ds(place, rows), :],
+            outs[out].at[pl.ds(first, rows), :],
+            out_sems.at[len(stores)],
+        )
+        copy.start()
+        stores.append(copy)
+        place += rows
+    wait_all(stores)
+
+
+def combine(order, name, *jobs):
+    inputs, plan, outs = [], [], []
+    for sizes, sums, use in jobs:
+        for out, first, rows, terms in sums:
+            places = []
+            for array, row in terms:
+                known = [index for index, other in enumerate(inputs) if other is array]
+                if not known:
+                    inputs.append(array)
+                places.append((known[0] if known else len(inputs) - 1, row))
+            plan.append((len(outs) + out, first, rows, tuple(places)))
+        outs += sizes
+    feature = inputs[0].shape[1]
+    reads = sum(rows * len(terms) for out, first, rows, terms in plan)
+    writes = sum(rows for out, first, rows, terms in plan)
+    results = order.kernel(
+        functools.partial(combine_body, plan, len(inputs)),
+        inputs,
+        [ANY] * len(inputs),
+        [((rows, feature), jnp.bfloat16, ANY) for rows in outs],
+        [
+            pltpu.VMEM((reads, feature), jnp.bfloat16),
+            pltpu.VMEM((writes, feature), jnp.bfloat16),
+            pltpu.SemaphoreType.DMA((sum(len(terms) for out, first, rows, terms in plan),)),
+            pltpu.SemaphoreType.DMA((len(plan),)),
+        ],
+        name,
+    )
+    for sizes, sums, use in jobs:
+        use(*results[: len(sizes)])
+        results = results[len(sizes) :]
+
+
+OWN, X, Y, DIAGONAL = range(4)
+X_FIRST = (OWN, Y, X, DIAGONAL)
+Y_FIRST = (OWN, X, Y, DIAGONAL)
+
+
+class Reduce:
+    def __init__(self, order, outs, slots, both=False, pad=0):
+        self.order = order
+        self.pad = pad
+        self.keep, self.upper, self.lower = outs if len(outs) == 3 else (outs[0], None, outs[1])
+        self.both = both
+        self.bits = (2, 4) if slots == X_FIRST else (4, 2)
+        self.rows = self.keep.shape[1] // 2
+        self.extra = self.keep.shape[0] - 4 * self.rows
+
+    def cores(self):
+        self.from_upper = None if self.upper is None else swap(self.order.tie(self.upper), 1)
+        self.from_lower = swap(self.order.tie(self.lower), 1)
+
+    def cores_done(self):
+        self.order.mark(*(value for value in (self.from_upper, self.from_lower) if value is not None))
+
+    def block(self, slot, first=0):
+        row = slot * self.rows + first
+        other = (self.from_lower, row) if slot < 2 or self.upper is None else (self.from_upper, row - 2 * self.rows)
+        return ((self.keep, row), other)
+
+    def extra_rows(self):
+        return ((self.keep, 4 * self.rows), (self.from_lower, (4 if self.upper is None else 2) * self.rows))
+
+    def first(self):
+        rows, extra = self.rows, self.extra
+        if not self.both:
+            plan = [(0, 0, rows, self.block(2)), (0, rows, rows, self.block(3))]
+            if extra:
+                plan.append((0, 2 * rows, extra, self.extra_rows()))
+            if self.pad:
+                plan.append((0, 2 * rows + extra, self.pad, self.block(2)[:1]))
+            return ([2 * rows + extra + self.pad], plan, self.first_sent)
+        cut = rows // 2
+        plan = [(0, 0, cut, self.block(3)), (1, 0, cut, self.block(3, cut))]
+        if extra:
+            plan.append((0, cut, extra, self.extra_rows()))
+        return ([cut + extra, cut], plan, self.first_sent)
+
+    def first_sent(self, *sent):
+        self.sent = sent[0]
+        self.landed = [swap(value, bit) for value, bit in zip(sent, (2, 4) if self.both else self.bits)]
+
+    def second(self):
+        rows, extra = self.rows, self.extra
+        if not self.both:
+            landed = self.landed[0]
+            plan = [(0, 0, rows, self.block(1) + ((landed, rows),))]
+            if extra:
+                plan.append((0, rows, extra, ((self.sent, 2 * rows), (landed, 2 * rows))))
+            return ([rows + extra], plan, self.second_sent)
+        cut = rows // 2
+        from_x, from_y = self.landed
+        plan = [
+            (0, 0, cut, self.block(1)),
+            (0, cut, cut, self.block(1, cut) + ((from_y, 0),)),
+            (1, 0, cut, self.block(2) + ((from_x, 0),)),
+            (1, cut, cut, self.block(2, cut)),
+        ]
+        if extra:
+            plan.append((1, rows, extra, ((self.sent, cut), (from_x, cut))))
+        return ([rows, rows + extra], plan, self.second_sent)
+
+    def second_sent(self, *sent):
+        self.sent_last = sent[-1]
+        self.last = [swap(value, bit) for value, bit in zip(sent, (2, 4) if self.both else self.bits[1:])]
+
+    def own(self, use):
+        rows, extra = self.rows, self.extra
+        terms = self.block(0) + tuple((value, 0) for value in self.last)
+        if not self.both:
+            terms += ((self.landed[0], 0),)
+        plan = [(0, 0, rows, terms)]
+        if extra:
+            plan.append((0, rows, extra, ((self.sent_last, rows), (self.last[-1], rows))))
+        return ([rows + extra], plan, use)
+
+
+def own_stack(pieces, use):
+    rows = pieces[0].rows
+    plan = [(0, index * rows) + piece.own(None)[1][0][2:] for index, piece in enumerate(pieces)]
+    return ([len(pieces) * rows], plan, use)
+
+
+class Line:
+    def __init__(self, value):
+        self.value = value
+        self.landed = lax.ppermute(value, "rep", [(0, 1), (3, 2)])
+
+    def part(self, first):
+        return (self, first)
+
+    def step(self, use):
+        rows = self.value.shape[0]
+        return ([rows], [(0, 0, rows, ((self.value, 0), (self.landed, 0)))], use)
+
+    def middle(self):
+        return self.step(self.middle_sent)
+
+    def middle_sent(self, value):
+        self.value = value
+        self.landed = lax.ppermute(value, "rep", [(1, 2), (2, 1)])
+
+    def outward(self):
+        return self.step(self.outward_sent)
+
+    def outward_sent(self, value):
+        self.value = value
+        self.landed = lax.ppermute(value, "rep", [(1, 0), (2, 3)])
+
+
+def finish_body(parts, inner, *refs):
+    wide, rest = refs[2 * len(parts)], list(refs[2 * len(parts) + 1 :])
+    feature = refs[0].shape[1]
     unit = feature // 8
-    parts = [block[j * unit : (j + 1) * unit] for j in range(4)]
-    return jnp.concatenate(parts, axis=1).astype(jnp.float32)
+    for index, first in enumerate(parts):
+        value, landed = refs[2 * index], refs[2 * index + 1]
+
+        def rows(begin, count):
+            mine = value[first + begin : first + begin + count, :].astype(jnp.float32)
+            other = landed[first + begin : first + begin + count, :].astype(jnp.float32)
+            return jnp.where(inner[0] == 1, mine, other)
+
+        for j in range(4):
+            column = (4 * index + j) * feature
+            if wide.shape[0] == unit:
+                wide[:, column : column + feature] = rows(j * unit, unit)
+            else:
+                wide[j * unit : (j + 1) * unit, :] = rows(j * unit, unit)
+        if first == 0 and value.shape[0] % (4 * unit):
+            rest.pop(0)[...] = rows(4 * unit, value.shape[0] - 4 * unit)
+
+
+def finish(order, inner, parts, wide, name):
+    operands = [inner]
+    for line, first in parts:
+        operands += [line.value, line.landed]
+    feature = operands[1].shape[1]
+    unit = feature // 8
+    shape = (unit, 4 * feature * len(parts)) if wide else (4 * unit, feature)
+    outs = [(shape, jnp.float32, VMEM)]
+    for line, first in parts:
+        rows = line.value.shape[0] % (4 * unit)
+        if rows:
+            outs.append(((rows, feature), jnp.float32, VMEM))
+    return order.kernel(
+        functools.partial(finish_body, [first for line, first in parts]),
+        operands,
+        [SMEM] + [VMEM] * (len(operands) - 1),
+        outs,
+        [],
+        name,
+    )
 
 
 def per_device(
@@ -874,79 +1185,156 @@
 ):
     feature = enc_in.shape[1]
     unit = feature // 8
-    table = lax.axis_index("fsdp").astype(jnp.int32) ^ jnp.arange(8, dtype=jnp.int32)
+    chip_index = lax.axis_index("fsdp").astype(jnp.int32)
+    table = chip_index ^ jnp.arange(8, dtype=jnp.int32)
+    place = lax.axis_index("rep")
+    inner = ((place == 1) | (place == 2)).astype(jnp.int32).reshape(1)
     ids = (table, bucket)
-    e_attn = gather_piece(pack_units([enc_attn, vec_rows(enc_vec, feature)], feature), 2 * unit)
-    e_feed = gather_piece(pack_units([enc_w1, enc_w2], feature), 4 * unit)
-    d_attn = gather_piece(pack_units([dec_attn, vec_rows(dec_vec, feature)], feature), 4 * unit)
-    d_feed = gather_piece(pack_units([dec_w1, dec_w2], feature), 4 * unit)
-    e_vec = gathered_vec(e_attn, 2 * unit, 4 * unit, table, enc_vec.shape[0], feature)
-    e_rows, e_tail = unpack(e_vec, 8, feature)
-    e_tail = e_tail.reshape(1, -1)
+    order = Order()
+    mark = order.mark
+    g_1, g_2, g_3, g_4 = (Gather(order, feature, "piece_" + name) for name in "1234")
+    half = 4 * unit
+    e_len, d_len = enc_vec.shape[0], dec_vec.shape[0]
+    vec_part = vec_rows(jnp.concatenate([enc_vec, dec_vec]), feature)
+    g_1.sides(enc_attn, dec_attn[:, : 4 * feature], vec_part)
+    g_2.sides(enc_w1, enc_w2)
+    g_1.corners()
+    g_2.corners()
+    mark(*g_2.mine[3:])
+    (attn_pair,) = g_1.join((0, 2 * half + vec_part.shape[0]))
+    (e_feed,) = g_2.join((0, 2 * half))
+    g_3.sides(dec_attn[:, 4 * feature :], dec_w1)
+    vecs = gathered_vec(order, attn_pair, table, vec_part.shape[0], feature)
+    e_rows, e_tail = unpack(vecs[:, :e_len].reshape(-1), 8, feature)
+    d_rows, d_tail = unpack(vecs[:, e_len : e_len + d_len].reshape(-1), 13, feature)
+    e_tail, d_tail = e_tail.reshape(1, -1), d_tail.reshape(1, -1)
     e_hid_a, e_first, *e_saved = attn_forward(
-        enc_in, None, e_rows[0:5], e_attn, ids, enc_lengths, 0, 2 * unit, False, "enc_attn"
-    )
+        order, enc_in, None, e_rows[0:5], (attn_pair, 0), ids, enc_lengths, False, "enc_attn"
+    )
+    mark(e_feed[1], d_rows, d_tail, e_tail)
+    g_4.sides(dec_w2)
+    d_hid_s, d_first, *s_saved = attn_forward(
+        order, dec_in, None, d_rows[0:5], (attn_pair, 4), ids, dec_lengths, True, "dec_self"
+    )
+    g_3.corners()
     e_hid_f, encoded, e_act, e_slope = feed_forward(
-        e_first, e_rows[5:8], e_tail, e_feed, table, 4 * unit, "enc_feed"
-    )
-    d_vec = gathered_vec(d_attn, 4 * unit, 8 * unit, table, dec_vec.shape[0], feature)
-    d_rows, d_tail = unpack(d_vec, 13, feature)
-    d_tail = d_tail.reshape(1, -1)
-    d_hid_s, d_first, *s_saved = attn_forward(
-        dec_in, None, d_rows[0:5], d_attn, ids, dec_lengths, 0, 4 * unit, True, "dec_self"
-    )
+        order, e_first, e_rows[5:8], e_tail, (e_feed, 0), (e_feed, 4), table, "enc_feed"
+    )
+    g_4.corners()
+    cross_pair, w1_pair = g_3.join((0, half), (half, half))
+    (w2_pair,) = g_4.join((0, half))
     d_hid_c, d_second, *c_saved = attn_forward(
-        d_first, encoded, d_rows[5:10], d_attn, ids, enc_lengths, 4, 4 * unit, False, "dec_cross"
+        order, d_first, encoded, d_rows[5:10], (cross_pair, 0), ids, enc_lengths, False, "dec_cross"
     )
     d_hid_f, decoded, d_act, d_slope = feed_forward(
-        d_second, d_rows[10:13], d_tail, d_feed, table, 4 * unit, "dec_feed"
-    )
-    gradient, d_gu, d_sums_f, d_bias, keep, send = feed_back_out(
-        [dec_cot], d_hid_f, d_rows[11:12], d_act, d_slope, d_feed, table, 4 * unit, "dec_feed_back_out"
-    )
-    grad_d_w2 = reduce_blocks(keep, send)
-    gradient, keep, send = feed_back_in(
-        gradient, d_gu, d_second, d_feed, table, 4 * unit, "dec_feed_back_in"
-    )
-    grad_d_w1 = reduce_blocks(keep, send)
-    gradient, grad_encoded, d_sums_c, keep, send = attn_back(
-        gradient, d_hid_c, d_rows[8:9], d_first, encoded, c_saved, d_attn, table, 4, 4 * unit, "cross_back"
-    )
-    grad_d_cross = reduce_blocks(keep, send)
-    e_gradient, e_gu, e_sums_f, e_bias, keep, send = feed_back_out(
-        [enc_cot, grad_encoded], e_hid_f, e_rows[6:7], e_act, e_slope, e_feed, table, 4 * unit, "enc_feed_back_out"
-    )
-    grad_e_w2 = reduce_blocks(keep, send)
-    e_gradient, keep, send = feed_back_in(
-        e_gradient, e_gu, e_first, e_feed, table, 4 * unit, "enc_feed_back_in"
-    )
-    grad_e_w1 = reduce_blocks(keep, send)
-    dec_in_grad, d_sums_s, keep, send = attn_back(
-        gradient, d_hid_s, d_rows[3:4], dec_in, None, s_saved, d_attn, table, 0, 4 * unit, "self_back"
-    )
-    grad_d_self = reduce_blocks(
-        keep, send, vec_blocks([d_sums_s, d_sums_c, d_sums_f], d_bias, table, feature)
-    )
-    enc_in_grad, e_sums_a, keep, send = attn_back(
-        e_gradient, e_hid_a, e_rows[3:4], enc_in, None, e_saved, e_attn, table, 0, 2 * unit, "enc_attn_back"
-    )
-    grad_e_attn = reduce_blocks(
-        keep, send, vec_blocks([e_sums_a, e_sums_f], e_bias, table, feature)
-    )
-    d_wide = jnp.concatenate([wide_out(grad_d_self, feature), wide_out(grad_d_cross, feature)], axis=1)
+        order, d_second, d_rows[10:13], d_tail, (w1_pair, 0), (w2_pair, 0), table, "dec_feed"
+    )
+    gradient, d_sums_f, *outs = feed_back_out(
+        order, [dec_cot], d_hid_f, d_rows[11:12], d_act, table, X_FIRST, "dec_back_out"
+    )
+    red_0 = Reduce(order, outs, X_FIRST)
+    red_0.cores()
+    gradient, d_bias, *outs = feed_back_in(
+        order, gradient, d_slope, d_second, (w1_pair, 0), (w2_pair, 0), table, Y_FIRST, "dec_back_in"
+    )
+    red_1 = Reduce(order, outs, Y_FIRST)
+    red_0.cores_done()
+    combine(order, "add_1", red_0.first())
+    red_1.cores()
+    gradient, grad_encoded, d_sums_c, *outs = attn_back(
+        order, gradient, d_hid_c, d_rows[8:9], d_first, encoded, c_saved, (cross_pair, 0), table, [],
+        X_FIRST, "cross_back",
+    )
+    red_2 = Reduce(order, outs, X_FIRST)
+    red_1.cores_done()
+    combine(order, "add_2", red_1.first())
+    red_2.cores()
+    e_gradient, e_sums_f, *outs = feed_back_out(
+        order, [enc_cot, grad_encoded], e_hid_f, e_rows[6:7], e_act, table, Y_FIRST, "enc_back_out"
+    )
+    red_3 = Reduce(order, outs, Y_FIRST, pad=2 * ROW_TILE)
+    combine(order, "add_3a", red_0.second())
+    red_2.cores_done()
+    combine(order, "add_3b", red_2.first())
+    red_3.cores()
+    e_gradient, e_bias, *outs = feed_back_in(
+        order, e_gradient, e_slope, e_first, (e_feed, 0), (e_feed, 4), table, X_FIRST, "enc_back_in"
+    )
+    red_4 = Reduce(order, outs, X_FIRST)
+    totals = {}
+
+    def keep_as(key):
+        return lambda value: totals.update({key: value})
+
+    mark(*red_0.last)
+    combine(order, "add_4a", red_1.second())
+    red_3.cores_done()
+    combine(order, "add_4b", red_3.first())
+    red_4.cores()
+    dec_in_grad, d_sums_s, *outs = attn_back(
+        order, gradient, d_hid_s, d_rows[3:4], dec_in, None, s_saved, (attn_pair, 4), table,
+        [d_sums_c, d_sums_f, d_bias], Y_FIRST, "self_back",
+    )
+    red_5 = Reduce(order, outs, Y_FIRST, True)
+    combine(order, "add_5a", red_2.second())
+    mark(*red_1.last)
+    red_4.cores_done()
+    combine(order, "add_5b", red_4.first())
+    red_5.cores()
+    enc_in_grad, e_sums_a, *outs = attn_back(
+        order, e_gradient, e_hid_a, e_rows[3:4], enc_in, None, e_saved, (attn_pair, 0), table,
+        [e_sums_f, e_bias], Y_FIRST, "enc_attn_back", True,
+    )
+    red_6 = Reduce(order, outs, Y_FIRST, True)
+    red_5.cores_done()
+    mark(*red_2.last)
+    combine(
+        order, "add_6a", red_3.second(), red_5.first(), own_stack([red_0, red_1], keep_as("a"))
+    )
+    line_a = Line(totals["a"])
+    mark(red_5.landed[1])
+    combine(order, "add_6b", red_4.second())
+    red_6.cores()
+    mark(*red_3.last)
+    red_6.cores_done()
+    combine(order, "add_6c", red_6.first())
+    mark(*red_6.landed, *red_4.last)
+    combine(order, "add_8", line_a.middle(), red_5.second(), own_stack([red_2, red_3], keep_as("b")))
+    line_b = Line(totals["b"])
+    mark(*red_5.last)
+    combine(order, "add_9", red_6.second(), red_4.own(keep_as(4)), red_5.own(keep_as(5)))
+    combine(order, "add_10", line_a.outward(), line_b.middle(), red_6.own(keep_as(6)))
+    line_4 = Line(totals[4])
+    line_5 = Line(order.tie(totals[5]))
+    combine(order, "add_11", line_b.outward(), line_4.middle())
+    combine(order, "add_12", line_5.middle())
+    line_6 = Line(order.tie(totals[6]))
+    (grad_d_w2,) = finish(order, inner, [line_a.part(0)], False, "out_0")
+    (grad_d_w1,) = finish(order, inner, [line_a.part(half)], True, "out_1")
+    combine(order, "add_13", line_4.outward(), line_6.middle())
+    combine(order, "add_14", line_5.outward())
+    (grad_e_w2,) = finish(order, inner, [line_b.part(half)], False, "out_3")
+    (grad_e_w1,) = finish(order, inner, [line_4.part(0)], True, "out_4")
+    combine(order, "add_15", line_6.outward())
+    grad_d_attn, d_vec = finish(order, inner, [line_5.part(0), line_b.part(0)], True, "out_5")
+    grad_e_attn, e_vec = finish(order, inner, [line_6.part(0)], True, "out_6")
+
+    def own_part(rows, length):
+        return lax.dynamic_slice(rows.reshape(-1), (chip_index * length,), (length,))
+
     return (
         encoded,
         decoded,
         enc_in_grad,
         dec_in_grad,
-        wide_out(grad_e_attn, feature),
-        grad_e_attn[4 * unit :].reshape(-1)[: enc_vec.shape[0]].astype(jnp.float32),
-        wide_out(grad_e_w1, feature),
-        grad_e_w2.astype(jnp.float32),
-        d_wide,
-        grad_d_self[4 * unit :].reshape(-1)[: dec_vec.shape[0]].astype(jnp.float32),
-        wide_out(grad_d_w1, feature),
-        grad_d_w2.astype(jnp.float32),
+        grad_e_attn,
+        own_part(e_vec, e_len),
+        grad_e_w1,
+        grad_e_w2,
+        grad_d_attn,
+        own_part(d_vec, d_len),
+        grad_d_w1,
+        grad_d_w2,
     )
 
 

time: 627 us -> 552 us (0.88)
  waiting for transfers between devices: 334 us -> 174 us
  Pallas kernels: 121 us -> 231 us
  other arithmetic: 26.3 us -> 3.67 us
  starting transfers between devices: 87.9 us -> 78.2 us
  local copies, waits for them, and re-layouts: 43.5 us -> 51.9 us
    pallas_call x12 -> x50, Pallas kernels: 121 us -> 231 us  [kernel(): pl.pallas_call(lambda *refs: body(*refs[:count], *refs[count + skip:]), o...]
    ppermute x73 -> x52, waiting for transfers between devices: 199 us -> 113 us  [swap(): return lax.ppermute(value, 'fsdp', [(i, i ^ bit) for i in range(8)])]
    ppermute x21 -> x15, waiting for transfers between devices: 135 us -> 61.1 us  [the longest x5 30.9 us: __init__(): self.landed = lax.ppermute(value, 'rep', [(0, 1), (3, 2)])]
    convert_element_type x46 -> x4, other arithmetic: 22.1 us -> 1.24 us  [unpack(): vector[:row_count * feature].astype(jnp.float32).reshape(row_count, feature)]
    unnamed x153 -> x154, local copies, waits for them, and re-layouts: 24.2 us -> 39.8 us
    ppermute x73 -> x52, starting transfers between devices: 56.4 us -> 46.5 us  [swap(): return lax.ppermute(value, 'fsdp', [(i, i ^ bit) for i in range(8)])]
    slice x36 -> x3, local copies, waits for them, and re-layouts: 10 us -> 2.33 us  [the longest x1 2.33 us: per_device(): g_3.sides(dec_attn[:, 4 * feature:], dec_w1)]
    ppermute x21 -> x15, starting transfers between devices: 31.5 us -> 31.7 us  [the longest x5 20.1 us: __init__(): self.landed = lax.ppermute(value, 'rep', [(0, 1), (3, 2)])]
  transfers between devices with their start and end apart: 94 -> 67, of which waited for: 37 -> 24; matrix products, arithmetic and copies ran while one was open for 9% -> 2% of each run, Pallas kernels for 17% -> 35%
where the time goes in v3:
time: 552 us; the launch traced here: 541 us
  Pallas kernels  231 us (42%)
  waiting for transfers between devices  174 us (32%)
  starting transfers between devices  78.2 us (14%)
  local copies, waits for them, and re-layouts  51.9 us (9%)
    pallas_call x50, Pallas kernels, kernel(): pl.pallas_call(lambda *refs: body(*refs[:count], *refs[count + skip:]), o...  231 us
    ppermute x52, waiting for transfers between devices, swap(): return lax.ppermute(value, 'fsdp', [(i, i ^ bit) for i in range(8)])  113 us
    ppermute x52, starting transfers between devices, swap(): return lax.ppermute(value, 'fsdp', [(i, i ^ bit) for i in range(8)])  46.5 us
    unnamed x154, local copies, waits for them, and re-layouts  39.8 us
    ppermute x5, waiting for transfers between devices, __init__(): self.landed = lax.ppermute(value, 'rep', [(0, 1), (3, 2)])  30.9 us
    ppermute x5, waiting for transfers between devices, outward_sent(): self.landed = lax.ppermute(value, 'rep', [(1, 0), (2, 3)])  30.2 us
    ppermute x5, starting transfers between devices, __init__(): self.landed = lax.ppermute(value, 'rep', [(0, 1), (3, 2)])  20.1 us
  transfers between devices with their start and end apart: 67, of which 24 were waited for; matrix products, arithmetic and copies ran while one was open for 2% of the time, Pallas kernels for 35%

profile of v3, /device:TPU:0, one launch (start us, length us, event | category | flops | bytes accessed | tf_op | source)
XLA Modules:
  0.0 541.3 jit_solution(15287678759391597480)
XLA Ops:
  14.0 23.2 %collective-permute-done.1.refs_1_.refs_2_ = bf16[784,768]{1,0:T(8,128)(2,1)S(1)} collective-permute-done((bf16[784,768]{1,0:T(8,128)(2,1)}, bf16[784,768]{1,0:T(8,128)(2,1)S(1)}, u32[]{:S(2)}, u32[]{:S(2)}) %collective-permute-start.1) | collective-permute-done | bytes 1204256 | tf_op jit(solution)/shard_map/ppermute | solution.py:325
  45.7 16.8 %collective-permute-done.5.refs_1_.refs_2_ = bf16[768,768]{1,0:T(8,128)(2,1)S(1)} collective-permute-done((bf16[768,768]{1,0:T(8,128)(2,1)}, bf16[768,768]{1,0:T(8,128)(2,1)S(1)}, u32[]{:S(2)}, u32[]{:S(2)}) %collective-permute-start.5) | collective-permute-done | bytes 1179680 | tf_op jit(solution)/shard_map/ppermute | solution.py:325
  70.7 4.4 collective-permute-done.2.refs_3_
  75.1 13.8 %collective-permute-done.7.refs_6_.refs_4_ = bf16[384,768]{1,0:T(8,128)(2,1)S(1)} collective-permute-done((bf16[384,768]{1,0:T(8,128)(2,1)}, bf16[384,768]{1,0:T(8,128)(2,1)S(1)}, u32[]{:S(2)}, u32[]{:S(2)}) %collective-permute-start.7) | collective-permute-done | bytes 589856 | tf_op jit(solution)/shard_map/ppermute | solution.py:325
  108.7 8.4 %enc_attn.1 = (f32[256,768]{1,0:T(8,128)}, bf16[256,768]{1,0:T(8,128)(2,1)}, bf16[256,768]{1,0:T(8,128)(2,1)}, bf16[256,768]{1,0:T(8,128)(2,1)}, bf16[256,768]{1...) custom-call(s32[8]{0:T(128)} %iota_xor_fusion.refs_0_, s32[1]{0:T(128)S(6)} %copy.27.refs_1_, ...), custom_call_target="tpu_custom_call" | custom-call | flops 1207959552 | bytes 5898240 | tf_op jit(solution)/shard_map/enc_attn/pallas_call | solution.py:364
  123.5 8.7 %dec_self.1 = (f32[256,768]{1,0:T(8,128)}, bf16[256,768]{1,0:T(8,128)(2,1)}, bf16[256,768]{1,0:T(8,128)(2,1)}, bf16[256,768]{1,0:T(8,128)(2,1)}, bf16[256,768]{1...) custom-call(s32[8]{0:T(128)} %iota_xor_fusion.refs_0_, s32[1]{0:T(128)S(6)} %copy.27.refs_1_, ...), custom_call_target="tpu_custom_call" | custom-call | flops 1207959552 | bytes 5898240 | tf_op jit(solution)/shard_map/dec_self/pallas_call | solution.py:364
  139.4 9.6 %enc_feed.1 = (f32[256,768]{1,0:T(8,128)}, bf16[256,768]{1,0:T(8,128)(2,1)}, bf16[256,3072]{1,0:T(8,128)(2,1)}, bf16[256,3072]{1,0:T(8,128)(2,1)}) custom-call(s32[8]{0:T(128)} %iota_xor_fusion.refs_0_, bf16[256,768]{1,0:T(8,128)(2,1)} %get-tuple-element.145.refs_1_.refs_3_, f32[3,768]{1,0:T(4,128)} %slice.123.refs_2_, f32[1,3072]{1,0:T(1,128)} %bitcast.8, ...), custom_call_target="tpu_custom_call" | custom-call | flops 2415919104 | bytes 18874368 | tf_op jit(solution)/shard_map/enc_feed/pallas_call | solution.py:364
  169.9 8.5 %dec_cross.1 = (f32[256,768]{1,0:T(8,128)}, bf16[256,768]{1,0:T(8,128)(2,1)}, bf16[256,768]{1,0:T(8,128)(2,1)}, bf16[256,768]{1,0:T(8,128)(2,1)}, bf16[256,768]{...) custom-call(s32[8]{0:T(128)} %iota_xor_fusion.refs_0_, s32[1]{0:T(128)S(6)} %copy.27.refs_1_, ...), custom_call_target="tpu_custom_call" | custom-call | flops 1207959552 | bytes 5898240 | tf_op jit(solution)/shard_map/dec_cross/pallas_call | solution.py:364
  180.7 9.3 %dec_feed.1 = (f32[256,768]{1,0:T(8,128)}, bf16[256,768]{1,0:T(8,128)(2,1)}, bf16[256,3072]{1,0:T(8,128)(2,1)}, bf16[256,3072]{1,0:T(8,128)(2,1)}) custom-call(s32[8]{0:T(128)} %iota_xor_fusion.refs_0_, bf16[256,768]{1,0:T(8,128)(2,1)} %get-tuple-element.156.refs_1_.refs_3_, f32[3,768]{1,0:T(4,128)} %slice.130.refs_2_, f32[1,3072]{1,0:T(1,128)} %bitcast.6, ...), custom_call_target="tpu_custom_call" | custom-call | flops 2415919104 | bytes 18874368 | tf_op jit(solution)/shard_map/dec_feed/pallas_call | solution.py:364
  189.9 7.1 %dec_back_out.1 = (f32[256,768]{1,0:T(8,128)}, f32[3,768]{1,0:T(4,128)}, bf16[1536,768]{1,0:T(8,128)(2,1)}, bf16[768,768]{1,0:T(8,128)(2,1)}, bf16[768,768]{1,0:T(8,128)(2,1)}) custom-call(s32[8]{0:T(128)} %iota_xor_fusion.refs_0_, bf16[256,768]{1,0:T(8,128)(2,1)} %refs_1_.9, f32[256,768]{1,0:T(8,128)} %get-tuple-element.160.refs_2_.refs_5_, ...), custom_call_target="tpu_custom_call" | custom-call | flops 1207959552 | bytes 9437184 | tf_op jit(solution)/shard_map/dec_back_out/pallas_call | solution.py:364
  197.6 11.3 %dec_back_in.1 = (f32[256,768]{1,0:T(8,128)}, f32[4,768]{1,0:T(4,128)}, bf16[1536,768]{1,0:T(8,128)(2,1)}, bf16[768,768]{1,0:T(8,128)(2,1)}, bf16[768,768]{1,0:T(8,128)(2,1)}) custom-call(s32[8]{0:T(128)} %iota_xor_fusion.refs_0_, f32[256,768]{1,0:T(8,128)} %get-tuple-element.162.refs_1_, bf16[256,3072]{1,0:T(8,128)(2,1)} %get-tuple-element.163.refs_2_, ...), custom_call_target="tpu_custom_call" | custom-call | flops 3623878656 | bytes 14155776 | tf_op jit(solution)/shard_map/dec_back_in/pallas_call | solution.py:364
  215.9 13.4 %cross_back.1 = (f32[256,768]{1,0:T(8,128)}, f32[256,768]{1,0:T(8,128)}, f32[5,768]{1,0:T(8,128)}, bf16[1536,768]{1,0:T(8,128)(2,1)}, bf16[768,768]{1,0:T(8,128)(2,1)}, /*index=5*/bf16[768,768]{1,0:T(8,128)(2,1)}) custom-call(s32[8]{0:T(128)} %iota_xor_fusion.refs_0_, f32[256,768]{1,0:T(8,128)} %get-tuple-element.169.refs_1_, ...), custom_call_target="tpu_custom_call" | custom-call | flops 2415919104 | bytes 11796480 | tf_op jit(solution)/shard_map/cross_back/pallas_call | solution.py:364
  236.1 7.1 %enc_back_out.1 = (f32[256,768]{1,0:T(8,128)}, f32[3,768]{1,0:T(4,128)}, bf16[1536,768]{1,0:T(8,128)(2,1)}, bf16[768,768]{1,0:T(8,128)(2,1)}, bf16[768,768]{1,0:T(8,128)(2,1)}) custom-call(s32[8]{0:T(128)} %iota_xor_fusion.refs_0_, bf16[256,768]{1,0:T(8,128)(2,1)} %refs_1_.10, f32[256,768]{1,0:T(8,128)} %get-tuple-element.183.refs_2_, ...), custom_call_target="tpu_custom_call" | custom-call | flops 1207959552 | bytes 9437184 | tf_op jit(solution)/shard_map/enc_back_out/pallas_call | solution.py:364
  254.0 11.3 %enc_back_in.1 = (f32[256,768]{1,0:T(8,128)}, f32[4,768]{1,0:T(4,128)}, bf16[1536,768]{1,0:T(8,128)(2,1)}, bf16[768,768]{1,0:T(8,128)(2,1)}, bf16[768,768]{1,0:T(8,128)(2,1)}) custom-call(s32[8]{0:T(128)} %iota_xor_fusion.refs_0_, f32[256,768]{1,0:T(8,128)} %get-tuple-element.193.refs_1_, bf16[256,3072]{1,0:T(8,128)(2,1)} %get-tuple-element.194.refs_2_, ...), custom_call_target="tpu_custom_call" | custom-call | flops 3623878656 | bytes 14155776 | tf_op jit(solution)/shard_map/enc_back_in/pallas_call | solution.py:364
  265.2 10.2 %collective-permute-done.31.refs_3_.refs_8_ = bf16[384,768]{1,0:T(8,128)(2,1)S(1)} collective-permute-done((bf16[384,768]{1,0:T(8,128)(2,1)S(1)}, bf16[384,768]{1,0:T(8,128)(2,1)S(1)}, u32[]{:S(2)}, u32[]{:S(2)}) %collective-permute-start.31) | collective-permute-done | bytes 589856 | tf_op jit(solution)/shard_map/ppermute | solution.py:325
  286.4 13.6 %self_back.1 = (f32[256,768]{1,0:T(8,128)}, f32[5,768]{1,0:T(8,128)}, bf16[1568,768]{1,0:T(8,128)(2,1)}, bf16[768,768]{1,0:T(8,128)(2,1)}, bf16[800,768]{1,0:T(8,128)(2,1)}) custom-call(s32[8]{0:T(128)} %iota_xor_fusion.refs_0_, f32[256,768]{1,0:T(8,128)} %get-tuple-element.210.refs_1_, f32[5,768]{1,0:T(8,128)} %get-tuple-element.190.refs_4_.refs_2_, ...), custom_call_target="tpu_custom_call" | custom-call | flops 2415919104 | bytes 11796480 | tf_op jit(solution)/shard_map/self_back/pallas_call | solution.py:364
  310.8 13.4 %enc_attn_back.1 = (f32[256,768]{1,0:T(8,128)}, f32[5,768]{1,0:T(8,128)}, bf16[1552,768]{1,0:T(8,128)(2,1)}, bf16[1552,768]{1,0:T(8,128)(2,1)}) custom-call(s32[8]{0:T(128)} %iota_xor_fusion.refs_0_, f32[256,768]{1,0:T(8,128)} %get-tuple-element.203.refs_1_, f32[3,768]{1,0:T(4,128)} %get-tuple-element.200.refs_3_.refs_2_, ...), custom_call_target="tpu_custom_call" | custom-call | flops 2415919104 | bytes 11796480 | tf_op jit(solution)/shard_map/enc_attn_back/pallas_call | solution.py:364
  328.3 4.8 add_6a.1
  336.4 4.9 collective-permute-done.41.refs_3_.refs_4_
  351.8 12.6 %collective-permute-done.43.refs_2_.refs_14_ = bf16[384,768]{1,0:T(8,128)(2,1)S(1)} collective-permute-done((bf16[384,768]{1,0:T(8,128)(2,1)S(1)}, bf16[384,768]{1,0:T(8,128)(2,1)S(1)}, u32[]{:S(2)}, u32[]{:S(2)}) %collective-permute-start.43) | collective-permute-done | bytes 589856 | tf_op jit(solution)/shard_map/ppermute | solution.py:325
  378.7 5.9 %add_8.1 = (bf16[768,768]{1,0:T(8,128)(2,1)}, bf16[384,768]{1,0:T(8,128)(2,1)}, bf16[416,768]{1,0:T(8,128)(2,1)}, bf16[768,768]{1,0:T(8,128)(2,1)}) custom-call(bf16[768,768]{1,0:T(8,128)(2,1)} %get-tuple-element.237.refs_0_, bf16[768,768]{1,0:T(8,128)(2,1)} %copy-done.46, bf16[1568,768]{1,0:T(8,128)(2,1)} %get-tuple-element.233.refs_3_.refs_2_.refs_9_, ...), custom_call_target="tpu_custom_call" | custom-call | tf_op jit(solution)/shard_map/add_8/pallas_call | solution.py:364
  388.4 4.3 collective-permute-start.50
  392.8 7.7 %collective-permute-done.51.refs_11_.refs_14_ = bf16[384,768]{1,0:T(8,128)(2,1)S(1)} collective-permute-done((bf16[384,768]{1,0:T(8,128)(2,1)}, bf16[384,768]{1,0:T(8,128)(2,1)S(1)}, u32[]{:S(2)}, u32[]{:S(2)}) %collective-permute-start.51) | collective-permute-done | bytes 589856 | tf_op jit(solution)/shard_map/ppermute | solution.py:325
  402.1 4.8 add_9.1
  409.0 8.2 %collective-permute-done.50.refs_3_ = bf16[768,768]{1,0:T(8,128)(2,1)S(1)} collective-permute-done((bf16[768,768]{1,0:T(8,128)(2,1)}, bf16[768,768]{1,0:T(8,128)(2,1)S(1)}, u32[]{:S(2)}, u32[]{:S(2)}) %collective-permute-start.50) | collective-permute-done | bytes 1179680 | tf_op jit(solution)/shard_map/ppermute | solution.py:1101
  422.6 4.5 add_10.1
  427.8 5.2 collective-permute-start.58
  435.9 20.6 %collective-permute-done.56.refs_3_ = bf16[384,768]{1,0:T(8,128)(2,1)S(1)} collective-permute-done((bf16[384,768]{1,0:T(8,128)(2,1)S(1)}, bf16[384,768]{1,0:T(8,128)(2,1)S(1)}, u32[]{:S(2)}, u32[]{:S(2)}) %collective-permute-start.56) | collective-permute-done | bytes 589856 | tf_op jit(solution)/shard_map/ppermute | solution.py:1101
  464.6 5.2 collective-permute-start.59
  488.8 13.3 %collective-permute-done.63.refs_2_.refs_4_ = bf16[768,768]{1,0:T(8,128)(2,1)S(1)} collective-permute-done((bf16[768,768]{1,0:T(8,128)(2,1)S(1)}, bf16[768,768]{1,0:T(8,128)(2,1)S(1)}, u32[]{:S(2)}, u32[]{:S(2)}) %collective-permute-start.63) | collective-permute-done | bytes 1179680 | tf_op jit(solution)/shard_map/ppermute | solution.py:1122
  505.8 8.9 %collective-permute-done.62.refs_2_ = bf16[384,768]{1,0:T(8,128)(2,1)S(1)} collective-permute-done((bf16[384,768]{1,0:T(8,128)(2,1)}, bf16[384,768]{1,0:T(8,128)(2,1)S(1)}, u32[]{:S(2)}, u32[]{:S(2)}) %collective-permute-start.62) | collective-permute-done | bytes 589856 | tf_op jit(solution)/shard_map/ppermute | solution.py:1122
  522.3 6.1 %collective-permute-done.66.refs_2_ = bf16[416,768]{1,0:T(8,128)(2,1)S(1)} collective-permute-done((bf16[416,768]{1,0:T(8,128)(2,1)}, bf16[416,768]{1,0:T(8,128)(2,1)S(1)}, u32[]{:S(2)}, u32[]{:S(2)}) %collective-permute-start.66) | collective-permute-done | bytes 639008 | tf_op jit(solution)/shard_map/ppermute | solution.py:1122
  (337 shorter events, 231.7 us)
Async XLA Ops:
  6.7 30.5 %collective-permute-start.1 = (bf16[784,768]{1,0:T(8,128)(2,1)}, bf16[784,768]{1,0:T(8,128)(2,1)S(1)}, u32[]{:S(2)}, u32[]{:S(2)}) collective-permute-start(bf16[784,768]{1,0:T(8,128)(2,1)} %piece_1_pack.1.refs_2_.refs_0_), channel_id=1, source_target_pairs={{0,4},{1,5},{2,6},{3,7},{4,0},{5,1},{6,2},{7,3},{8,12},{9,13},{10,... | collective-permute-start | bytes 3612680 | tf_op jit(solution)/shard_map/ppermute | solution.py:325
  9.6 29.6 %collective-permute-start = (bf16[784,768]{1,0:T(8,128)(2,1)}, bf16[784,768]{1,0:T(8,128)(2,1)S(1)}, u32[]{:S(2)}, u32[]{:S(2)}) collective-permute-start(bf16[784,768]{1,0:T(8,128)(2,1)} %piece_1_pack.1.refs_2_.refs_0_), channel_id=1, source_target_pairs={{0,2},{1,3},{2,0},{3,1},{4,6},{5,7},{6,4},{7,5},{8,10},{9,11},{10,... | collective-permute-start | bytes 3612680 | tf_op jit(solution)/shard_map/ppermute | solution.py:325
  13.5 49.0 %collective-permute-start.5 = (bf16[768,768]{1,0:T(8,128)(2,1)}, bf16[768,768]{1,0:T(8,128)(2,1)S(1)}, u32[]{:S(2)}, u32[]{:S(2)}) collective-permute-start(bf16[768,768]{1,0:T(8,128)(2,1)} %piece_2_pack.1.refs_2_.refs_0_), channel_id=1, source_target_pairs={{0,4},{1,5},{2,6},{3,7},{4,0},{5,1},{6,2},{7,3},{8,12},{9,13},{10,... | collective-permute-start | bytes 3538952 | tf_op jit(solution)/shard_map/ppermute | solution.py:325
  14.0 50.6 %collective-permute-start.4 = (bf16[768,768]{1,0:T(8,128)(2,1)}, bf16[768,768]{1,0:T(8,128)(2,1)S(1)}, u32[]{:S(2)}, u32[]{:S(2)}) collective-permute-start(bf16[768,768]{1,0:T(8,128)(2,1)} %piece_2_pack.1.refs_2_.refs_0_), channel_id=1, source_target_pairs={{0,2},{1,3},{2,0},{3,1},{4,6},{5,7},{6,4},{7,5},{8,10},{9,11},{10,... | collective-permute-start | bytes 3538952 | tf_op jit(solution)/shard_map/ppermute | solution.py:325
  43.1 45.8 %collective-permute-start.3 = (bf16[400,768]{1,0:T(8,128)(2,1)}, bf16[400,768]{1,0:T(8,128)(2,1)S(1)}, u32[]{:S(2)}, u32[]{:S(2)}) collective-permute-start(bf16[400,768]{1,0:T(8,128)(2,1)} %get-tuple-element.142), channel_id=1, source_target_pairs={{0,2},{1,3},{2,0},{3,1},{4,6},{5,7},{6,4},{7,5},{8,10},{9,11},{10,... | collective-permute-start | bytes 1843208 | tf_op jit(solution)/shard_map/ppermute | solution.py:325
  44.6 30.5 %collective-permute-start.2 = (bf16[384,768]{1,0:T(8,128)(2,1)}, bf16[384,768]{1,0:T(8,128)(2,1)S(1)}, u32[]{:S(2)}, u32[]{:S(2)}) collective-permute-start(bf16[384,768]{1,0:T(8,128)(2,1)} %get-tuple-element.141.refs_2_), channel_id=1, source_target_pairs={{0,4},{1,5},{2,6},{3,7},{4,0},{5,1},{6,2},{7,3},{8,12},{9,13},{10,... | collective-permute-start | bytes 1769480 | tf_op jit(solution)/shard_map/ppermute | solution.py:325
  68.3 20.6 %collective-permute-start.7 = (bf16[384,768]{1,0:T(8,128)(2,1)}, bf16[384,768]{1,0:T(8,128)(2,1)S(1)}, u32[]{:S(2)}, u32[]{:S(2)}) collective-permute-start(bf16[384,768]{1,0:T(8,128)(2,1)} %get-tuple-element.144), channel_id=1, source_target_pairs={{0,2},{1,3},{2,0},{3,1},{4,6},{5,7},{6,4},{7,5},{8,10},{9,11},{10,... | collective-permute-start | bytes 1769480 | tf_op jit(solution)/shard_map/ppermute | solution.py:325
  102.5 29.8 %collective-permute-start.11 = (bf16[768,768]{1,0:T(8,128)(2,1)}, bf16[768,768]{1,0:T(8,128)(2,1)S(1)}, u32[]{:S(2)}, u32[]{:S(2)}) collective-permute-start(bf16[768,768]{1,0:T(8,128)(2,1)} %piece_3_pack.1.refs_3_.refs_0_), channel_id=1, source_target_pairs={{0,4},{1,5},{2,6},{3,7},{4,0},{5,1},{6,2},{7,3},{8,12},{9,13},{10,... | collective-permute-start | bytes 3538952 | tf_op jit(solution)/shard_map/ppermute | solution.py:325
  102.8 29.5 %collective-permute-start.10 = (bf16[768,768]{1,0:T(8,128)(2,1)}, bf16[768,768]{1,0:T(8,128)(2,1)S(1)}, u32[]{:S(2)}, u32[]{:S(2)}) collective-permute-start(bf16[768,768]{1,0:T(8,128)(2,1)} %piece_3_pack.1.refs_3_.refs_0_), channel_id=1, source_target_pairs={{0,2},{1,3},{2,0},{3,1},{4,6},{5,7},{6,4},{7,5},{8,10},{9,11},{10,... | collective-permute-start | bytes 3538952 | tf_op jit(solution)/shard_map/ppermute | solution.py:325
  120.9 28.1 %collective-permute-start.15 = (bf16[384,768]{1,0:T(8,128)(2,1)}, bf16[384,768]{1,0:T(8,128)(2,1)S(1)}, u32[]{:S(2)}, u32[]{:S(2)}) collective-permute-start(bf16[384,768]{1,0:T(8,128)(2,1)} %piece_4_pack.1.refs_7_.refs_0_), channel_id=1, source_target_pairs={{0,4},{1,5},{2,6},{3,7},{4,0},{5,1},{6,2},{7,3},{8,12},{9,13},{10,... | collective-permute-start | bytes 1769480 | tf_op jit(solution)/shard_map/ppermute | solution.py:325
  122.4 26.6 %collective-permute-start.14 = (bf16[384,768]{1,0:T(8,128)(2,1)}, bf16[384,768]{1,0:T(8,128)(2,1)S(1)}, u32[]{:S(2)}, u32[]{:S(2)}) collective-permute-start(bf16[384,768]{1,0:T(8,128)(2,1)} %piece_4_pack.1.refs_7_.refs_0_), channel_id=1, source_target_pairs={{0,2},{1,3},{2,0},{3,1},{4,6},{5,7},{6,4},{7,5},{8,10},{9,11},{10,... | collective-permute-start | bytes 1769480 | tf_op jit(solution)/shard_map/ppermute | solution.py:325
  136.4 20.7 %collective-permute-start.13 = (bf16[384,768]{1,0:T(8,128)(2,1)}, bf16[384,768]{1,0:T(8,128)(2,1)S(1)}, u32[]{:S(2)}, u32[]{:S(2)}) collective-permute-start(bf16[384,768]{1,0:T(8,128)(2,1)} %get-tuple-element.151), channel_id=1, source_target_pairs={{0,2},{1,3},{2,0},{3,1},{4,6},{5,7},{6,4},{7,5},{8,10},{9,11},{10,... | collective-permute-start | bytes 1769480 | tf_op jit(solution)/shard_map/ppermute | solution.py:325
  214.2 29.1 %collective-permute-start.27 = (bf16[768,768]{1,0:T(8,128)(2,1)}, bf16[768,768]{1,0:T(8,128)(2,1)S(1)}, u32[]{:S(2)}, u32[]{:S(2)}) collective-permute-start(bf16[768,768]{1,0:T(8,128)(2,1)} %add_1.1.refs_13_), channel_id=1, source_target_pairs={{0,2},{1,3},{2,0},{3,1},{4,6},{5,7},{6,4},{7,5},{8,10},{9,11},{10,... | collective-permute-start | bytes 3538952 | tf_op jit(solution)/shard_map/ppermute | solution.py:325
  234.6 40.9 %collective-permute-start.30 = (bf16[768,768]{1,0:T(8,128)(2,1)}, bf16[768,768]{1,0:T(8,128)(2,1)S(1)}, u32[]{:S(2)}, u32[]{:S(2)}) collective-permute-start(bf16[768,768]{1,0:T(8,128)(2,1)} %add_2.1.refs_6_), channel_id=1, source_target_pairs={{0,4},{1,5},{2,6},{3,7},{4,0},{5,1},{6,2},{7,3},{8,12},{9,13},{10,... | collective-permute-start | bytes 3538952 | tf_op jit(solution)/shard_map/ppermute | solution.py:325
  250.7 28.3 %collective-permute-start.29 = (bf16[768,768]{1,0:T(8,128)(2,1)}, bf16[768,768]{1,0:T(8,128)(2,1)S(1)}, u32[]{:S(2)}, u32[]{:S(2)}) collective-permute-start(bf16[768,768]{1,0:T(8,128)(2,1)} %get-tuple-element.220), channel_id=1, source_target_pairs={{0,1},{1,0},{2,3},{3,2},{4,5},{5,4},{6,7},{7,6},{8,9},{9,8},{10,11... | collective-permute-start | bytes 3538952 | tf_op jit(solution)/shard_map/ppermute | solution.py:325
  250.8 28.3 %collective-permute-start.28 = (bf16[768,768]{1,0:T(8,128)(2,1)}, bf16[768,768]{1,0:T(8,128)(2,1)S(1)}, u32[]{:S(2)}, u32[]{:S(2)}) collective-permute-start(bf16[768,768]{1,0:T(8,128)(2,1)} %get-tuple-element.219), channel_id=1, source_target_pairs={{0,1},{1,0},{2,3},{3,2},{4,5},{5,4},{6,7},{7,6},{8,9},{9,8},{10,11... | collective-permute-start | bytes 3538952 | tf_op jit(solution)/shard_map/ppermute | solution.py:325
  251.3 24.2 %collective-permute-start.31 = (bf16[384,768]{1,0:T(8,128)(2,1)S(1)}, bf16[384,768]{1,0:T(8,128)(2,1)S(1)}, u32[]{:S(2)}, u32[]{:S(2)}) collective-permute-start(bf16[384,768]{1,0:T(8,128)(2,1)S(1)} %copy-done.41), channel_id=1, source_target_pairs={{0,4},{1,5},{2,6},{3,7},{4,0},{5,1},{6,2},{7,3},{8,12},{9,13},{10,... | collective-permute-start | bytes 1769480 | tf_op jit(solution)/shard_map/ppermute | solution.py:325
  252.5 47.5 %collective-permute-start.35 = (bf16[768,768]{1,0:T(8,128)(2,1)}, bf16[768,768]{1,0:T(8,128)(2,1)S(1)}, u32[]{:S(2)}, u32[]{:S(2)}) collective-permute-start(bf16[768,768]{1,0:T(8,128)(2,1)} %add_3b.1.refs_8_), channel_id=1, source_target_pairs={{0,2},{1,3},{2,0},{3,1},{4,6},{5,7},{6,4},{7,5},{8,10},{9,11},{10,... | collective-permute-start | bytes 3538952 | tf_op jit(solution)/shard_map/ppermute | solution.py:325
  284.7 41.6 %collective-permute-start.36 = (bf16[800,768]{1,0:T(8,128)(2,1)}, bf16[800,768]{1,0:T(8,128)(2,1)S(1)}, u32[]{:S(2)}, u32[]{:S(2)}) collective-permute-start(bf16[800,768]{1,0:T(8,128)(2,1)} %add_4b.1.refs_15_), channel_id=1, source_target_pairs={{0,4},{1,5},{2,6},{3,7},{4,0},{5,1},{6,2},{7,3},{8,12},{9,13},{10,... | collective-permute-start | bytes 3686408 | tf_op jit(solution)/shard_map/ppermute | solution.py:325
  308.2 28.2 %collective-permute-start.44 = (bf16[768,768]{1,0:T(8,128)(2,1)}, bf16[768,768]{1,0:T(8,128)(2,1)S(1)}, u32[]{:S(2)}, u32[]{:S(2)}) collective-permute-start(bf16[768,768]{1,0:T(8,128)(2,1)} %add_5b.1.refs_14_), channel_id=1, source_target_pairs={{0,2},{1,3},{2,0},{3,1},{4,6},{5,7},{6,4},{7,5},{8,10},{9,11},{10,... | collective-permute-start | bytes 3538952 | tf_op jit(solution)/shard_map/ppermute | solution.py:325
  344.4 29.6 %collective-permute-start.40 = (bf16[768,768]{1,0:T(8,128)(2,1)S(1)}, bf16[768,768]{1,0:T(8,128)(2,1)S(1)}, u32[]{:S(2)}, u32[]{:S(2)}) collective-permute-start(bf16[768,768]{1,0:T(8,128)(2,1)S(1)} %copy-done.45), channel_id=1, source_target_pairs={{0,8},{24,16},{1,9},{25,17},{2,10},{26,18},{3,11},{27,19},{4,12},{... | collective-permute-start | bytes 3538952 | tf_op jit(solution)/shard_map/ppermute | solution.py:1101
  349.8 22.1 %collective-permute-start.48 = (bf16[384,768]{1,0:T(8,128)(2,1)}, bf16[384,768]{1,0:T(8,128)(2,1)S(1)}, u32[]{:S(2)}, u32[]{:S(2)}) collective-permute-start(bf16[384,768]{1,0:T(8,128)(2,1)} %add_6b.1.refs_4_), channel_id=1, source_target_pairs={{0,4},{1,5},{2,6},{3,7},{4,0},{5,1},{6,2},{7,3},{8,12},{9,13},{10,... | collective-permute-start | bytes 1769480 | tf_op jit(solution)/shard_map/ppermute | solution.py:325
  387.7 21.3 %collective-permute-start.49 = (bf16[768,768]{1,0:T(8,128)(2,1)}, bf16[768,768]{1,0:T(8,128)(2,1)S(1)}, u32[]{:S(2)}, u32[]{:S(2)}) collective-permute-start(bf16[768,768]{1,0:T(8,128)(2,1)} %get-tuple-element.247.refs_0_), channel_id=1, source_target_pairs={{8,16},{16,8},{9,17},{17,9},{10,18},{18,10},{11,19},{19,11},{12,20... | collective-permute-start | bytes 3538952 | tf_op jit(solution)/shard_map/ppermute | solution.py:1115
  388.4 28.8 %collective-permute-start.50 = (bf16[768,768]{1,0:T(8,128)(2,1)}, bf16[768,768]{1,0:T(8,128)(2,1)S(1)}, u32[]{:S(2)}, u32[]{:S(2)}) collective-permute-start(bf16[768,768]{1,0:T(8,128)(2,1)} %get-tuple-element.248.refs_2_), channel_id=1, source_target_pairs={{0,8},{24,16},{1,9},{25,17},{2,10},{26,18},{3,11},{27,19},{4,12},{... | collective-permute-start | bytes 3538952 | tf_op jit(solution)/shard_map/ppermute | solution.py:1101
  427.0 29.4 %collective-permute-start.55 = (bf16[768,768]{1,0:T(8,128)(2,1)}, bf16[768,768]{1,0:T(8,128)(2,1)S(1)}, u32[]{:S(2)}, u32[]{:S(2)}) collective-permute-start(bf16[768,768]{1,0:T(8,128)(2,1)} %get-tuple-element.253.refs_0_), channel_id=1, source_target_pairs={{8,16},{16,8},{9,17},{17,9},{10,18},{18,10},{11,19},{19,11},{12,20... | collective-permute-start | bytes 3538952 | tf_op jit(solution)/shard_map/ppermute | solution.py:1115
  427.8 33.6 %collective-permute-start.58 = (bf16[416,768]{1,0:T(8,128)(2,1)S(1)}, bf16[416,768]{1,0:T(8,128)(2,1)S(1)}, u32[]{:S(2)}, u32[]{:S(2)}) collective-permute-start(bf16[416,768]{1,0:T(8,128)(2,1)S(1)} %copy-done.53), channel_id=1, source_target_pairs={{0,8},{24,16},{1,9},{25,17},{2,10},{26,18},{3,11},{27,19},{4,12},{... | collective-permute-start | bytes 1916936 | tf_op jit(solution)/shard_map/ppermute | solution.py:1101
  433.0 23.4 %collective-permute-start.56 = (bf16[384,768]{1,0:T(8,128)(2,1)S(1)}, bf16[384,768]{1,0:T(8,128)(2,1)S(1)}, u32[]{:S(2)}, u32[]{:S(2)}) collective-permute-start(bf16[384,768]{1,0:T(8,128)(2,1)S(1)} %copy-done.63), channel_id=1, source_target_pairs={{0,8},{24,16},{1,9},{25,17},{2,10},{26,18},{3,11},{27,19},{4,12},{... | collective-permute-start | bytes 1769480 | tf_op jit(solution)/shard_map/ppermute | solution.py:1101
  434.6 39.5 %collective-permute-start.60 = (bf16[768,768]{1,0:T(8,128)(2,1)}, bf16[768,768]{1,0:T(8,128)(2,1)S(1)}, u32[]{:S(2)}, u32[]{:S(2)}) collective-permute-start(bf16[768,768]{1,0:T(8,128)(2,1)} %get-tuple-element.261.refs_1_), channel_id=1, source_target_pairs={{8,0},{16,24},{9,1},{17,25},{10,2},{18,26},{11,3},{19,27},{12,4},{... | collective-permute-start | bytes 3538952 | tf_op jit(solution)/shard_map/ppermute | solution.py:1122
  471.3 30.8 %collective-permute-start.63 = (bf16[768,768]{1,0:T(8,128)(2,1)S(1)}, bf16[768,768]{1,0:T(8,128)(2,1)S(1)}, u32[]{:S(2)}, u32[]{:S(2)}) collective-permute-start(bf16[768,768]{1,0:T(8,128)(2,1)S(1)} %copy-done.20), channel_id=1, source_target_pairs={{8,0},{16,24},{9,1},{17,25},{10,2},{18,26},{11,3},{19,27},{12,4},{... | collective-permute-start | bytes 3538952 | tf_op jit(solution)/shard_map/ppermute | solution.py:1122
  483.2 34.7 %collective-permute-start.61 = (bf16[400,768]{1,0:T(8,128)(2,1)}, bf16[400,768]{1,0:T(8,128)(2,1)S(1)}, u32[]{:S(2)}, u32[]{:S(2)}) collective-permute-start(bf16[400,768]{1,0:T(8,128)(2,1)} %get-tuple-element.263.refs_0_), channel_id=1, source_target_pairs={{8,16},{16,8},{9,17},{17,9},{10,18},{18,10},{11,19},{19,11},{12,20... | collective-permute-start | bytes 1843208 | tf_op jit(solution)/shard_map/ppermute | solution.py:1115
  483.9 30.8 %collective-permute-start.62 = (bf16[384,768]{1,0:T(8,128)(2,1)}, bf16[384,768]{1,0:T(8,128)(2,1)S(1)}, u32[]{:S(2)}, u32[]{:S(2)}) collective-permute-start(bf16[384,768]{1,0:T(8,128)(2,1)} %get-tuple-element.264.refs_2_.refs_1_), channel_id=1, source_target_pairs={{8,0},{16,24},{9,1},{17,25},{10,2},{18,26},{11,3},{19,27},{12,4},{... | collective-permute-start | bytes 1769480 | tf_op jit(solution)/shard_map/ppermute | solution.py:1122
  487.5 40.9 %collective-permute-start.66 = (bf16[416,768]{1,0:T(8,128)(2,1)}, bf16[416,768]{1,0:T(8,128)(2,1)S(1)}, u32[]{:S(2)}, u32[]{:S(2)}) collective-permute-start(bf16[416,768]{1,0:T(8,128)(2,1)} %add_14.1.refs_3_.refs_1_), channel_id=1, source_target_pairs={{8,0},{16,24},{9,1},{17,25},{10,2},{18,26},{11,3},{19,27},{12,4},{... | collective-permute-start | bytes 1916936 | tf_op jit(solution)/shard_map/ppermute | solution.py:1122
  (112 other events, 755.5 us)

commit v4 on v3

--- a/solution.py
+++ b/solution.py
@@ -11,6 +11,9 @@
 PAIR = 2 * HEAD
 ROW_TILE = 16
 VMEM_BYTES = 56 * 1024 * 1024
+SMALL_VMEM_BYTES = 20 * 1024 * 1024
+MIDDLE_VMEM_BYTES = 44 * 1024 * 1024
+MIDDLE = ('enc_attn', 'dec_self', 'cross_back', 'enc_back_out', 'self_back')
 ANY = pl.BlockSpec(memory_space=pl.ANY)
 SMEM = pl.BlockSpec(memory_space=pltpu.SMEM)
 VMEM = pl.BlockSpec(memory_space=pltpu.VMEM)
@@ -361,13 +364,16 @@
         extra = self.waits + ([] if self.token is None else [self.token])
         self.waits = []
         count, skip = len(operands), len(extra)
+        grant = SMALL_VMEM_BYTES if not flops else MIDDLE_VMEM_BYTES if name in MIDDLE else VMEM_BYTES
         results = pl.pallas_call(
             lambda *refs: body(*refs[:count], *refs[count + skip :]),
             out_shape=[jax.ShapeDtypeStruct(shape, dtype) for shape, dtype, spec in outs],
             in_specs=list(specs) + [ANY] * skip,
             out_specs=[spec for shape, dtype, spec in outs],
             scratch_shapes=scratch,
-            compiler_params=pltpu.CompilerParams(vmem_limit_bytes=VMEM_BYTES),
+            compiler_params=pltpu.CompilerParams(
+                vmem_limit_bytes=grant
+            ),
             cost_estimate=pl.CostEstimate(flops=flops, bytes_accessed=moved, transcendentals=0),
             name=name,
         )(*operands, *extra)
@@ -473,8 +479,26 @@
     wait_all(stores)
 
 
-def vec_body(table, mine, theirs, out, sems):
-    rows = out.shape[0] // 8
+LANES = 128
+
+
+def chunk_count(length):
+    return max(-(-((place * length) % LANES + length) // LANES) for place in range(8))
+
+
+def vec_shards(vectors, chip_index, feature):
+    parts = []
+    for vector in vectors:
+        length = vector.shape[0]
+        blank = jnp.zeros((chunk_count(length) * LANES,), vector.dtype)
+        parts.append(lax.dynamic_update_slice(blank, vector, ((chip_index * length) % LANES,)))
+    return vec_rows(jnp.concatenate(parts), feature)
+
+
+def vec_body(lengths, sections, table, mine, theirs, *refs):
+    outs, landed, wide, sems = refs[:-3], refs[-3], refs[-2], refs[-1]
+    rows = landed.shape[0] // 8
+    feature = landed.shape[1]
     block = mine.shape[0] // 4
     copies = []
     for chip in range(4):
@@ -482,25 +506,57 @@
             copies.append(
                 pltpu.make_async_copy(
                     source.at[pl.ds((chip + 1) * block - rows, rows), :],
-                    out.at[pl.ds(pl.multiple_of(table[2 * chip + core] * rows, ROW_TILE), rows), :],
+                    landed.at[pl.ds(pl.multiple_of(table[2 * chip + core] * rows, ROW_TILE), rows), :],
                     sems.at[len(copies)],
                 )
             )
     for copy in copies:
         copy.start()
     wait_all(copies)
-
-
-def gathered_vec(order, buffers, table, rows, feature):
-    (out,) = order.kernel(
-        vec_body,
+    wide[...] = landed[...].astype(jnp.float32)
+    per_row = feature // LANES
+    outs = list(outs)
+    skip = 0
+    for length, section in zip(lengths, sections):
+        targets = []
+        for count in section:
+            out = outs.pop(0)
+            targets += [(out, row, lane * LANES) for row in range(count) for lane in range(per_row)]
+        out = outs.pop(0)
+        targets += [(out, 0, lane * LANES) for lane in range(out.shape[1] // LANES)]
+        filled = set()
+        for place in range(8):
+            base = place * length // LANES
+            used = -(-((place * length) % LANES + length) // LANES)
+            for chunk in range(used):
+                flat = (skip + chunk) * LANES
+                row, lane = place * rows + flat // feature, flat % feature
+                value = wide[row : row + 1, lane : lane + LANES]
+                out, row, lane = targets[base + chunk]
+                if base + chunk in filled:
+                    value = value + out[row : row + 1, lane : lane + LANES]
+                out[row : row + 1, lane : lane + LANES] = value
+                filled.add(base + chunk)
+        skip += chunk_count(length)
+
+
+def gathered_vecs(order, buffers, table, rows, feature, lengths, sections):
+    outs = []
+    for length, section in zip(lengths, sections):
+        outs += [((count, feature), jnp.float32, VMEM) for count in section]
+        outs.append(((1, 8 * length - sum(section) * feature), jnp.float32, VMEM))
+    return order.kernel(
+        functools.partial(vec_body, lengths, sections),
         [table, *buffers],
         [SMEM] + [ANY] * 2,
-        [((8 * rows, feature), jnp.bfloat16, VMEM)],
-        [pltpu.SemaphoreType.DMA((8,))],
+        outs,
+        [
+            pltpu.VMEM((8 * rows, feature), jnp.bfloat16),
+            pltpu.VMEM((8 * rows, feature), jnp.float32),
+            pltpu.SemaphoreType.DMA((8,)),
+        ],
         "vectors",
     )
-    return out.reshape(8, rows * feature)
 
 
 class Loader:
@@ -757,7 +813,7 @@
     hidden, gain, active, g_out, sums, keep, upper, lower, stage, out_sems = refs
     feature = hidden.shape[1]
     store = Storer((keep, upper, lower), table, slots, out_sems)
-    gradient, grad_gain, grad_shift = layer_norm_back(hidden[...], gain[...], gradient)
+    gradient, grad_gain, grad_shift = layer_norm_back(hidden[...], gain[1:2, :], gradient)
     sums[0:1, :] = jnp.sum(gradient, axis=0, keepdims=True)
     sums[1:2, :] = grad_gain
     sums[2:3, :] = grad_shift
@@ -854,7 +910,7 @@
     waits = [load.wide(first_unit + i, w) for i, w in enumerate((w_q, w_k, w_v))]
     store = Storer(grads, table, slots, out_sems)
     lanes = head_lanes(rows)
-    total, grad_gain, grad_shift = layer_norm_back(hidden[...], gain[...], gradient[...])
+    total, grad_gain, grad_shift = layer_norm_back(hidden[...], gain[3:4, :], gradient[...])
     sums[2:3, :] = jnp.sum(total, axis=0, keepdims=True)
     sums[3:4, :] = grad_gain
     sums[4:5, :] = grad_shift
@@ -1195,7 +1251,7 @@
     g_1, g_2, g_3, g_4 = (Gather(order, feature, "piece_" + name) for name in "1234")
     half = 4 * unit
     e_len, d_len = enc_vec.shape[0], dec_vec.shape[0]
-    vec_part = vec_rows(jnp.concatenate([enc_vec, dec_vec]), feature)
+    vec_part = vec_shards([enc_vec, dec_vec], chip_index, feature)
     g_1.sides(enc_attn, dec_attn[:, : 4 * feature], vec_part)
     g_2.sides(enc_w1, enc_w2)
     g_1.corners()
@@ -1204,33 +1260,32 @@
     (attn_pair,) = g_1.join((0, 2 * half + vec_part.shape[0]))
     (e_feed,) = g_2.join((0, 2 * half))
     g_3.sides(dec_attn[:, 4 * feature :], dec_w1)
-    vecs = gathered_vec(order, attn_pair, table, vec_part.shape[0], feature)
-    e_rows, e_tail = unpack(vecs[:, :e_len].reshape(-1), 8, feature)
-    d_rows, d_tail = unpack(vecs[:, e_len : e_len + d_len].reshape(-1), 13, feature)
-    e_tail, d_tail = e_tail.reshape(1, -1), d_tail.reshape(1, -1)
+    e_attn_vec, e_feed_vec, e_tail, d_self_vec, d_cross_vec, d_feed_vec, d_tail = gathered_vecs(
+        order, attn_pair, table, vec_part.shape[0], feature, (e_len, d_len), ((5, 3), (5, 5, 3))
+    )
     e_hid_a, e_first, *e_saved = attn_forward(
-        order, enc_in, None, e_rows[0:5], (attn_pair, 0), ids, enc_lengths, False, "enc_attn"
-    )
-    mark(e_feed[1], d_rows, d_tail, e_tail)
+        order, enc_in, None, e_attn_vec, (attn_pair, 0), ids, enc_lengths, False, "enc_attn"
+    )
+    mark(e_feed[1])
     g_4.sides(dec_w2)
     d_hid_s, d_first, *s_saved = attn_forward(
-        order, dec_in, None, d_rows[0:5], (attn_pair, 4), ids, dec_lengths, True, "dec_self"
+        order, dec_in, None, d_self_vec, (attn_pair, 4), ids, dec_lengths, True, "dec_self"
     )
     g_3.corners()
     e_hid_f, encoded, e_act, e_slope = feed_forward(
-        order, e_first, e_rows[5:8], e_tail, (e_feed, 0), (e_feed, 4), table, "enc_feed"
+        order, e_first, e_feed_vec, e_tail, (e_feed, 0), (e_feed, 4), table, "enc_feed"
     )
     g_4.corners()
     cross_pair, w1_pair = g_3.join((0, half), (half, half))
     (w2_pair,) = g_4.join((0, half))
     d_hid_c, d_second, *c_saved = attn_forward(
-        order, d_first, encoded, d_rows[5:10], (cross_pair, 0), ids, enc_lengths, False, "dec_cross"
+        order, d_first, encoded, d_cross_vec, (cross_pair, 0), ids, enc_lengths, False, "dec_cross"
     )
     d_hid_f, decoded, d_act, d_slope = feed_forward(
-        order, d_second, d_rows[10:13], d_tail, (w1_pair, 0), (w2_pair, 0), table, "dec_feed"
+        order, d_second, d_feed_vec, d_tail, (w1_pair, 0), (w2_pair, 0), table, "dec_feed"
     )
     gradient, d_sums_f, *outs = feed_back_out(
-        order, [dec_cot], d_hid_f, d_rows[11:12], d_act, table, X_FIRST, "dec_back_out"
+        order, [dec_cot], d_hid_f, d_feed_vec, d_act, table, X_FIRST, "dec_back_out"
     )
     red_0 = Reduce(order, outs, X_FIRST)
     red_0.cores()
@@ -1242,7 +1297,7 @@
     combine(order, "add_1", red_0.first())
     red_1.cores()
     gradient, grad_encoded, d_sums_c, *outs = attn_back(
-        order, gradient, d_hid_c, d_rows[8:9], d_first, encoded, c_saved, (cross_pair, 0), table, [],
+        order, gradient, d_hid_c, d_cross_vec, d_first, encoded, c_saved, (cross_pair, 0), table, [],
         X_FIRST, "cross_back",
     )
     red_2 = Reduce(order, outs, X_FIRST)
@@ -1250,7 +1305,7 @@
     combine(order, "add_2", red_1.first())
     red_2.cores()
     e_gradient, e_sums_f, *outs = feed_back_out(
-        order, [enc_cot, grad_encoded], e_hid_f, e_rows[6:7], e_act, table, Y_FIRST, "enc_back_out"
+        order, [enc_cot, grad_encoded], e_hid_f, e_feed_vec, e_act, table, Y_FIRST, "enc_back_out"
     )
     red_3 = Reduce(order, outs, Y_FIRST, pad=2 * ROW_TILE)
     combine(order, "add_3a", red_0.second())
@@ -1272,7 +1327,7 @@
     combine(order, "add_4b", red_3.first())
     red_4.cores()
     dec_in_grad, d_sums_s, *outs = attn_back(
-        order, gradient, d_hid_s, d_rows[3:4], dec_in, None, s_saved, (attn_pair, 4), table,
+        order, gradient, d_hid_s, d_self_vec, dec_in, None, s_saved, (attn_pair, 4), table,
         [d_sums_c, d_sums_f, d_bias], Y_FIRST, "self_back",
     )
     red_5 = Reduce(order, outs, Y_FIRST, True)
@@ -1282,7 +1337,7 @@
     combine(order, "add_5b", red_4.first())
     red_5.cores()
     enc_in_grad, e_sums_a, *outs = attn_back(
-        order, e_gradient, e_hid_a, e_rows[3:4], enc_in, None, e_saved, (attn_pair, 0), table,
+        order, e_gradient, e_hid_a, e_attn_vec, enc_in, None, e_saved, (attn_pair, 0), table,
         [e_sums_f, e_bias], Y_FIRST, "enc_attn_back", True,
     )
     red_6 = Reduce(order, outs, Y_FIRST, True)

time: 552 us -> 519 us (0.940)
  Pallas kernels: 231 us -> 183 us
  waiting for transfers between devices: 174 us -> 207 us
  local copies, waits for them, and re-layouts: 51.9 us -> 39.4 us
    pallas_call x50, Pallas kernels: 231 us -> 183 us  [kernel(): pl.pallas_call(lambda *refs: body(*refs[:count], *refs[count + skip:]), o...]
    ppermute x52, waiting for transfers between devices: 113 us -> 138 us  [swap(): return lax.ppermute(value, 'fsdp', [(i, i ^ bit) for i in range(8)])]
    ppermute x5, waiting for transfers between devices: 30.2 us -> 36.4 us  [outward_sent(): self.landed = lax.ppermute(value, 'rep', [(1, 0), (2, 3)])]
    unnamed x154 -> x216, local copies, waits for them, and re-layouts: 39.8 us -> 35.7 us
  transfers between devices with their start and end apart: 67 -> 67, of which waited for: 24 -> 27; matrix products, arithmetic and copies ran while one was open for 2% -> 0% of each run, Pallas kernels for 35% -> 30%
where the time goes in v4:
time: 519 us; the launch traced here: 512 us
  waiting for transfers between devices  207 us (40%)
  Pallas kernels  183 us (35%)
  starting transfers between devices  78.5 us (15%)
  local copies, waits for them, and re-layouts  39.4 us (8%)
    pallas_call x50, Pallas kernels, kernel(): pl.pallas_call(lambda *refs: body(*refs[:count], *refs[count + skip:]), o...  183 us
    ppermute x52, waiting for transfers between devices, swap(): return lax.ppermute(value, 'fsdp', [(i, i ^ bit) for i in range(8)])  138 us
    ppermute x52, starting transfers between devices, swap(): return lax.ppermute(value, 'fsdp', [(i, i ^ bit) for i in range(8)])  47.4 us
    ppermute x5, waiting for transfers between devices, outward_sent(): self.landed = lax.ppermute(value, 'rep', [(1, 0), (2, 3)])  36.4 us
    unnamed x216, local copies, waits for them, and re-layouts  35.7 us
    ppermute x5, waiting for transfers between devices, __init__(): self.landed = lax.ppermute(value, 'rep', [(0, 1), (3, 2)])  32.7 us
    ppermute x5, starting transfers between devices, __init__(): self.landed = lax.ppermute(value, 'rep', [(0, 1), (3, 2)])  19.5 us
  transfers between devices with their start and end apart: 67, of which 27 were waited for; matrix products, arithmetic and copies ran while one was open for 0% of the time, Pallas kernels for 30%

profile of v4, /device:TPU:0, one launch (start us, length us, event | category | flops | bytes accessed | tf_op | source)
XLA Modules:
  0.0 512.3 jit_solution(8691977871295864550)
XLA Ops:
  9.6 24.6 %collective-permute-done.1.refs_1_.refs_2_ = bf16[784,768]{1,0:T(8,128)(2,1)S(1)} collective-permute-done((bf16[784,768]{1,0:T(8,128)(2,1)S(1)}, bf16[784,768]{1,0:T(8,128)(2,1)S(1)}, u32[]{:S(2)}, u32[]{:S(2)}) %collective-permute-start.1) | collective-permute-done | bytes 1204256 | tf_op jit(solution)/shard_map/ppermute | solution.py:328
  38.4 21.0 %collective-permute-done.5.refs_1_.refs_2_ = bf16[768,768]{1,0:T(8,128)(2,1)S(1)} collective-permute-done((bf16[768,768]{1,0:T(8,128)(2,1)S(1)}, bf16[768,768]{1,0:T(8,128)(2,1)S(1)}, u32[]{:S(2)}, u32[]{:S(2)}) %collective-permute-start.5) | collective-permute-done | bytes 1179680 | tf_op jit(solution)/shard_map/ppermute | solution.py:328
  63.7 8.4 %collective-permute-done.2.refs_3_ = bf16[384,768]{1,0:T(8,128)(2,1)S(1)} collective-permute-done((bf16[384,768]{1,0:T(8,128)(2,1)S(1)}, bf16[384,768]{1,0:T(8,128)(2,1)S(1)}, u32[]{:S(2)}, u32[]{:S(2)}) %collective-permute-start.2) | collective-permute-done | bytes 589856 | tf_op jit(solution)/shard_map/ppermute | solution.py:328
  72.1 13.8 %collective-permute-done.7.refs_6_.refs_4_ = bf16[384,768]{1,0:T(8,128)(2,1)S(1)} collective-permute-done((bf16[384,768]{1,0:T(8,128)(2,1)S(1)}, bf16[384,768]{1,0:T(8,128)(2,1)S(1)}, u32[]{:S(2)}, u32[]{:S(2)}) %collective-permute-start.7) | collective-permute-done | bytes 589856 | tf_op jit(solution)/shard_map/ppermute | solution.py:328
  99.7 8.6 %enc_attn.1 = (f32[256,768]{1,0:T(8,128)S(1)}, bf16[256,768]{1,0:T(8,128)(2,1)S(1)}, bf16[256,768]{1,0:T(8,128)(2,1)S(1)}, bf16[256,768]{1,0:T(8,128)(2,1)S(1)},...) custom-call(s32[8]{0:T(128)S(1)} %iota_xor_fusion.refs_0_, ...), custom_call_target="tpu_custom_call" | custom-call | flops 1207959552 | bytes 5898240 | tf_op jit(solution)/shard_map/enc_attn/pallas_call | solution.py:368
  113.6 9.0 %dec_self.1 = (f32[256,768]{1,0:T(8,128)S(1)}, bf16[256,768]{1,0:T(8,128)(2,1)S(1)}, bf16[256,768]{1,0:T(8,128)(2,1)S(1)}, bf16[256,768]{1,0:T(8,128)(2,1)S(1)},...) custom-call(s32[8]{0:T(128)S(1)} %iota_xor_fusion.refs_0_, ...), custom_call_target="tpu_custom_call" | custom-call | flops 1207959552 | bytes 5898240 | tf_op jit(solution)/shard_map/dec_self/pallas_call | solution.py:368
  129.1 9.2 %enc_feed.1 = (f32[256,768]{1,0:T(8,128)}, bf16[256,768]{1,0:T(8,128)(2,1)}, bf16[256,3072]{1,0:T(8,128)(2,1)}, bf16[256,3072]{1,0:T(8,128)(2,1)}) custom-call(s32[8]{0:T(128)} %copy-done.90, bf16[256,768]{1,0:T(8,128)(2,1)} %copy-done.55, f32[3,768]{1,0:T(4,128)} %copy-done.83, f32[1,3072]{1,0:T(1,128)} %copy-done.101, bf16[3072,768]{1,0:T(8,128)(2,1)} %copy-done.1, ...), custom_call_target="tpu_custom_call" | custom-call | flops 2415919104 | bytes 18874368 | tf_op jit(solution)/shard_map/enc_feed/pallas_call | solution.py:368
  158.1 8.6 %dec_cross.1 = (f32[256,768]{1,0:T(8,128)}, bf16[256,768]{1,0:T(8,128)(2,1)}, bf16[256,768]{1,0:T(8,128)(2,1)}, bf16[256,768]{1,0:T(8,128)(2,1)}, bf16[256,768]{...) custom-call(s32[8]{0:T(128)} %copy-done.90, s32[1]{0:T(128)S(6)} %copy.28.refs_1_, ...), custom_call_target="tpu_custom_call" | custom-call | flops 1207959552 | bytes 5898240 | tf_op jit(solution)/shard_map/dec_cross/pallas_call | solution.py:368
  168.1 9.2 %dec_feed.1 = (f32[256,768]{1,0:T(8,128)}, bf16[256,768]{1,0:T(8,128)(2,1)}, bf16[256,3072]{1,0:T(8,128)(2,1)}, bf16[256,3072]{1,0:T(8,128)(2,1)}) custom-call(s32[8]{0:T(128)} %copy-done.90, bf16[256,768]{1,0:T(8,128)(2,1)} %get-tuple-element.168.refs_1_.refs_3_, f32[3,768]{1,0:T(4,128)} %copy-done.99, f32[1,3072]{1,0:T(1,128)} %copy-done.100, ...), custom_call_target="tpu_custom_call" | custom-call | flops 2415919104 | bytes 18874368 | tf_op jit(solution)/shard_map/dec_feed/pallas_call | solution.py:368
  177.3 6.9 %dec_back_out.1 = (f32[256,768]{1,0:T(8,128)}, f32[3,768]{1,0:T(4,128)}, bf16[1536,768]{1,0:T(8,128)(2,1)}, bf16[768,768]{1,0:T(8,128)(2,1)}, bf16[768,768]{1,0:T(8,128)(2,1)}) custom-call(s32[8]{0:T(128)} %copy-done.90, bf16[256,768]{1,0:T(8,128)(2,1)} %refs_1_.9, f32[256,768]{1,0:T(8,128)} %get-tuple-element.174.refs_2_.refs_5_, f32[3,768]{1,0:T(4,128)} %copy-done.99, ...), custom_call_target="tpu_custom_call" | custom-call | flops 1207959552 | bytes 9437184 | tf_op jit(solution)/shard_map/dec_back_out/pallas_call | solution.py:368
  184.8 11.6 %dec_back_in.1 = (f32[256,768]{1,0:T(8,128)}, f32[4,768]{1,0:T(4,128)}, bf16[1536,768]{1,0:T(8,128)(2,1)}, bf16[768,768]{1,0:T(8,128)(2,1)}, bf16[768,768]{1,0:T(8,128)(2,1)}) custom-call(s32[8]{0:T(128)} %copy-done.90, f32[256,768]{1,0:T(8,128)} %get-tuple-element.176.refs_1_, bf16[256,3072]{1,0:T(8,128)(2,1)} %get-tuple-element.177.refs_2_, ...), custom_call_target="tpu_custom_call" | custom-call | flops 3623878656 | bytes 14155776 | tf_op jit(solution)/shard_map/dec_back_in/pallas_call | solution.py:368
  201.3 11.7 %cross_back.1 = (f32[256,768]{1,0:T(8,128)S(1)}, f32[256,768]{1,0:T(8,128)S(1)}, f32[5,768]{1,0:T(8,128)S(1)}, bf16[1536,768]{1,0:T(8,128)(2,1)}, bf16[768,768]{1,0:T(8,128)(2,1)}, /*index=5*/bf16[768,768]{1,0:T(8,128)(2,1)}) custom-call(s32[8]{0:T(128)S(1)} %copy-done.91, f32[256,768]{1,0:T(8,128)S(1)} %copy-done.59, f32[256,768]{1,0:T(8,128)S(1)} %copy-done.40, ...), custom_call_target="tpu_custom_call" | custom-call | flops 2415919104 | bytes 11796480 | tf_op jit(solution)/shard_map/cross_back/pallas_call | solution.py:368
  222.2 5.5 %collective-permute-done.27.refs_2_.refs_9_ = bf16[768,768]{1,0:T(8,128)(2,1)S(1)} collective-permute-done((bf16[768,768]{1,0:T(8,128)(2,1)}, bf16[768,768]{1,0:T(8,128)(2,1)S(1)}, u32[]{:S(2)}, u32[]{:S(2)}) %collective-permute-start.27) | collective-permute-done | bytes 1179680 | tf_op jit(solution)/shard_map/ppermute | solution.py:328
  238.7 11.3 %enc_back_in.1 = (f32[256,768]{1,0:T(8,128)}, f32[4,768]{1,0:T(4,128)}, bf16[1536,768]{1,0:T(8,128)(2,1)}, bf16[768,768]{1,0:T(8,128)(2,1)}, bf16[768,768]{1,0:T(8,128)(2,1)}) custom-call(s32[8]{0:T(128)} %copy-done.90, f32[256,768]{1,0:T(8,128)} %copy-done.58, bf16[256,3072]{1,0:T(8,128)(2,1)} %get-tuple-element.208.refs_2_, bf16[256,768]{1,0:T(8,128)(2,1)} %copy-done.55, ...), custom_call_target="tpu_custom_call" | custom-call | flops 3623878656 | bytes 14155776 | tf_op jit(solution)/shard_map/enc_back_in/pallas_call | solution.py:368
  250.0 6.8 %collective-permute-done.31.refs_3_.refs_8_ = bf16[384,768]{1,0:T(8,128)(2,1)} collective-permute-done((bf16[384,768]{1,0:T(8,128)(2,1)}, bf16[384,768]{1,0:T(8,128)(2,1)}, u32[]{:S(2)}, u32[]{:S(2)}) %collective-permute-start.31) | collective-permute-done | bytes 589856 | tf_op jit(solution)/shard_map/ppermute | solution.py:328
  266.8 11.9 %self_back.1 = (f32[256,768]{1,0:T(8,128)}, f32[5,768]{1,0:T(8,128)S(1)}, bf16[1568,768]{1,0:T(8,128)(2,1)}, bf16[768,768]{1,0:T(8,128)(2,1)}, bf16[800,768]{1,0:T(8,128)(2,1)}) custom-call(s32[8]{0:T(128)S(1)} %copy-done.92, f32[256,768]{1,0:T(8,128)S(1)} %copy-done.57, f32[5,768]{1,0:T(8,128)S(1)} %get-tuple-element.204.refs_4_.refs_2_, ...), custom_call_target="tpu_custom_call" | custom-call | flops 2415919104 | bytes 11796480 | tf_op jit(solution)/shard_map/self_back/pallas_call | solution.py:368
  285.8 13.3 %enc_attn_back.1 = (f32[256,768]{1,0:T(8,128)}, f32[5,768]{1,0:T(8,128)}, bf16[1552,768]{1,0:T(8,128)(2,1)}, bf16[1552,768]{1,0:T(8,128)(2,1)}) custom-call(s32[8]{0:T(128)} %copy-done.90, f32[256,768]{1,0:T(8,128)} %get-tuple-element.217.refs_1_, f32[3,768]{1,0:T(4,128)} %copy-done.93, f32[4,768]{1,0:T(4,128)} %get-tuple-element.218.refs_4_.refs_3_, ...), custom_call_target="tpu_custom_call" | custom-call | flops 2415919104 | bytes 11796480 | tf_op jit(solution)/shard_map/enc_attn_back/pallas_call | solution.py:368
  299.1 7.7 %collective-permute-done.39.refs_16_.refs_10_ = bf16[384,768]{1,0:T(8,128)(2,1)} collective-permute-done((bf16[384,768]{1,0:T(8,128)(2,1)}, bf16[384,768]{1,0:T(8,128)(2,1)}, u32[]{:S(2)}, u32[]{:S(2)}) %collective-permute-start.39) | collective-permute-done | bytes 589856 | tf_op jit(solution)/shard_map/ppermute | solution.py:328
  320.7 6.2 %collective-permute-done.41.refs_3_.refs_4_ = bf16[192,768]{1,0:T(8,128)(2,1)S(1)} collective-permute-done((bf16[192,768]{1,0:T(8,128)(2,1)S(1)}, bf16[192,768]{1,0:T(8,128)(2,1)S(1)}, u32[]{:S(2)}, u32[]{:S(2)}) %collective-permute-start.41) | collective-permute-done | bytes 294944 | tf_op jit(solution)/shard_map/ppermute | solution.py:328
  336.0 12.6 %collective-permute-done.43.refs_2_.refs_14_ = bf16[384,768]{1,0:T(8,128)(2,1)S(1)} collective-permute-done((bf16[384,768]{1,0:T(8,128)(2,1)S(1)}, bf16[384,768]{1,0:T(8,128)(2,1)S(1)}, u32[]{:S(2)}, u32[]{:S(2)}) %collective-permute-start.43) | collective-permute-done | bytes 589856 | tf_op jit(solution)/shard_map/ppermute | solution.py:328
  362.1 4.9 add_8.1
  370.8 4.3 collective-permute-start.50
  375.2 7.8 %collective-permute-done.51.refs_11_.refs_14_ = bf16[384,768]{1,0:T(8,128)(2,1)S(1)} collective-permute-done((bf16[384,768]{1,0:T(8,128)(2,1)S(1)}, bf16[384,768]{1,0:T(8,128)(2,1)S(1)}, u32[]{:S(2)}, u32[]{:S(2)}) %collective-permute-start.51) | collective-permute-done | bytes 589856 | tf_op jit(solution)/shard_map/ppermute | solution.py:328
  382.9 4.1 add_9.1
  389.9 9.4 %collective-permute-done.50.refs_3_ = bf16[768,768]{1,0:T(8,128)(2,1)S(1)} collective-permute-done((bf16[768,768]{1,0:T(8,128)(2,1)S(1)}, bf16[768,768]{1,0:T(8,128)(2,1)S(1)}, u32[]{:S(2)}, u32[]{:S(2)}) %collective-permute-start.50) | collective-permute-done | bytes 1179680 | tf_op jit(solution)/shard_map/ppermute | solution.py:1157
  406.1 5.0 collective-permute-start.58
  413.7 21.1 %collective-permute-done.56.refs_3_ = bf16[384,768]{1,0:T(8,128)(2,1)S(1)} collective-permute-done((bf16[384,768]{1,0:T(8,128)(2,1)S(1)}, bf16[384,768]{1,0:T(8,128)(2,1)S(1)}, u32[]{:S(2)}, u32[]{:S(2)}) %collective-permute-start.56) | collective-permute-done | bytes 589856 | tf_op jit(solution)/shard_map/ppermute | solution.py:1157
  437.7 5.2 %collective-permute-start.59 = (bf16[400,768]{1,0:T(8,128)(2,1)S(1)}, bf16[400,768]{1,0:T(8,128)(2,1)}, u32[]{:S(2)}, u32[]{:S(2)}) collective-permute-start(bf16[400,768]{1,0:T(8,128)(2,1)S(1)} %get-tuple-element.274.refs_4_.refs_2_), channel_id=1, source_target_pairs={{0,8},{24,16},{1,9},{25,17},{2,10},{26,18},{3,11},{27,19},{4,12},{... | collective-permute-start | bytes 1843208 | tf_op jit(solution)/shard_map/ppermute | solution.py:1157
  461.3 14.2 %collective-permute-done.63.refs_2_.refs_4_ = bf16[768,768]{1,0:T(8,128)(2,1)} collective-permute-done((bf16[768,768]{1,0:T(8,128)(2,1)}, bf16[768,768]{1,0:T(8,128)(2,1)}, u32[]{:S(2)}, u32[]{:S(2)}) %collective-permute-start.63) | collective-permute-done | bytes 1179680 | tf_op jit(solution)/shard_map/ppermute | solution.py:1178
  478.3 9.8 %collective-permute-done.62.refs_2_ = bf16[384,768]{1,0:T(8,128)(2,1)S(1)} collective-permute-done((bf16[384,768]{1,0:T(8,128)(2,1)S(1)}, bf16[384,768]{1,0:T(8,128)(2,1)S(1)}, u32[]{:S(2)}, u32[]{:S(2)}) %collective-permute-start.62) | collective-permute-done | bytes 589856 | tf_op jit(solution)/shard_map/ppermute | solution.py:1178
  493.7 8.0 %collective-permute-done.66.refs_2_ = bf16[416,768]{1,0:T(8,128)(2,1)S(1)} collective-permute-done((bf16[416,768]{1,0:T(8,128)(2,1)S(1)}, bf16[416,768]{1,0:T(8,128)(2,1)S(1)}, u32[]{:S(2)}, u32[]{:S(2)}) %collective-permute-start.66) | collective-permute-done | bytes 639008 | tf_op jit(solution)/shard_map/ppermute | solution.py:1178
  505.7 4.3 collective-permute-done.65.refs_2_
  (378 shorter events, 193.0 us)
Async XLA Ops:
  3.8 30.4 %collective-permute-start.1 = (bf16[784,768]{1,0:T(8,128)(2,1)S(1)}, bf16[784,768]{1,0:T(8,128)(2,1)S(1)}, u32[]{:S(2)}, u32[]{:S(2)}) collective-permute-start(bf16[784,768]{1,0:T(8,128)(2,1)S(1)} %piece_1_pack.1.refs_2_.refs_0_), channel_id=1, source_target_pairs={{0,4},{1,5},{2,6},{3,7},{4,0},{5,1},{6,2},{7,3},{8,12},{9,13},{10,... | collective-permute-start | bytes 3612680 | tf_op jit(solution)/shard_map/ppermute | solution.py:328
  6.9 29.4 %collective-permute-start = (bf16[784,768]{1,0:T(8,128)(2,1)S(1)}, bf16[784,768]{1,0:T(8,128)(2,1)S(1)}, u32[]{:S(2)}, u32[]{:S(2)}) collective-permute-start(bf16[784,768]{1,0:T(8,128)(2,1)S(1)} %piece_1_pack.1.refs_2_.refs_0_), channel_id=1, source_target_pairs={{0,2},{1,3},{2,0},{3,1},{4,6},{5,7},{6,4},{7,5},{8,10},{9,11},{10,... | collective-permute-start | bytes 3612680 | tf_op jit(solution)/shard_map/ppermute | solution.py:328
  8.4 51.0 %collective-permute-start.5 = (bf16[768,768]{1,0:T(8,128)(2,1)S(1)}, bf16[768,768]{1,0:T(8,128)(2,1)S(1)}, u32[]{:S(2)}, u32[]{:S(2)}) collective-permute-start(bf16[768,768]{1,0:T(8,128)(2,1)S(1)} %piece_2_pack.1.refs_2_.refs_0_), channel_id=1, source_target_pairs={{0,4},{1,5},{2,6},{3,7},{4,0},{5,1},{6,2},{7,3},{8,12},{9,13},{10,... | collective-permute-start | bytes 3538952 | tf_op jit(solution)/shard_map/ppermute | solution.py:328
  9.0 52.5 %collective-permute-start.4 = (bf16[768,768]{1,0:T(8,128)(2,1)S(1)}, bf16[768,768]{1,0:T(8,128)(2,1)S(1)}, u32[]{:S(2)}, u32[]{:S(2)}) collective-permute-start(bf16[768,768]{1,0:T(8,128)(2,1)S(1)} %piece_2_pack.1.refs_2_.refs_0_), channel_id=1, source_target_pairs={{0,2},{1,3},{2,0},{3,1},{4,6},{5,7},{6,4},{7,5},{8,10},{9,11},{10,... | collective-permute-start | bytes 3538952 | tf_op jit(solution)/shard_map/ppermute | solution.py:328
  36.4 49.5 %collective-permute-start.3 = (bf16[400,768]{1,0:T(8,128)(2,1)S(1)}, bf16[400,768]{1,0:T(8,128)(2,1)S(1)}, u32[]{:S(2)}, u32[]{:S(2)}) collective-permute-start(bf16[400,768]{1,0:T(8,128)(2,1)S(1)} %get-tuple-element.149), channel_id=1, source_target_pairs={{0,2},{1,3},{2,0},{3,1},{4,6},{5,7},{6,4},{7,5},{8,10},{9,11},{10,... | collective-permute-start | bytes 1843208 | tf_op jit(solution)/shard_map/ppermute | solution.py:328
  37.9 34.2 %collective-permute-start.2 = (bf16[384,768]{1,0:T(8,128)(2,1)S(1)}, bf16[384,768]{1,0:T(8,128)(2,1)S(1)}, u32[]{:S(2)}, u32[]{:S(2)}) collective-permute-start(bf16[384,768]{1,0:T(8,128)(2,1)S(1)} %get-tuple-element.148.refs_2_), channel_id=1, source_target_pairs={{0,4},{1,5},{2,6},{3,7},{4,0},{5,1},{6,2},{7,3},{8,12},{9,13},{10,... | collective-permute-start | bytes 1769480 | tf_op jit(solution)/shard_map/ppermute | solution.py:328
  61.6 24.3 %collective-permute-start.7 = (bf16[384,768]{1,0:T(8,128)(2,1)S(1)}, bf16[384,768]{1,0:T(8,128)(2,1)S(1)}, u32[]{:S(2)}, u32[]{:S(2)}) collective-permute-start(bf16[384,768]{1,0:T(8,128)(2,1)S(1)} %get-tuple-element.151), channel_id=1, source_target_pairs={{0,2},{1,3},{2,0},{3,1},{4,6},{5,7},{6,4},{7,5},{8,10},{9,11},{10,... | collective-permute-start | bytes 1769480 | tf_op jit(solution)/shard_map/ppermute | solution.py:328
  63.2 22.7 %collective-permute-start.6 = (bf16[384,768]{1,0:T(8,128)(2,1)S(1)}, bf16[384,768]{1,0:T(8,128)(2,1)S(1)}, u32[]{:S(2)}, u32[]{:S(2)}) collective-permute-start(bf16[384,768]{1,0:T(8,128)(2,1)S(1)} %get-tuple-element.150.refs_7_), channel_id=1, source_target_pairs={{0,4},{1,5},{2,6},{3,7},{4,0},{5,1},{6,2},{7,3},{8,12},{9,13},{10,... | collective-permute-start | bytes 1769480 | tf_op jit(solution)/shard_map/ppermute | solution.py:328
  92.4 33.0 %collective-permute-start.11 = (bf16[768,768]{1,0:T(8,128)(2,1)S(1)}, bf16[768,768]{1,0:T(8,128)(2,1)S(1)}, u32[]{:S(2)}, u32[]{:S(2)}) collective-permute-start(bf16[768,768]{1,0:T(8,128)(2,1)S(1)} %piece_3_pack.1.refs_3_.refs_0_), channel_id=1, source_target_pairs={{0,4},{1,5},{2,6},{3,7},{4,0},{5,1},{6,2},{7,3},{8,12},{9,13},{10,... | collective-permute-start | bytes 3538952 | tf_op jit(solution)/shard_map/ppermute | solution.py:328
  92.8 32.6 %collective-permute-start.10 = (bf16[768,768]{1,0:T(8,128)(2,1)S(1)}, bf16[768,768]{1,0:T(8,128)(2,1)S(1)}, u32[]{:S(2)}, u32[]{:S(2)}) collective-permute-start(bf16[768,768]{1,0:T(8,128)(2,1)S(1)} %piece_3_pack.1.refs_3_.refs_0_), channel_id=1, source_target_pairs={{0,2},{1,3},{2,0},{3,1},{4,6},{5,7},{6,4},{7,5},{8,10},{9,11},{10,... | collective-permute-start | bytes 3538952 | tf_op jit(solution)/shard_map/ppermute | solution.py:328
  111.6 26.6 %collective-permute-start.15 = (bf16[384,768]{1,0:T(8,128)(2,1)S(1)}, bf16[384,768]{1,0:T(8,128)(2,1)}, u32[]{:S(2)}, u32[]{:S(2)}) collective-permute-start(bf16[384,768]{1,0:T(8,128)(2,1)S(1)} %piece_4_pack.1.refs_7_.refs_0_), channel_id=1, source_target_pairs={{0,4},{1,5},{2,6},{3,7},{4,0},{5,1},{6,2},{7,3},{8,12},{9,13},{10,... | collective-permute-start | bytes 1769480 | tf_op jit(solution)/shard_map/ppermute | solution.py:328
  112.0 26.3 %collective-permute-start.14 = (bf16[384,768]{1,0:T(8,128)(2,1)S(1)}, bf16[384,768]{1,0:T(8,128)(2,1)}, u32[]{:S(2)}, u32[]{:S(2)}) collective-permute-start(bf16[384,768]{1,0:T(8,128)(2,1)S(1)} %piece_4_pack.1.refs_7_.refs_0_), channel_id=1, source_target_pairs={{0,2},{1,3},{2,0},{3,1},{4,6},{5,7},{6,4},{7,5},{8,10},{9,11},{10,... | collective-permute-start | bytes 1769480 | tf_op jit(solution)/shard_map/ppermute | solution.py:328
  199.6 28.2 %collective-permute-start.27 = (bf16[768,768]{1,0:T(8,128)(2,1)}, bf16[768,768]{1,0:T(8,128)(2,1)S(1)}, u32[]{:S(2)}, u32[]{:S(2)}) collective-permute-start(bf16[768,768]{1,0:T(8,128)(2,1)} %add_1.1.refs_13_), channel_id=1, source_target_pairs={{0,2},{1,3},{2,0},{3,1},{4,6},{5,7},{6,4},{7,5},{8,10},{9,11},{10,... | collective-permute-start | bytes 3538952 | tf_op jit(solution)/shard_map/ppermute | solution.py:328
  215.8 40.9 %collective-permute-start.30 = (bf16[768,768]{1,0:T(8,128)(2,1)}, bf16[768,768]{1,0:T(8,128)(2,1)}, u32[]{:S(2)}, u32[]{:S(2)}) collective-permute-start(bf16[768,768]{1,0:T(8,128)(2,1)} %add_2.1.refs_6_), channel_id=1, source_target_pairs={{0,4},{1,5},{2,6},{3,7},{4,0},{5,1},{6,2},{7,3},{8,12},{9,13},{10,... | collective-permute-start | bytes 3538952 | tf_op jit(solution)/shard_map/ppermute | solution.py:328
  234.9 26.0 %collective-permute-start.29 = (bf16[768,768]{1,0:T(8,128)(2,1)}, bf16[768,768]{1,0:T(8,128)(2,1)S(1)}, u32[]{:S(2)}, u32[]{:S(2)}) collective-permute-start(bf16[768,768]{1,0:T(8,128)(2,1)} %get-tuple-element.234), channel_id=1, source_target_pairs={{0,1},{1,0},{2,3},{3,2},{4,5},{5,4},{6,7},{7,6},{8,9},{9,8},{10,11... | collective-permute-start | bytes 3538952 | tf_op jit(solution)/shard_map/ppermute | solution.py:328
  235.0 25.9 %collective-permute-start.28 = (bf16[768,768]{1,0:T(8,128)(2,1)}, bf16[768,768]{1,0:T(8,128)(2,1)}, u32[]{:S(2)}, u32[]{:S(2)}) collective-permute-start(bf16[768,768]{1,0:T(8,128)(2,1)} %get-tuple-element.233), channel_id=1, source_target_pairs={{0,1},{1,0},{2,3},{3,2},{4,5},{5,4},{6,7},{7,6},{8,9},{9,8},{10,11... | collective-permute-start | bytes 3538952 | tf_op jit(solution)/shard_map/ppermute | solution.py:328
  237.2 41.5 %collective-permute-start.35 = (bf16[768,768]{1,0:T(8,128)(2,1)}, bf16[768,768]{1,0:T(8,128)(2,1)}, u32[]{:S(2)}, u32[]{:S(2)}) collective-permute-start(bf16[768,768]{1,0:T(8,128)(2,1)} %add_3b.1.refs_8_), channel_id=1, source_target_pairs={{0,2},{1,3},{2,0},{3,1},{4,6},{5,7},{6,4},{7,5},{8,10},{9,11},{10,... | collective-permute-start | bytes 3538952 | tf_op jit(solution)/shard_map/ppermute | solution.py:328
  265.1 41.7 %collective-permute-start.36 = (bf16[800,768]{1,0:T(8,128)(2,1)}, bf16[800,768]{1,0:T(8,128)(2,1)}, u32[]{:S(2)}, u32[]{:S(2)}) collective-permute-start(bf16[800,768]{1,0:T(8,128)(2,1)} %add_4b.1.refs_15_), channel_id=1, source_target_pairs={{0,4},{1,5},{2,6},{3,7},{4,0},{5,1},{6,2},{7,3},{8,12},{9,13},{10,... | collective-permute-start | bytes 3686408 | tf_op jit(solution)/shard_map/ppermute | solution.py:328
  283.2 23.6 %collective-permute-start.38 = (bf16[800,768]{1,0:T(8,128)(2,1)}, bf16[800,768]{1,0:T(8,128)(2,1)}, u32[]{:S(2)}, u32[]{:S(2)}) collective-permute-start(bf16[800,768]{1,0:T(8,128)(2,1)} %get-tuple-element.249), channel_id=1, source_target_pairs={{0,1},{1,0},{2,3},{3,2},{4,5},{5,4},{6,7},{7,6},{8,9},{9,8},{10,11... | collective-permute-start | bytes 3686408 | tf_op jit(solution)/shard_map/ppermute | solution.py:328
  283.2 23.5 %collective-permute-start.37 = (bf16[768,768]{1,0:T(8,128)(2,1)}, bf16[768,768]{1,0:T(8,128)(2,1)S(1)}, u32[]{:S(2)}, u32[]{:S(2)}) collective-permute-start(bf16[768,768]{1,0:T(8,128)(2,1)} %get-tuple-element.248), channel_id=1, source_target_pairs={{0,1},{1,0},{2,3},{3,2},{4,5},{5,4},{6,7},{7,6},{8,9},{9,8},{10,11... | collective-permute-start | bytes 3538952 | tf_op jit(solution)/shard_map/ppermute | solution.py:328
  283.7 37.0 %collective-permute-start.44 = (bf16[768,768]{1,0:T(8,128)(2,1)}, bf16[768,768]{1,0:T(8,128)(2,1)}, u32[]{:S(2)}, u32[]{:S(2)}) collective-permute-start(bf16[768,768]{1,0:T(8,128)(2,1)} %add_5b.1.refs_14_), channel_id=1, source_target_pairs={{0,2},{1,3},{2,0},{3,1},{4,6},{5,7},{6,4},{7,5},{8,10},{9,11},{10,... | collective-permute-start | bytes 3538952 | tf_op jit(solution)/shard_map/ppermute | solution.py:328
  328.7 29.5 %collective-permute-start.40 = (bf16[768,768]{1,0:T(8,128)(2,1)S(1)}, bf16[768,768]{1,0:T(8,128)(2,1)S(1)}, u32[]{:S(2)}, u32[]{:S(2)}) collective-permute-start(bf16[768,768]{1,0:T(8,128)(2,1)S(1)} %get-tuple-element.251.refs_0_), channel_id=1, source_target_pairs={{0,8},{24,16},{1,9},{25,17},{2,10},{26,18},{3,11},{27,19},{4,12},{... | collective-permute-start | bytes 3538952 | tf_op jit(solution)/shard_map/ppermute | solution.py:1157
  334.0 22.0 %collective-permute-start.48 = (bf16[384,768]{1,0:T(8,128)(2,1)S(1)}, bf16[384,768]{1,0:T(8,128)(2,1)S(1)}, u32[]{:S(2)}, u32[]{:S(2)}) collective-permute-start(bf16[384,768]{1,0:T(8,128)(2,1)S(1)} %add_6b.1.refs_4_), channel_id=1, source_target_pairs={{0,4},{1,5},{2,6},{3,7},{4,0},{5,1},{6,2},{7,3},{8,12},{9,13},{10,... | collective-permute-start | bytes 1769480 | tf_op jit(solution)/shard_map/ppermute | solution.py:328
  370.8 28.5 %collective-permute-start.50 = (bf16[768,768]{1,0:T(8,128)(2,1)S(1)}, bf16[768,768]{1,0:T(8,128)(2,1)S(1)}, u32[]{:S(2)}, u32[]{:S(2)}) collective-permute-start(bf16[768,768]{1,0:T(8,128)(2,1)S(1)} %get-tuple-element.262.refs_2_), channel_id=1, source_target_pairs={{0,8},{24,16},{1,9},{25,17},{2,10},{26,18},{3,11},{27,19},{4,12},{... | collective-permute-start | bytes 3538952 | tf_op jit(solution)/shard_map/ppermute | solution.py:1157
  405.4 29.4 %collective-permute-start.55 = (bf16[768,768]{1,0:T(8,128)(2,1)S(1)}, bf16[768,768]{1,0:T(8,128)(2,1)S(1)}, u32[]{:S(2)}, u32[]{:S(2)}) collective-permute-start(bf16[768,768]{1,0:T(8,128)(2,1)S(1)} %get-tuple-element.267.refs_0_), channel_id=1, source_target_pairs={{8,16},{16,8},{9,17},{17,9},{10,18},{18,10},{11,19},{19,11},{12,20... | collective-permute-start | bytes 3538952 | tf_op jit(solution)/shard_map/ppermute | solution.py:1171
  406.1 30.8 %collective-permute-start.58 = (bf16[416,768]{1,0:T(8,128)(2,1)S(1)}, bf16[416,768]{1,0:T(8,128)(2,1)S(1)}, u32[]{:S(2)}, u32[]{:S(2)}) collective-permute-start(bf16[416,768]{1,0:T(8,128)(2,1)S(1)} %get-tuple-element.273.refs_0_), channel_id=1, source_target_pairs={{0,8},{24,16},{1,9},{25,17},{2,10},{26,18},{3,11},{27,19},{4,12},{... | collective-permute-start | bytes 1916936 | tf_op jit(solution)/shard_map/ppermute | solution.py:1157
  411.1 23.7 %collective-permute-start.56 = (bf16[384,768]{1,0:T(8,128)(2,1)S(1)}, bf16[384,768]{1,0:T(8,128)(2,1)S(1)}, u32[]{:S(2)}, u32[]{:S(2)}) collective-permute-start(bf16[384,768]{1,0:T(8,128)(2,1)S(1)} %get-tuple-element.268.refs_2_), channel_id=1, source_target_pairs={{0,8},{24,16},{1,9},{25,17},{2,10},{26,18},{3,11},{27,19},{4,12},{... | collective-permute-start | bytes 1769480 | tf_op jit(solution)/shard_map/ppermute | solution.py:1157
  412.4 34.8 %collective-permute-start.60 = (bf16[768,768]{1,0:T(8,128)(2,1)S(1)}, bf16[768,768]{1,0:T(8,128)(2,1)}, u32[]{:S(2)}, u32[]{:S(2)}) collective-permute-start(bf16[768,768]{1,0:T(8,128)(2,1)S(1)} %get-tuple-element.275.refs_1_), channel_id=1, source_target_pairs={{8,0},{16,24},{9,1},{17,25},{10,2},{18,26},{11,3},{19,27},{12,4},{... | collective-permute-start | bytes 3538952 | tf_op jit(solution)/shard_map/ppermute | solution.py:1178
  444.4 31.1 %collective-permute-start.63 = (bf16[768,768]{1,0:T(8,128)(2,1)}, bf16[768,768]{1,0:T(8,128)(2,1)}, u32[]{:S(2)}, u32[]{:S(2)}) collective-permute-start(bf16[768,768]{1,0:T(8,128)(2,1)} %get-tuple-element.279.refs_1_.refs_3_), channel_id=1, source_target_pairs={{8,0},{16,24},{9,1},{17,25},{10,2},{18,26},{11,3},{19,27},{12,4},{... | collective-permute-start | bytes 3538952 | tf_op jit(solution)/shard_map/ppermute | solution.py:1178
  456.4 34.1 %collective-permute-start.61 = (bf16[400,768]{1,0:T(8,128)(2,1)S(1)}, bf16[400,768]{1,0:T(8,128)(2,1)S(1)}, u32[]{:S(2)}, u32[]{:S(2)}) collective-permute-start(bf16[400,768]{1,0:T(8,128)(2,1)S(1)} %get-tuple-element.277.refs_0_), channel_id=1, source_target_pairs={{8,16},{16,8},{9,17},{17,9},{10,18},{18,10},{11,19},{19,11},{12,20... | collective-permute-start | bytes 1843208 | tf_op jit(solution)/shard_map/ppermute | solution.py:1171
  457.1 31.0 %collective-permute-start.62 = (bf16[384,768]{1,0:T(8,128)(2,1)S(1)}, bf16[384,768]{1,0:T(8,128)(2,1)S(1)}, u32[]{:S(2)}, u32[]{:S(2)}) collective-permute-start(bf16[384,768]{1,0:T(8,128)(2,1)S(1)} %get-tuple-element.278.refs_2_.refs_1_), channel_id=1, source_target_pairs={{8,0},{16,24},{9,1},{17,25},{10,2},{18,26},{11,3},{19,27},{12,4},{... | collective-permute-start | bytes 1769480 | tf_op jit(solution)/shard_map/ppermute | solution.py:1178
  460.0 41.8 %collective-permute-start.66 = (bf16[416,768]{1,0:T(8,128)(2,1)S(1)}, bf16[416,768]{1,0:T(8,128)(2,1)S(1)}, u32[]{:S(2)}, u32[]{:S(2)}) collective-permute-start(bf16[416,768]{1,0:T(8,128)(2,1)S(1)} %add_14.1.refs_3_.refs_1_), channel_id=1, source_target_pairs={{8,0},{16,24},{9,1},{17,25},{10,2},{18,26},{11,3},{19,27},{12,4},{... | collective-permute-start | bytes 1916936 | tf_op jit(solution)/shard_map/ppermute | solution.py:1178
  (143 other events, 1064.2 us)

commit v5 on v4

--- a/solution.py
+++ b/solution.py
@@ -13,6 +13,7 @@
 VMEM_BYTES = 56 * 1024 * 1024
 SMALL_VMEM_BYTES = 20 * 1024 * 1024
 MIDDLE_VMEM_BYTES = 44 * 1024 * 1024
+WIDE = ("add_6a", "add_6b", "add_6c", "add_8", "add_9")
 MIDDLE = ('enc_attn', 'dec_self', 'cross_back', 'enc_back_out', 'self_back')
 ANY = pl.BlockSpec(memory_space=pl.ANY)
 SMEM = pl.BlockSpec(memory_space=pltpu.SMEM)
@@ -364,7 +365,7 @@
         extra = self.waits + ([] if self.token is None else [self.token])
         self.waits = []
         count, skip = len(operands), len(extra)
-        grant = SMALL_VMEM_BYTES if not flops else MIDDLE_VMEM_BYTES if name in MIDDLE else VMEM_BYTES
+        grant = SMALL_VMEM_BYTES if not flops and name not in WIDE else MIDDLE_VMEM_BYTES if name in MIDDLE else VMEM_BYTES
         results = pl.pallas_call(
             lambda *refs: body(*refs[:count], *refs[count + skip :]),
             out_shape=[jax.ShapeDtypeStruct(shape, dtype) for shape, dtype, spec in outs],
@@ -1344,29 +1345,31 @@
     red_5.cores_done()
     mark(*red_2.last)
     combine(
-        order, "add_6a", red_3.second(), red_5.first(), own_stack([red_0, red_1], keep_as("a"))
+        order, "add_6a", red_3.second(), red_4.second(), own_stack([red_0, red_1], keep_as("a"))
     )
     line_a = Line(totals["a"])
-    mark(red_5.landed[1])
-    combine(order, "add_6b", red_4.second())
     red_6.cores()
-    mark(*red_3.last)
     red_6.cores_done()
-    combine(order, "add_6c", red_6.first())
-    mark(*red_6.landed, *red_4.last)
-    combine(order, "add_8", line_a.middle(), red_5.second(), own_stack([red_2, red_3], keep_as("b")))
-    line_b = Line(totals["b"])
-    mark(*red_5.last)
-    combine(order, "add_9", red_6.second(), red_4.own(keep_as(4)), red_5.own(keep_as(5)))
-    combine(order, "add_10", line_a.outward(), line_b.middle(), red_6.own(keep_as(6)))
-    line_4 = Line(totals[4])
+    combine(
+        order, "add_6b", red_5.first(), red_6.first(), own_stack([red_2, red_3], keep_as("b")),
+        red_4.own(keep_as(4)),
+    )
+    combine(order, "add_7", line_a.middle())
+    mark(*red_6.landed)
+    combine(order, "add_8", red_5.second())
+    line_b = Line(order.tie(totals["b"]))
+    line_4 = Line(order.tie(totals[4]))
+    combine(order, "add_9", red_6.second(), red_5.own(keep_as(5)), line_a.outward())
+    combine(order, "add_10", line_b.middle())
+    combine(order, "add_11", red_6.own(keep_as(6)), line_4.middle())
     line_5 = Line(order.tie(totals[5]))
-    combine(order, "add_11", line_b.outward(), line_4.middle())
-    combine(order, "add_12", line_5.middle())
-    line_6 = Line(order.tie(totals[6]))
+    line_6 = Line(totals[6])
+    mark(line_a.landed)
+    combine(order, "add_12", line_b.outward())
     (grad_d_w2,) = finish(order, inner, [line_a.part(0)], False, "out_0")
     (grad_d_w1,) = finish(order, inner, [line_a.part(half)], True, "out_1")
-    combine(order, "add_13", line_4.outward(), line_6.middle())
+    combine(order, "add_13", line_4.outward(), line_5.middle(), line_6.middle())
+    mark(line_b.landed)
     combine(order, "add_14", line_5.outward())
     (grad_e_w2,) = finish(order, inner, [line_b.part(half)], False, "out_3")
     (grad_e_w1,) = finish(order, inner, [line_4.part(0)], True, "out_4")

time: 519 us -> 499 us (0.961)
  waiting for transfers between devices: 207 us -> 195 us
  starting transfers between devices: 78.5 us -> 73.2 us
    ppermute x5, waiting for transfers between devices: 32.7 us -> 20.4 us  [__init__(): self.landed = lax.ppermute(value, 'rep', [(0, 1), (3, 2)])]
    ppermute x5, waiting for transfers between devices: 36.4 us -> 30.4 us  [outward_sent(): self.landed = lax.ppermute(value, 'rep', [(1, 0), (2, 3)])]
    ppermute x52, waiting for transfers between devices: 138 us -> 144 us  [swap(): return lax.ppermute(value, 'fsdp', [(i, i ^ bit) for i in range(8)])]
    unnamed x216 -> x242, local copies, waits for them, and re-layouts: 35.7 us -> 38.4 us
  transfers between devices with their start and end apart: 67 -> 67, of which waited for: 27 -> 29; matrix products, arithmetic and copies ran while one was open for 0% -> 0% of each run, Pallas kernels for 30% -> 31%
where the time goes in v5:
time: 499 us; the launch traced here: 492 us
  waiting for transfers between devices  195 us (39%)
  Pallas kernels  178 us (36%)
  starting transfers between devices  73.2 us (15%)
  local copies, waits for them, and re-layouts  42.1 us (8%)
    pallas_call x50, Pallas kernels, kernel(): pl.pallas_call(lambda *refs: body(*refs[:count], *refs[count + skip:]), o...  178 us
    ppermute x52, waiting for transfers between devices, swap(): return lax.ppermute(value, 'fsdp', [(i, i ^ bit) for i in range(8)])  144 us
    ppermute x52, starting transfers between devices, swap(): return lax.ppermute(value, 'fsdp', [(i, i ^ bit) for i in range(8)])  44.4 us
    unnamed x242, local copies, waits for them, and re-layouts  38.4 us
    ppermute x5, waiting for transfers between devices, outward_sent(): self.landed = lax.ppermute(value, 'rep', [(1, 0), (2, 3)])  30.4 us
    ppermute x5, waiting for transfers between devices, __init__(): self.landed = lax.ppermute(value, 'rep', [(0, 1), (3, 2)])  20.4 us
    ppermute x5, starting transfers between devices, __init__(): self.landed = lax.ppermute(value, 'rep', [(0, 1), (3, 2)])  17.9 us
  transfers between devices with their start and end apart: 67, of which 29 were waited for; matrix products, arithmetic and copies ran while one was open for 0% of the time, Pallas kernels for 31%

profile of v5, /device:TPU:0, one launch (start us, length us, event | category | flops | bytes accessed | tf_op | source)
XLA Modules:
  0.0 492.4 jit_solution(14459143875944322097)
XLA Ops:
  9.6 24.6 %collective-permute-done.1.refs_1_.refs_2_ = bf16[784,768]{1,0:T(8,128)(2,1)S(1)} collective-permute-done((bf16[784,768]{1,0:T(8,128)(2,1)S(1)}, bf16[784,768]{1,0:T(8,128)(2,1)S(1)}, u32[]{:S(2)}, u32[]{:S(2)}) %collective-permute-start.1) | collective-permute-done | bytes 1204256 | tf_op jit(solution)/shard_map/ppermute | solution.py:329
  38.4 21.0 %collective-permute-done.5.refs_1_.refs_2_ = bf16[768,768]{1,0:T(8,128)(2,1)S(1)} collective-permute-done((bf16[768,768]{1,0:T(8,128)(2,1)S(1)}, bf16[768,768]{1,0:T(8,128)(2,1)S(1)}, u32[]{:S(2)}, u32[]{:S(2)}) %collective-permute-start.5) | collective-permute-done | bytes 1179680 | tf_op jit(solution)/shard_map/ppermute | solution.py:329
  63.7 8.4 %collective-permute-done.2.refs_3_ = bf16[384,768]{1,0:T(8,128)(2,1)S(1)} collective-permute-done((bf16[384,768]{1,0:T(8,128)(2,1)S(1)}, bf16[384,768]{1,0:T(8,128)(2,1)S(1)}, u32[]{:S(2)}, u32[]{:S(2)}) %collective-permute-start.2) | collective-permute-done | bytes 589856 | tf_op jit(solution)/shard_map/ppermute | solution.py:329
  72.1 13.8 %collective-permute-done.7.refs_6_.refs_4_ = bf16[384,768]{1,0:T(8,128)(2,1)S(1)} collective-permute-done((bf16[384,768]{1,0:T(8,128)(2,1)S(1)}, bf16[384,768]{1,0:T(8,128)(2,1)S(1)}, u32[]{:S(2)}, u32[]{:S(2)}) %collective-permute-start.7) | collective-permute-done | bytes 589856 | tf_op jit(solution)/shard_map/ppermute | solution.py:329
  99.7 8.6 %enc_attn.1 = (f32[256,768]{1,0:T(8,128)S(1)}, bf16[256,768]{1,0:T(8,128)(2,1)S(1)}, bf16[256,768]{1,0:T(8,128)(2,1)S(1)}, bf16[256,768]{1,0:T(8,128)(2,1)S(1)},...) custom-call(s32[8]{0:T(128)S(1)} %iota_xor_fusion.refs_0_, ...), custom_call_target="tpu_custom_call" | custom-call | flops 1207959552 | bytes 5898240 | tf_op jit(solution)/shard_map/enc_attn/pallas_call | solution.py:369
  113.1 9.0 %dec_self.1 = (f32[256,768]{1,0:T(8,128)S(1)}, bf16[256,768]{1,0:T(8,128)(2,1)S(1)}, bf16[256,768]{1,0:T(8,128)(2,1)S(1)}, bf16[256,768]{1,0:T(8,128)(2,1)S(1)},...) custom-call(s32[8]{0:T(128)S(1)} %iota_xor_fusion.refs_0_, ...), custom_call_target="tpu_custom_call" | custom-call | flops 1207959552 | bytes 5898240 | tf_op jit(solution)/shard_map/dec_self/pallas_call | solution.py:369
  130.8 9.3 %enc_feed.1 = (f32[256,768]{1,0:T(8,128)}, bf16[256,768]{1,0:T(8,128)(2,1)}, bf16[256,3072]{1,0:T(8,128)(2,1)}, bf16[256,3072]{1,0:T(8,128)(2,1)}) custom-call(s32[8]{0:T(128)} %copy-done.92, bf16[256,768]{1,0:T(8,128)(2,1)} %copy-done.53, f32[3,768]{1,0:T(4,128)} %copy-done.87, f32[1,3072]{1,0:T(1,128)} %copy-done.102, bf16[3072,768]{1,0:T(8,128)(2,1)} %copy-done.1, ...), custom_call_target="tpu_custom_call" | custom-call | flops 2415919104 | bytes 18874368 | tf_op jit(solution)/shard_map/enc_feed/pallas_call | solution.py:369
  158.1 8.6 %dec_cross.1 = (f32[256,768]{1,0:T(8,128)}, bf16[256,768]{1,0:T(8,128)(2,1)}, bf16[256,768]{1,0:T(8,128)(2,1)}, bf16[256,768]{1,0:T(8,128)(2,1)}, bf16[256,768]{...) custom-call(s32[8]{0:T(128)} %copy-done.92, s32[1]{0:T(128)S(6)} %copy.28.refs_1_, ...), custom_call_target="tpu_custom_call" | custom-call | flops 1207959552 | bytes 5898240 | tf_op jit(solution)/shard_map/dec_cross/pallas_call | solution.py:369
  166.6 9.3 %dec_feed.1 = (f32[256,768]{1,0:T(8,128)}, bf16[256,768]{1,0:T(8,128)(2,1)}, bf16[256,3072]{1,0:T(8,128)(2,1)}, bf16[256,3072]{1,0:T(8,128)(2,1)}) custom-call(s32[8]{0:T(128)} %copy-done.92, bf16[256,768]{1,0:T(8,128)(2,1)} %get-tuple-element.169.refs_1_.refs_3_, f32[3,768]{1,0:T(4,128)} %copy-done.100, f32[1,3072]{1,0:T(1,128)} %copy-done.101, ...), custom_call_target="tpu_custom_call" | custom-call | flops 2415919104 | bytes 18874368 | tf_op jit(solution)/shard_map/dec_feed/pallas_call | solution.py:369
  175.9 6.9 %dec_back_out.1 = (f32[256,768]{1,0:T(8,128)}, f32[3,768]{1,0:T(4,128)}, bf16[1536,768]{1,0:T(8,128)(2,1)}, bf16[768,768]{1,0:T(8,128)(2,1)}, bf16[768,768]{1,0:T(8,128)(2,1)}) custom-call(s32[8]{0:T(128)} %copy-done.92, bf16[256,768]{1,0:T(8,128)(2,1)} %refs_1_.9, f32[256,768]{1,0:T(8,128)} %get-tuple-element.175.refs_2_.refs_5_, f32[3,768]{1,0:T(4,128)} %copy-done.100, ...), custom_call_target="tpu_custom_call" | custom-call | flops 1207959552 | bytes 9437184 | tf_op jit(solution)/shard_map/dec_back_out/pallas_call | solution.py:369
  183.4 11.6 %dec_back_in.1 = (f32[256,768]{1,0:T(8,128)}, f32[4,768]{1,0:T(4,128)}, bf16[1536,768]{1,0:T(8,128)(2,1)}, bf16[768,768]{1,0:T(8,128)(2,1)}, bf16[768,768]{1,0:T(8,128)(2,1)}) custom-call(s32[8]{0:T(128)} %copy-done.92, f32[256,768]{1,0:T(8,128)} %get-tuple-element.177.refs_1_, bf16[256,3072]{1,0:T(8,128)(2,1)} %get-tuple-element.178.refs_2_, ...), custom_call_target="tpu_custom_call" | custom-call | flops 3623878656 | bytes 14155776 | tf_op jit(solution)/shard_map/dec_back_in/pallas_call | solution.py:369
  199.3 11.7 %cross_back.1 = (f32[256,768]{1,0:T(8,128)S(1)}, f32[256,768]{1,0:T(8,128)S(1)}, f32[5,768]{1,0:T(8,128)S(1)}, bf16[1536,768]{1,0:T(8,128)(2,1)}, bf16[768,768]{1,0:T(8,128)(2,1)}, /*index=5*/bf16[768,768]{1,0:T(8,128)(2,1)}) custom-call(s32[8]{0:T(128)S(1)} %copy-done.93, f32[256,768]{1,0:T(8,128)S(1)} %copy-done.59, f32[256,768]{1,0:T(8,128)S(1)} %copy-done.37, ...), custom_call_target="tpu_custom_call" | custom-call | flops 2415919104 | bytes 11796480 | tf_op jit(solution)/shard_map/cross_back/pallas_call | solution.py:369
  220.3 5.3 %collective-permute-done.27.refs_2_.refs_9_ = bf16[768,768]{1,0:T(8,128)(2,1)S(1)} collective-permute-done((bf16[768,768]{1,0:T(8,128)(2,1)S(1)}, bf16[768,768]{1,0:T(8,128)(2,1)S(1)}, u32[]{:S(2)}, u32[]{:S(2)}) %collective-permute-start.27) | collective-permute-done | bytes 1179680 | tf_op jit(solution)/shard_map/ppermute | solution.py:329
  236.5 11.2 %enc_back_in.1 = (f32[256,768]{1,0:T(8,128)}, f32[4,768]{1,0:T(4,128)}, bf16[1536,768]{1,0:T(8,128)(2,1)}, bf16[768,768]{1,0:T(8,128)(2,1)}, bf16[768,768]{1,0:T(8,128)(2,1)}) custom-call(s32[8]{0:T(128)} %copy-done.92, f32[256,768]{1,0:T(8,128)} %copy-done.58, bf16[256,3072]{1,0:T(8,128)(2,1)} %get-tuple-element.209.refs_2_, bf16[256,768]{1,0:T(8,128)(2,1)} %copy-done.53, ...), custom_call_target="tpu_custom_call" | custom-call | flops 3623878656 | bytes 14155776 | tf_op jit(solution)/shard_map/enc_back_in/pallas_call | solution.py:369
  247.7 7.0 %collective-permute-done.31.refs_3_.refs_8_ = bf16[384,768]{1,0:T(8,128)(2,1)} collective-permute-done((bf16[384,768]{1,0:T(8,128)(2,1)}, bf16[384,768]{1,0:T(8,128)(2,1)}, u32[]{:S(2)}, u32[]{:S(2)}) %collective-permute-start.31) | collective-permute-done | bytes 589856 | tf_op jit(solution)/shard_map/ppermute | solution.py:329
  263.8 11.9 %self_back.1 = (f32[256,768]{1,0:T(8,128)}, f32[5,768]{1,0:T(8,128)S(1)}, bf16[1568,768]{1,0:T(8,128)(2,1)}, bf16[768,768]{1,0:T(8,128)(2,1)}, bf16[800,768]{1,0:T(8,128)(2,1)}) custom-call(s32[8]{0:T(128)S(1)} %copy-done.94, f32[256,768]{1,0:T(8,128)S(1)} %copy-done.57, f32[5,768]{1,0:T(8,128)S(1)} %get-tuple-element.205.refs_4_.refs_2_, ...), custom_call_target="tpu_custom_call" | custom-call | flops 2415919104 | bytes 11796480 | tf_op jit(solution)/shard_map/self_back/pallas_call | solution.py:369
  282.1 13.2 %enc_attn_back.1 = (f32[256,768]{1,0:T(8,128)}, f32[5,768]{1,0:T(8,128)}, bf16[1552,768]{1,0:T(8,128)(2,1)}, bf16[1552,768]{1,0:T(8,128)(2,1)}) custom-call(s32[8]{0:T(128)} %copy-done.92, f32[256,768]{1,0:T(8,128)} %get-tuple-element.218.refs_1_, f32[3,768]{1,0:T(4,128)} %copy-done.95, f32[4,768]{1,0:T(4,128)} %get-tuple-element.219.refs_4_.refs_3_, ...), custom_call_target="tpu_custom_call" | custom-call | flops 2415919104 | bytes 11796480 | tf_op jit(solution)/shard_map/enc_attn_back/pallas_call | solution.py:369
  295.3 8.2 %collective-permute-done.40.refs_16_.refs_7_ = bf16[384,768]{1,0:T(8,128)(2,1)S(1)} collective-permute-done((bf16[384,768]{1,0:T(8,128)(2,1)}, bf16[384,768]{1,0:T(8,128)(2,1)S(1)}, u32[]{:S(2)}, u32[]{:S(2)}) %collective-permute-start.40) | collective-permute-done | bytes 589856 | tf_op jit(solution)/shard_map/ppermute | solution.py:329
  303.6 4.5 collective-permute-done.37.refs_5_.refs_16_
  309.6 4.9 add_6a.1
  320.3 13.7 %collective-permute-done.43.refs_15_ = bf16[384,768]{1,0:T(8,128)(2,1)S(1)} collective-permute-done((bf16[384,768]{1,0:T(8,128)(2,1)}, bf16[384,768]{1,0:T(8,128)(2,1)S(1)}, u32[]{:S(2)}, u32[]{:S(2)}) %collective-permute-start.43) | collective-permute-done | bytes 589856 | tf_op jit(solution)/shard_map/ppermute | solution.py:329
  336.0 5.7 %add_6b.1 = (bf16[224,768]{1,0:T(8,128)(2,1)}, bf16[192,768]{1,0:T(8,128)(2,1)}, bf16[208,768]{1,0:T(8,128)(2,1)}, bf16[192,768]{1,0:T(8,128)(2,1)}, bf16[768,768]{1,0:T(8,128)(2,1)}, /*index=5*/bf16[384,768]{1,0:T(8,128)(2,1)}) custom-call(bf16[1568,768]{1,0:T(8,128)(2,1)} %get-tuple-element.255.refs_0_.refs_5_, bf16[768,768]{1,0:T(8,128)(2,1)} %copy-done.106, ...), custom_call_target="tpu_custom_call" | custom-call | tf_op jit(solution)/shard_map/add_6b/pallas_call | solution.py:369
  348.8 5.1 %collective-permute-done.44.refs_7_.refs_2_ = bf16[192,768]{1,0:T(8,128)(2,1)S(1)} collective-permute-done((bf16[192,768]{1,0:T(8,128)(2,1)}, bf16[192,768]{1,0:T(8,128)(2,1)S(1)}, u32[]{:S(2)}, u32[]{:S(2)}) %collective-permute-start.44) | collective-permute-done | bytes 294944 | tf_op jit(solution)/shard_map/ppermute | solution.py:329
  354.0 4.1 collective-permute-done.46.refs_2_
  366.9 11.9 %collective-permute-done.49.refs_7_ = bf16[384,768]{1,0:T(8,128)(2,1)S(1)} collective-permute-done((bf16[384,768]{1,0:T(8,128)(2,1)}, bf16[384,768]{1,0:T(8,128)(2,1)S(1)}, u32[]{:S(2)}, u32[]{:S(2)}) %collective-permute-start.49) | collective-permute-done | bytes 589856 | tf_op jit(solution)/shard_map/ppermute | solution.py:329
  381.1 5.3 %add_9.1 = (bf16[384,768]{1,0:T(8,128)(2,1)}, bf16[400,768]{1,0:T(8,128)(2,1)}, bf16[416,768]{1,0:T(8,128)(2,1)}, bf16[768,768]{1,0:T(8,128)(2,1)}) custom-call(bf16[1552,768]{1,0:T(8,128)(2,1)} %get-tuple-element.248.refs_3_.refs_0_, bf16[1552,768]{1,0:T(8,128)(2,1)} %copy-done.3, bf16[192,768]{1,0:T(8,128)(2,1)} %copy-done.111, ...), custom_call_target="tpu_custom_call" | custom-call | tf_op jit(solution)/shard_map/add_9/pallas_call | solution.py:369
  392.2 7.2 %collective-permute-start.54 = (bf16[384,768]{1,0:T(8,128)(2,1)S(1)}, bf16[384,768]{1,0:T(8,128)(2,1)S(1)}, u32[]{:S(2)}, u32[]{:S(2)}) collective-permute-start(bf16[384,768]{1,0:T(8,128)(2,1)S(1)} %copy-done.63), channel_id=1, source_target_pairs={{0,8},{24,16},{1,9},{25,17},{2,10},{26,18},{3,11},{27,19},{4,12},{... | collective-permute-start | bytes 1769480 | tf_op jit(solution)/shard_map/ppermute | solution.py:1158
  400.9 8.2 %collective-permute-done.54.refs_6_ = bf16[384,768]{1,0:T(8,128)(2,1)S(1)} collective-permute-done((bf16[384,768]{1,0:T(8,128)(2,1)S(1)}, bf16[384,768]{1,0:T(8,128)(2,1)S(1)}, u32[]{:S(2)}, u32[]{:S(2)}) %collective-permute-start.54) | collective-permute-done | bytes 589856 | tf_op jit(solution)/shard_map/ppermute | solution.py:1158
  427.5 11.7 %collective-permute-done.58.refs_5_ = bf16[400,768]{1,0:T(8,128)(2,1)} collective-permute-done((bf16[400,768]{1,0:T(8,128)(2,1)}, bf16[400,768]{1,0:T(8,128)(2,1)}, u32[]{:S(2)}, u32[]{:S(2)}) %collective-permute-start.58) | collective-permute-done | bytes 614432 | tf_op jit(solution)/shard_map/ppermute | solution.py:1158
  450.2 15.1 %collective-permute-done.62.refs_2_ = bf16[384,768]{1,0:T(8,128)(2,1)S(1)} collective-permute-done((bf16[384,768]{1,0:T(8,128)(2,1)S(1)}, bf16[384,768]{1,0:T(8,128)(2,1)S(1)}, u32[]{:S(2)}, u32[]{:S(2)}) %collective-permute-start.62) | collective-permute-done | bytes 589856 | tf_op jit(solution)/shard_map/ppermute | solution.py:1179
  471.5 7.5 %collective-permute-done.66.refs_2_ = bf16[416,768]{1,0:T(8,128)(2,1)} collective-permute-done((bf16[416,768]{1,0:T(8,128)(2,1)S(1)}, bf16[416,768]{1,0:T(8,128)(2,1)}, u32[]{:S(2)}, u32[]{:S(2)}) %collective-permute-start.66) | collective-permute-done | bytes 639008 | tf_op jit(solution)/shard_map/ppermute | solution.py:1179
  481.8 6.5 %collective-permute-done.65.refs_2_ = bf16[400,768]{1,0:T(8,128)(2,1)} collective-permute-done((bf16[400,768]{1,0:T(8,128)(2,1)}, bf16[400,768]{1,0:T(8,128)(2,1)}, u32[]{:S(2)}, u32[]{:S(2)}) %collective-permute-start.65) | collective-permute-done | bytes 614432 | tf_op jit(solution)/shard_map/ppermute | solution.py:1179
  (404 shorter events, 178.2 us)
Async XLA Ops:
  3.8 30.4 %collective-permute-start.1 = (bf16[784,768]{1,0:T(8,128)(2,1)S(1)}, bf16[784,768]{1,0:T(8,128)(2,1)S(1)}, u32[]{:S(2)}, u32[]{:S(2)}) collective-permute-start(bf16[784,768]{1,0:T(8,128)(2,1)S(1)} %piece_1_pack.1.refs_2_.refs_0_), channel_id=1, source_target_pairs={{0,4},{1,5},{2,6},{3,7},{4,0},{5,1},{6,2},{7,3},{8,12},{9,13},{10,... | collective-permute-start | bytes 3612680 | tf_op jit(solution)/shard_map/ppermute | solution.py:329
  6.9 29.4 %collective-permute-start = (bf16[784,768]{1,0:T(8,128)(2,1)S(1)}, bf16[784,768]{1,0:T(8,128)(2,1)S(1)}, u32[]{:S(2)}, u32[]{:S(2)}) collective-permute-start(bf16[784,768]{1,0:T(8,128)(2,1)S(1)} %piece_1_pack.1.refs_2_.refs_0_), channel_id=1, source_target_pairs={{0,2},{1,3},{2,0},{3,1},{4,6},{5,7},{6,4},{7,5},{8,10},{9,11},{10,... | collective-permute-start | bytes 3612680 | tf_op jit(solution)/shard_map/ppermute | solution.py:329
  8.4 51.0 %collective-permute-start.5 = (bf16[768,768]{1,0:T(8,128)(2,1)S(1)}, bf16[768,768]{1,0:T(8,128)(2,1)S(1)}, u32[]{:S(2)}, u32[]{:S(2)}) collective-permute-start(bf16[768,768]{1,0:T(8,128)(2,1)S(1)} %piece_2_pack.1.refs_2_.refs_0_), channel_id=1, source_target_pairs={{0,4},{1,5},{2,6},{3,7},{4,0},{5,1},{6,2},{7,3},{8,12},{9,13},{10,... | collective-permute-start | bytes 3538952 | tf_op jit(solution)/shard_map/ppermute | solution.py:329
  9.0 52.5 %collective-permute-start.4 = (bf16[768,768]{1,0:T(8,128)(2,1)S(1)}, bf16[768,768]{1,0:T(8,128)(2,1)S(1)}, u32[]{:S(2)}, u32[]{:S(2)}) collective-permute-start(bf16[768,768]{1,0:T(8,128)(2,1)S(1)} %piece_2_pack.1.refs_2_.refs_0_), channel_id=1, source_target_pairs={{0,2},{1,3},{2,0},{3,1},{4,6},{5,7},{6,4},{7,5},{8,10},{9,11},{10,... | collective-permute-start | bytes 3538952 | tf_op jit(solution)/shard_map/ppermute | solution.py:329
  36.4 49.5 %collective-permute-start.3 = (bf16[400,768]{1,0:T(8,128)(2,1)S(1)}, bf16[400,768]{1,0:T(8,128)(2,1)S(1)}, u32[]{:S(2)}, u32[]{:S(2)}) collective-permute-start(bf16[400,768]{1,0:T(8,128)(2,1)S(1)} %get-tuple-element.150), channel_id=1, source_target_pairs={{0,2},{1,3},{2,0},{3,1},{4,6},{5,7},{6,4},{7,5},{8,10},{9,11},{10,... | collective-permute-start | bytes 1843208 | tf_op jit(solution)/shard_map/ppermute | solution.py:329
  37.9 34.2 %collective-permute-start.2 = (bf16[384,768]{1,0:T(8,128)(2,1)S(1)}, bf16[384,768]{1,0:T(8,128)(2,1)S(1)}, u32[]{:S(2)}, u32[]{:S(2)}) collective-permute-start(bf16[384,768]{1,0:T(8,128)(2,1)S(1)} %get-tuple-element.149.refs_2_), channel_id=1, source_target_pairs={{0,4},{1,5},{2,6},{3,7},{4,0},{5,1},{6,2},{7,3},{8,12},{9,13},{10,... | collective-permute-start | bytes 1769480 | tf_op jit(solution)/shard_map/ppermute | solution.py:329
  61.6 24.3 %collective-permute-start.7 = (bf16[384,768]{1,0:T(8,128)(2,1)S(1)}, bf16[384,768]{1,0:T(8,128)(2,1)S(1)}, u32[]{:S(2)}, u32[]{:S(2)}) collective-permute-start(bf16[384,768]{1,0:T(8,128)(2,1)S(1)} %get-tuple-element.152), channel_id=1, source_target_pairs={{0,2},{1,3},{2,0},{3,1},{4,6},{5,7},{6,4},{7,5},{8,10},{9,11},{10,... | collective-permute-start | bytes 1769480 | tf_op jit(solution)/shard_map/ppermute | solution.py:329
  63.2 22.7 %collective-permute-start.6 = (bf16[384,768]{1,0:T(8,128)(2,1)S(1)}, bf16[384,768]{1,0:T(8,128)(2,1)S(1)}, u32[]{:S(2)}, u32[]{:S(2)}) collective-permute-start(bf16[384,768]{1,0:T(8,128)(2,1)S(1)} %get-tuple-element.151.refs_7_), channel_id=1, source_target_pairs={{0,4},{1,5},{2,6},{3,7},{4,0},{5,1},{6,2},{7,3},{8,12},{9,13},{10,... | collective-permute-start | bytes 1769480 | tf_op jit(solution)/shard_map/ppermute | solution.py:329
  92.4 34.7 %collective-permute-start.11 = (bf16[768,768]{1,0:T(8,128)(2,1)S(1)}, bf16[768,768]{1,0:T(8,128)(2,1)S(1)}, u32[]{:S(2)}, u32[]{:S(2)}) collective-permute-start(bf16[768,768]{1,0:T(8,128)(2,1)S(1)} %piece_3_pack.1.refs_3_.refs_0_), channel_id=1, source_target_pairs={{0,4},{1,5},{2,6},{3,7},{4,0},{5,1},{6,2},{7,3},{8,12},{9,13},{10,... | collective-permute-start | bytes 3538952 | tf_op jit(solution)/shard_map/ppermute | solution.py:329
  92.8 34.3 %collective-permute-start.10 = (bf16[768,768]{1,0:T(8,128)(2,1)S(1)}, bf16[768,768]{1,0:T(8,128)(2,1)S(1)}, u32[]{:S(2)}, u32[]{:S(2)}) collective-permute-start(bf16[768,768]{1,0:T(8,128)(2,1)S(1)} %piece_3_pack.1.refs_3_.refs_0_), channel_id=1, source_target_pairs={{0,2},{1,3},{2,0},{3,1},{4,6},{5,7},{6,4},{7,5},{8,10},{9,11},{10,... | collective-permute-start | bytes 3538952 | tf_op jit(solution)/shard_map/ppermute | solution.py:329
  111.0 29.0 %collective-permute-start.15 = (bf16[384,768]{1,0:T(8,128)(2,1)S(1)}, bf16[384,768]{1,0:T(8,128)(2,1)S(1)}, u32[]{:S(2)}, u32[]{:S(2)}) collective-permute-start(bf16[384,768]{1,0:T(8,128)(2,1)S(1)} %piece_4_pack.1.refs_7_.refs_0_), channel_id=1, source_target_pairs={{0,4},{1,5},{2,6},{3,7},{4,0},{5,1},{6,2},{7,3},{8,12},{9,13},{10,... | collective-permute-start | bytes 1769480 | tf_op jit(solution)/shard_map/ppermute | solution.py:329
  111.4 28.7 %collective-permute-start.14 = (bf16[384,768]{1,0:T(8,128)(2,1)S(1)}, bf16[384,768]{1,0:T(8,128)(2,1)S(1)}, u32[]{:S(2)}, u32[]{:S(2)}) collective-permute-start(bf16[384,768]{1,0:T(8,128)(2,1)S(1)} %piece_4_pack.1.refs_7_.refs_0_), channel_id=1, source_target_pairs={{0,2},{1,3},{2,0},{3,1},{4,6},{5,7},{6,4},{7,5},{8,10},{9,11},{10,... | collective-permute-start | bytes 1769480 | tf_op jit(solution)/shard_map/ppermute | solution.py:329
  197.6 28.0 %collective-permute-start.27 = (bf16[768,768]{1,0:T(8,128)(2,1)S(1)}, bf16[768,768]{1,0:T(8,128)(2,1)S(1)}, u32[]{:S(2)}, u32[]{:S(2)}) collective-permute-start(bf16[768,768]{1,0:T(8,128)(2,1)S(1)} %add_1.1.refs_13_), channel_id=1, source_target_pairs={{0,2},{1,3},{2,0},{3,1},{4,6},{5,7},{6,4},{7,5},{8,10},{9,11},{10,... | collective-permute-start | bytes 3538952 | tf_op jit(solution)/shard_map/ppermute | solution.py:329
  213.8 40.9 %collective-permute-start.30 = (bf16[768,768]{1,0:T(8,128)(2,1)}, bf16[768,768]{1,0:T(8,128)(2,1)}, u32[]{:S(2)}, u32[]{:S(2)}) collective-permute-start(bf16[768,768]{1,0:T(8,128)(2,1)} %add_2.1.refs_6_), channel_id=1, source_target_pairs={{0,4},{1,5},{2,6},{3,7},{4,0},{5,1},{6,2},{7,3},{8,12},{9,13},{10,... | collective-permute-start | bytes 3538952 | tf_op jit(solution)/shard_map/ppermute | solution.py:329
  232.7 25.6 %collective-permute-start.29 = (bf16[768,768]{1,0:T(8,128)(2,1)}, bf16[768,768]{1,0:T(8,128)(2,1)S(1)}, u32[]{:S(2)}, u32[]{:S(2)}) collective-permute-start(bf16[768,768]{1,0:T(8,128)(2,1)} %get-tuple-element.235), channel_id=1, source_target_pairs={{0,1},{1,0},{2,3},{3,2},{4,5},{5,4},{6,7},{7,6},{8,9},{9,8},{10,11... | collective-permute-start | bytes 3538952 | tf_op jit(solution)/shard_map/ppermute | solution.py:329
  232.8 25.5 %collective-permute-start.28 = (bf16[768,768]{1,0:T(8,128)(2,1)}, bf16[768,768]{1,0:T(8,128)(2,1)}, u32[]{:S(2)}, u32[]{:S(2)}) collective-permute-start(bf16[768,768]{1,0:T(8,128)(2,1)} %get-tuple-element.234), channel_id=1, source_target_pairs={{0,1},{1,0},{2,3},{3,2},{4,5},{5,4},{6,7},{7,6},{8,9},{9,8},{10,11... | collective-permute-start | bytes 3538952 | tf_op jit(solution)/shard_map/ppermute | solution.py:329
  235.0 40.8 %collective-permute-start.35 = (bf16[768,768]{1,0:T(8,128)(2,1)}, bf16[768,768]{1,0:T(8,128)(2,1)}, u32[]{:S(2)}, u32[]{:S(2)}) collective-permute-start(bf16[768,768]{1,0:T(8,128)(2,1)} %add_3b.1.refs_8_), channel_id=1, source_target_pairs={{0,2},{1,3},{2,0},{3,1},{4,6},{5,7},{6,4},{7,5},{8,10},{9,11},{10,... | collective-permute-start | bytes 3538952 | tf_op jit(solution)/shard_map/ppermute | solution.py:329
  262.2 41.4 %collective-permute-start.36 = (bf16[800,768]{1,0:T(8,128)(2,1)S(1)}, bf16[800,768]{1,0:T(8,128)(2,1)}, u32[]{:S(2)}, u32[]{:S(2)}) collective-permute-start(bf16[800,768]{1,0:T(8,128)(2,1)S(1)} %add_4b.1.refs_15_), channel_id=1, source_target_pairs={{0,4},{1,5},{2,6},{3,7},{4,0},{5,1},{6,2},{7,3},{8,12},{9,13},{10,... | collective-permute-start | bytes 3686408 | tf_op jit(solution)/shard_map/ppermute | solution.py:329
  279.6 28.5 %collective-permute-start.39 = (bf16[800,768]{1,0:T(8,128)(2,1)}, bf16[800,768]{1,0:T(8,128)(2,1)S(1)}, u32[]{:S(2)}, u32[]{:S(2)}) collective-permute-start(bf16[800,768]{1,0:T(8,128)(2,1)} %get-tuple-element.251), channel_id=1, source_target_pairs={{0,1},{1,0},{2,3},{3,2},{4,5},{5,4},{6,7},{7,6},{8,9},{9,8},{10,11... | collective-permute-start | bytes 3686408 | tf_op jit(solution)/shard_map/ppermute | solution.py:329
  279.7 23.9 %collective-permute-start.38 = (bf16[768,768]{1,0:T(8,128)(2,1)}, bf16[768,768]{1,0:T(8,128)(2,1)S(1)}, u32[]{:S(2)}, u32[]{:S(2)}) collective-permute-start(bf16[768,768]{1,0:T(8,128)(2,1)} %get-tuple-element.250), channel_id=1, source_target_pairs={{0,1},{1,0},{2,3},{3,2},{4,5},{5,4},{6,7},{7,6},{8,9},{9,8},{10,11... | collective-permute-start | bytes 3538952 | tf_op jit(solution)/shard_map/ppermute | solution.py:329
  280.2 28.0 %collective-permute-start.37 = (bf16[768,768]{1,0:T(8,128)(2,1)S(1)}, bf16[768,768]{1,0:T(8,128)(2,1)S(1)}, u32[]{:S(2)}, u32[]{:S(2)}) collective-permute-start(bf16[768,768]{1,0:T(8,128)(2,1)S(1)} %add_5b.1.refs_14_), channel_id=1, source_target_pairs={{0,2},{1,3},{2,0},{3,1},{4,6},{5,7},{6,4},{7,5},{8,10},{9,11},{10,... | collective-permute-start | bytes 3538952 | tf_op jit(solution)/shard_map/ppermute | solution.py:329
  281.6 21.9 %collective-permute-start.40 = (bf16[384,768]{1,0:T(8,128)(2,1)}, bf16[384,768]{1,0:T(8,128)(2,1)S(1)}, u32[]{:S(2)}, u32[]{:S(2)}) collective-permute-start(bf16[384,768]{1,0:T(8,128)(2,1)} %add_5a.1.refs_5_), channel_id=1, source_target_pairs={{0,4},{1,5},{2,6},{3,7},{4,0},{5,1},{6,2},{7,3},{8,12},{9,13},{10,... | collective-permute-start | bytes 1769480 | tf_op jit(solution)/shard_map/ppermute | solution.py:329
  314.5 31.3 %collective-permute-start.48 = (bf16[768,768]{1,0:T(8,128)(2,1)}, bf16[768,768]{1,0:T(8,128)(2,1)S(1)}, u32[]{:S(2)}, u32[]{:S(2)}) collective-permute-start(bf16[768,768]{1,0:T(8,128)(2,1)} %get-tuple-element.262.refs_0_), channel_id=1, source_target_pairs={{0,8},{24,16},{1,9},{25,17},{2,10},{26,18},{3,11},{27,19},{4,12},{... | collective-permute-start | bytes 3538952 | tf_op jit(solution)/shard_map/ppermute | solution.py:1158
  347.9 32.1 %collective-permute-start.51 = (bf16[768,768]{1,0:T(8,128)(2,1)S(1)}, bf16[768,768]{1,0:T(8,128)(2,1)S(1)}, u32[]{:S(2)}, u32[]{:S(2)}) collective-permute-start(bf16[768,768]{1,0:T(8,128)(2,1)S(1)} %add_7.1.refs_8_.refs_10_), channel_id=1, source_target_pairs={{8,16},{16,8},{9,17},{17,9},{10,18},{18,10},{11,19},{19,11},{12,20... | collective-permute-start | bytes 3538952 | tf_op jit(solution)/shard_map/ppermute | solution.py:1172
  362.3 26.0 %collective-permute-start.55 = (bf16[768,768]{1,0:T(8,128)(2,1)S(1)}, bf16[768,768]{1,0:T(8,128)(2,1)S(1)}, u32[]{:S(2)}, u32[]{:S(2)}) collective-permute-start(bf16[768,768]{1,0:T(8,128)(2,1)S(1)} %copy-done.54), channel_id=1, source_target_pairs={{0,8},{24,16},{1,9},{25,17},{2,10},{26,18},{3,11},{27,19},{4,12},{... | collective-permute-start | bytes 3538952 | tf_op jit(solution)/shard_map/ppermute | solution.py:1158
  386.4 33.9 %collective-permute-start.59 = (bf16[768,768]{1,0:T(8,128)(2,1)}, bf16[768,768]{1,0:T(8,128)(2,1)S(1)}, u32[]{:S(2)}, u32[]{:S(2)}) collective-permute-start(bf16[768,768]{1,0:T(8,128)(2,1)} %get-tuple-element.277.refs_1_), channel_id=1, source_target_pairs={{8,0},{16,24},{9,1},{17,25},{10,2},{18,26},{11,3},{19,27},{12,4},{... | collective-permute-start | bytes 3538952 | tf_op jit(solution)/shard_map/ppermute | solution.py:1179
  390.4 29.9 %collective-permute-start.60 = (bf16[768,768]{1,0:T(8,128)(2,1)S(1)}, bf16[768,768]{1,0:T(8,128)(2,1)S(1)}, u32[]{:S(2)}, u32[]{:S(2)}) collective-permute-start(bf16[768,768]{1,0:T(8,128)(2,1)S(1)} %add_10.1.refs_7_.refs_0_), channel_id=1, source_target_pairs={{8,16},{16,8},{9,17},{17,9},{10,18},{18,10},{11,19},{19,11},{12,20... | collective-permute-start | bytes 3538952 | tf_op jit(solution)/shard_map/ppermute | solution.py:1172
  413.8 25.4 %collective-permute-start.57 = (bf16[416,768]{1,0:T(8,128)(2,1)}, bf16[416,768]{1,0:T(8,128)(2,1)}, u32[]{:S(2)}, u32[]{:S(2)}) collective-permute-start(bf16[416,768]{1,0:T(8,128)(2,1)} %get-tuple-element.275.refs_2_), channel_id=1, source_target_pairs={{0,8},{24,16},{1,9},{25,17},{2,10},{26,18},{3,11},{27,19},{4,12},{... | collective-permute-start | bytes 1916936 | tf_op jit(solution)/shard_map/ppermute | solution.py:1158
  416.7 22.5 %collective-permute-start.58 = (bf16[400,768]{1,0:T(8,128)(2,1)}, bf16[400,768]{1,0:T(8,128)(2,1)}, u32[]{:S(2)}, u32[]{:S(2)}) collective-permute-start(bf16[400,768]{1,0:T(8,128)(2,1)} %get-tuple-element.276.refs_4_), channel_id=1, source_target_pairs={{0,8},{24,16},{1,9},{25,17},{2,10},{26,18},{3,11},{27,19},{4,12},{... | collective-permute-start | bytes 1843208 | tf_op jit(solution)/shard_map/ppermute | solution.py:1158
  421.4 25.5 %collective-permute-start.63 = (bf16[768,768]{1,0:T(8,128)(2,1)S(1)}, bf16[768,768]{1,0:T(8,128)(2,1)S(1)}, u32[]{:S(2)}, u32[]{:S(2)}) collective-permute-start(bf16[768,768]{1,0:T(8,128)(2,1)S(1)} %add_12.1.refs_3_.refs_1_), channel_id=1, source_target_pairs={{8,0},{16,24},{9,1},{17,25},{10,2},{18,26},{11,3},{19,27},{12,4},{... | collective-permute-start | bytes 3538952 | tf_op jit(solution)/shard_map/ppermute | solution.py:1179
  443.6 24.1 %collective-permute-start.61 = (bf16[400,768]{1,0:T(8,128)(2,1)S(1)}, bf16[400,768]{1,0:T(8,128)(2,1)S(1)}, u32[]{:S(2)}, u32[]{:S(2)}) collective-permute-start(bf16[400,768]{1,0:T(8,128)(2,1)S(1)} %get-tuple-element.279.refs_0_), channel_id=1, source_target_pairs={{8,16},{16,8},{9,17},{17,9},{10,18},{18,10},{11,19},{19,11},{12,20... | collective-permute-start | bytes 1843208 | tf_op jit(solution)/shard_map/ppermute | solution.py:1172
  447.7 31.3 %collective-permute-start.66 = (bf16[416,768]{1,0:T(8,128)(2,1)S(1)}, bf16[416,768]{1,0:T(8,128)(2,1)}, u32[]{:S(2)}, u32[]{:S(2)}) collective-permute-start(bf16[416,768]{1,0:T(8,128)(2,1)S(1)} %add_14.1.refs_3_.refs_1_), channel_id=1, source_target_pairs={{8,0},{16,24},{9,1},{17,25},{10,2},{18,26},{11,3},{19,27},{12,4},{... | collective-permute-start | bytes 1916936 | tf_op jit(solution)/shard_map/ppermute | solution.py:1179
  (156 other events, 1078.0 us)

commit v6 on v5

--- a/solution.py
+++ b/solution.py
@@ -1350,10 +1350,9 @@
     line_a = Line(totals["a"])
     red_6.cores()
     red_6.cores_done()
-    combine(
-        order, "add_6b", red_5.first(), red_6.first(), own_stack([red_2, red_3], keep_as("b")),
-        red_4.own(keep_as(4)),
-    )
+    mark(*red_3.last, *red_4.last)
+    combine(order, "add_6b", red_5.first(), red_6.first())
+    combine(order, "add_6c", own_stack([red_2, red_3], keep_as("b")), red_4.own(keep_as(4)))
     combine(order, "add_7", line_a.middle())
     mark(*red_6.landed)
     combine(order, "add_8", red_5.second())

time: 499 us -> 494 us (0.990)
    unnamed x242 -> x238, local copies, waits for them, and re-layouts: 38.4 us -> 37.1 us
    pallas_call x50 -> x51, Pallas kernels: 178 us -> 179 us  [kernel(): pl.pallas_call(lambda *refs: body(*refs[:count], *refs[count + skip:]), o...]
where the time goes in v6:
time: 494 us; the launch traced here: 488 us
  waiting for transfers between devices  191 us (39%)
  Pallas kernels  179 us (36%)
  starting transfers between devices  73.2 us (15%)
  local copies, waits for them, and re-layouts  40.8 us (8%)
    pallas_call x51, Pallas kernels, kernel(): pl.pallas_call(lambda *refs: body(*refs[:count], *refs[count + skip:]), o...  179 us
    ppermute x52, waiting for transfers between devices, swap(): return lax.ppermute(value, 'fsdp', [(i, i ^ bit) for i in range(8)])  140 us
    ppermute x52, starting transfers between devices, swap(): return lax.ppermute(value, 'fsdp', [(i, i ^ bit) for i in range(8)])  44.4 us
    unnamed x238, local copies, waits for them, and re-layouts  37.1 us
    ppermute x5, waiting for transfers between devices, outward_sent(): self.landed = lax.ppermute(value, 'rep', [(1, 0), (2, 3)])  30.4 us
    ppermute x5, waiting for transfers between devices, __init__(): self.landed = lax.ppermute(value, 'rep', [(0, 1), (3, 2)])  20.4 us
    ppermute x5, starting transfers between devices, __init__(): self.landed = lax.ppermute(value, 'rep', [(0, 1), (3, 2)])  17.9 us
  transfers between devices with their start and end apart: 67, of which 29 were waited for; matrix products, arithmetic and copies ran while one was open for 0% of the time, Pallas kernels for 31%

profile of v6, /device:TPU:0, one launch (start us, length us, event | category | flops | bytes accessed | tf_op | source)
XLA Modules:
  0.0 487.6 jit_solution(17182438713991918754)
XLA Ops:
  9.6 24.6 %collective-permute-done.1.refs_1_.refs_2_ = bf16[784,768]{1,0:T(8,128)(2,1)S(1)} collective-permute-done((bf16[784,768]{1,0:T(8,128)(2,1)S(1)}, bf16[784,768]{1,0:T(8,128)(2,1)S(1)}, u32[]{:S(2)}, u32[]{:S(2)}) %collective-permute-start.1) | collective-permute-done | bytes 1204256 | tf_op jit(solution)/shard_map/ppermute | solution.py:329
  38.4 21.0 %collective-permute-done.5.refs_1_.refs_2_ = bf16[768,768]{1,0:T(8,128)(2,1)S(1)} collective-permute-done((bf16[768,768]{1,0:T(8,128)(2,1)S(1)}, bf16[768,768]{1,0:T(8,128)(2,1)S(1)}, u32[]{:S(2)}, u32[]{:S(2)}) %collective-permute-start.5) | collective-permute-done | bytes 1179680 | tf_op jit(solution)/shard_map/ppermute | solution.py:329
  63.7 8.4 %collective-permute-done.2.refs_3_ = bf16[384,768]{1,0:T(8,128)(2,1)S(1)} collective-permute-done((bf16[384,768]{1,0:T(8,128)(2,1)S(1)}, bf16[384,768]{1,0:T(8,128)(2,1)S(1)}, u32[]{:S(2)}, u32[]{:S(2)}) %collective-permute-start.2) | collective-permute-done | bytes 589856 | tf_op jit(solution)/shard_map/ppermute | solution.py:329
  72.1 13.8 %collective-permute-done.7.refs_6_.refs_4_ = bf16[384,768]{1,0:T(8,128)(2,1)S(1)} collective-permute-done((bf16[384,768]{1,0:T(8,128)(2,1)S(1)}, bf16[384,768]{1,0:T(8,128)(2,1)S(1)}, u32[]{:S(2)}, u32[]{:S(2)}) %collective-permute-start.7) | collective-permute-done | bytes 589856 | tf_op jit(solution)/shard_map/ppermute | solution.py:329
  99.7 8.6 %enc_attn.1 = (f32[256,768]{1,0:T(8,128)S(1)}, bf16[256,768]{1,0:T(8,128)(2,1)S(1)}, bf16[256,768]{1,0:T(8,128)(2,1)S(1)}, bf16[256,768]{1,0:T(8,128)(2,1)S(1)},...) custom-call(s32[8]{0:T(128)S(1)} %iota_xor_fusion.refs_0_, ...), custom_call_target="tpu_custom_call" | custom-call | flops 1207959552 | bytes 5898240 | tf_op jit(solution)/shard_map/enc_attn/pallas_call | solution.py:369
  113.0 9.0 %dec_self.1 = (f32[256,768]{1,0:T(8,128)S(1)}, bf16[256,768]{1,0:T(8,128)(2,1)S(1)}, bf16[256,768]{1,0:T(8,128)(2,1)S(1)}, bf16[256,768]{1,0:T(8,128)(2,1)S(1)},...) custom-call(s32[8]{0:T(128)S(1)} %iota_xor_fusion.refs_0_, ...), custom_call_target="tpu_custom_call" | custom-call | flops 1207959552 | bytes 5898240 | tf_op jit(solution)/shard_map/dec_self/pallas_call | solution.py:369
  130.7 9.3 %enc_feed.1 = (f32[256,768]{1,0:T(8,128)}, bf16[256,768]{1,0:T(8,128)(2,1)}, bf16[256,3072]{1,0:T(8,128)(2,1)}, bf16[256,3072]{1,0:T(8,128)(2,1)}) custom-call(s32[8]{0:T(128)} %copy-done.89, bf16[256,768]{1,0:T(8,128)(2,1)} %copy-done.52, f32[3,768]{1,0:T(4,128)} %copy-done.84, f32[1,3072]{1,0:T(1,128)} %copy-done.99, bf16[3072,768]{1,0:T(8,128)(2,1)} %copy-done.1, ...), custom_call_target="tpu_custom_call" | custom-call | flops 2415919104 | bytes 18874368 | tf_op jit(solution)/shard_map/enc_feed/pallas_call | solution.py:369
  158.1 8.5 %dec_cross.1 = (f32[256,768]{1,0:T(8,128)}, bf16[256,768]{1,0:T(8,128)(2,1)}, bf16[256,768]{1,0:T(8,128)(2,1)}, bf16[256,768]{1,0:T(8,128)(2,1)}, bf16[256,768]{...) custom-call(s32[8]{0:T(128)} %copy-done.89, s32[1]{0:T(128)S(6)} %copy.28.refs_1_, ...), custom_call_target="tpu_custom_call" | custom-call | flops 1207959552 | bytes 5898240 | tf_op jit(solution)/shard_map/dec_cross/pallas_call | solution.py:369
  166.6 9.3 %dec_feed.1 = (f32[256,768]{1,0:T(8,128)}, bf16[256,768]{1,0:T(8,128)(2,1)}, bf16[256,3072]{1,0:T(8,128)(2,1)}, bf16[256,3072]{1,0:T(8,128)(2,1)}) custom-call(s32[8]{0:T(128)} %copy-done.89, bf16[256,768]{1,0:T(8,128)(2,1)} %get-tuple-element.169.refs_1_.refs_3_, f32[3,768]{1,0:T(4,128)} %copy-done.97, f32[1,3072]{1,0:T(1,128)} %copy-done.98, ...), custom_call_target="tpu_custom_call" | custom-call | flops 2415919104 | bytes 18874368 | tf_op jit(solution)/shard_map/dec_feed/pallas_call | solution.py:369
  175.9 6.9 %dec_back_out.1 = (f32[256,768]{1,0:T(8,128)}, f32[3,768]{1,0:T(4,128)}, bf16[1536,768]{1,0:T(8,128)(2,1)}, bf16[768,768]{1,0:T(8,128)(2,1)}, bf16[768,768]{1,0:T(8,128)(2,1)}) custom-call(s32[8]{0:T(128)} %copy-done.89, bf16[256,768]{1,0:T(8,128)(2,1)} %refs_1_.9, f32[256,768]{1,0:T(8,128)} %get-tuple-element.175.refs_2_.refs_5_, f32[3,768]{1,0:T(4,128)} %copy-done.97, ...), custom_call_target="tpu_custom_call" | custom-call | flops 1207959552 | bytes 9437184 | tf_op jit(solution)/shard_map/dec_back_out/pallas_call | solution.py:369
  183.4 11.6 %dec_back_in.1 = (f32[256,768]{1,0:T(8,128)}, f32[4,768]{1,0:T(4,128)}, bf16[1536,768]{1,0:T(8,128)(2,1)}, bf16[768,768]{1,0:T(8,128)(2,1)}, bf16[768,768]{1,0:T(8,128)(2,1)}) custom-call(s32[8]{0:T(128)} %copy-done.89, f32[256,768]{1,0:T(8,128)} %get-tuple-element.177.refs_1_, bf16[256,3072]{1,0:T(8,128)(2,1)} %get-tuple-element.178.refs_2_, ...), custom_call_target="tpu_custom_call" | custom-call | flops 3623878656 | bytes 14155776 | tf_op jit(solution)/shard_map/dec_back_in/pallas_call | solution.py:369
  199.3 11.7 %cross_back.1 = (f32[256,768]{1,0:T(8,128)S(1)}, f32[256,768]{1,0:T(8,128)S(1)}, f32[5,768]{1,0:T(8,128)S(1)}, bf16[1536,768]{1,0:T(8,128)(2,1)}, bf16[768,768]{1,0:T(8,128)(2,1)}, /*index=5*/bf16[768,768]{1,0:T(8,128)(2,1)}) custom-call(s32[8]{0:T(128)S(1)} %copy-done.90, f32[256,768]{1,0:T(8,128)S(1)} %copy-done.58, f32[256,768]{1,0:T(8,128)S(1)} %copy-done.34, ...), custom_call_target="tpu_custom_call" | custom-call | flops 2415919104 | bytes 11796480 | tf_op jit(solution)/shard_map/cross_back/pallas_call | solution.py:369
  215.4 4.0 enc_back_out.1
  220.2 5.3 %collective-permute-done.27.refs_2_.refs_9_ = bf16[768,768]{1,0:T(8,128)(2,1)S(1)} collective-permute-done((bf16[768,768]{1,0:T(8,128)(2,1)S(1)}, bf16[768,768]{1,0:T(8,128)(2,1)S(1)}, u32[]{:S(2)}, u32[]{:S(2)}) %collective-permute-start.27) | collective-permute-done | bytes 1179680 | tf_op jit(solution)/shard_map/ppermute | solution.py:329
  236.2 11.2 %enc_back_in.1 = (f32[256,768]{1,0:T(8,128)}, f32[4,768]{1,0:T(4,128)}, bf16[1536,768]{1,0:T(8,128)(2,1)}, bf16[768,768]{1,0:T(8,128)(2,1)}, bf16[768,768]{1,0:T(8,128)(2,1)}) custom-call(s32[8]{0:T(128)} %copy-done.89, f32[256,768]{1,0:T(8,128)} %copy-done.57, bf16[256,3072]{1,0:T(8,128)(2,1)} %get-tuple-element.209.refs_2_, bf16[256,768]{1,0:T(8,128)(2,1)} %copy-done.52, ...), custom_call_target="tpu_custom_call" | custom-call | flops 3623878656 | bytes 14155776 | tf_op jit(solution)/shard_map/enc_back_in/pallas_call | solution.py:369
  247.4 7.3 %collective-permute-done.31.refs_3_.refs_8_ = bf16[384,768]{1,0:T(8,128)(2,1)} collective-permute-done((bf16[384,768]{1,0:T(8,128)(2,1)}, bf16[384,768]{1,0:T(8,128)(2,1)}, u32[]{:S(2)}, u32[]{:S(2)}) %collective-permute-start.31) | collective-permute-done | bytes 589856 | tf_op jit(solution)/shard_map/ppermute | solution.py:329
  262.1 11.9 %self_back.1 = (f32[256,768]{1,0:T(8,128)}, f32[5,768]{1,0:T(8,128)S(1)}, bf16[1568,768]{1,0:T(8,128)(2,1)}, bf16[768,768]{1,0:T(8,128)(2,1)}, bf16[800,768]{1,0:T(8,128)(2,1)}) custom-call(s32[8]{0:T(128)S(1)} %copy-done.91, f32[256,768]{1,0:T(8,128)S(1)} %copy-done.56, f32[5,768]{1,0:T(8,128)S(1)} %get-tuple-element.205.refs_4_.refs_2_, ...), custom_call_target="tpu_custom_call" | custom-call | flops 2415919104 | bytes 11796480 | tf_op jit(solution)/shard_map/self_back/pallas_call | solution.py:369
  280.5 13.2 %enc_attn_back.1 = (f32[256,768]{1,0:T(8,128)}, f32[5,768]{1,0:T(8,128)}, bf16[1552,768]{1,0:T(8,128)(2,1)}, bf16[1552,768]{1,0:T(8,128)(2,1)}) custom-call(s32[8]{0:T(128)} %copy-done.89, f32[256,768]{1,0:T(8,128)} %get-tuple-element.218.refs_1_, f32[3,768]{1,0:T(4,128)} %copy-done.92, f32[4,768]{1,0:T(4,128)} %get-tuple-element.219.refs_4_.refs_3_, ...), custom_call_target="tpu_custom_call" | custom-call | flops 2415919104 | bytes 11796480 | tf_op jit(solution)/shard_map/enc_attn_back/pallas_call | solution.py:369
  293.7 8.2 %collective-permute-done.40.refs_16_.refs_2_ = bf16[384,768]{1,0:T(8,128)(2,1)S(1)} collective-permute-done((bf16[384,768]{1,0:T(8,128)(2,1)}, bf16[384,768]{1,0:T(8,128)(2,1)S(1)}, u32[]{:S(2)}, u32[]{:S(2)}) %collective-permute-start.40) | collective-permute-done | bytes 589856 | tf_op jit(solution)/shard_map/ppermute | solution.py:329
  301.9 4.6 collective-permute-done.37.refs_5_.refs_11_
  307.9 4.9 add_6a.1
  318.7 13.7 %collective-permute-done.43.refs_7_.refs_10_ = bf16[384,768]{1,0:T(8,128)(2,1)S(1)} collective-permute-done((bf16[384,768]{1,0:T(8,128)(2,1)}, bf16[384,768]{1,0:T(8,128)(2,1)S(1)}, u32[]{:S(2)}, u32[]{:S(2)}) %collective-permute-start.43) | collective-permute-done | bytes 589856 | tf_op jit(solution)/shard_map/ppermute | solution.py:329
  341.0 4.3 add_6c.1
  349.1 4.1 collective-permute-done.46.refs_2_
  362.1 11.9 %collective-permute-done.49.refs_7_ = bf16[384,768]{1,0:T(8,128)(2,1)S(1)} collective-permute-done((bf16[384,768]{1,0:T(8,128)(2,1)}, bf16[384,768]{1,0:T(8,128)(2,1)S(1)}, u32[]{:S(2)}, u32[]{:S(2)}) %collective-permute-start.49) | collective-permute-done | bytes 589856 | tf_op jit(solution)/shard_map/ppermute | solution.py:329
  376.4 5.3 %add_9.1 = (bf16[384,768]{1,0:T(8,128)(2,1)}, bf16[400,768]{1,0:T(8,128)(2,1)}, bf16[416,768]{1,0:T(8,128)(2,1)}, bf16[768,768]{1,0:T(8,128)(2,1)}) custom-call(bf16[1552,768]{1,0:T(8,128)(2,1)} %get-tuple-element.248.refs_3_.refs_0_, bf16[1552,768]{1,0:T(8,128)(2,1)} %copy-done.3, bf16[192,768]{1,0:T(8,128)(2,1)} %copy-done.110, ...), custom_call_target="tpu_custom_call" | custom-call | tf_op jit(solution)/shard_map/add_9/pallas_call | solution.py:369
  387.3 7.2 %collective-permute-start.54 = (bf16[384,768]{1,0:T(8,128)(2,1)S(1)}, bf16[384,768]{1,0:T(8,128)(2,1)S(1)}, u32[]{:S(2)}, u32[]{:S(2)}) collective-permute-start(bf16[384,768]{1,0:T(8,128)(2,1)S(1)} %copy-done.39), channel_id=1, source_target_pairs={{0,8},{24,16},{1,9},{25,17},{2,10},{26,18},{3,11},{27,19},{4,12},{... | collective-permute-start | bytes 1769480 | tf_op jit(solution)/shard_map/ppermute | solution.py:1158
  396.1 8.1 %collective-permute-done.54.refs_6_ = bf16[384,768]{1,0:T(8,128)(2,1)S(1)} collective-permute-done((bf16[384,768]{1,0:T(8,128)(2,1)S(1)}, bf16[384,768]{1,0:T(8,128)(2,1)S(1)}, u32[]{:S(2)}, u32[]{:S(2)}) %collective-permute-start.54) | collective-permute-done | bytes 589856 | tf_op jit(solution)/shard_map/ppermute | solution.py:1158
  422.7 11.7 %collective-permute-done.58.refs_5_ = bf16[400,768]{1,0:T(8,128)(2,1)} collective-permute-done((bf16[400,768]{1,0:T(8,128)(2,1)}, bf16[400,768]{1,0:T(8,128)(2,1)}, u32[]{:S(2)}, u32[]{:S(2)}) %collective-permute-start.58) | collective-permute-done | bytes 614432 | tf_op jit(solution)/shard_map/ppermute | solution.py:1158
  445.3 15.0 %collective-permute-done.62.refs_2_ = bf16[384,768]{1,0:T(8,128)(2,1)S(1)} collective-permute-done((bf16[384,768]{1,0:T(8,128)(2,1)S(1)}, bf16[384,768]{1,0:T(8,128)(2,1)S(1)}, u32[]{:S(2)}, u32[]{:S(2)}) %collective-permute-start.62) | collective-permute-done | bytes 589856 | tf_op jit(solution)/shard_map/ppermute | solution.py:1179
  466.7 7.5 %collective-permute-done.66.refs_2_ = bf16[416,768]{1,0:T(8,128)(2,1)} collective-permute-done((bf16[416,768]{1,0:T(8,128)(2,1)S(1)}, bf16[416,768]{1,0:T(8,128)(2,1)}, u32[]{:S(2)}, u32[]{:S(2)}) %collective-permute-start.66) | collective-permute-done | bytes 639008 | tf_op jit(solution)/shard_map/ppermute | solution.py:1179
  476.9 6.5 %collective-permute-done.65.refs_2_ = bf16[400,768]{1,0:T(8,128)(2,1)} collective-permute-done((bf16[400,768]{1,0:T(8,128)(2,1)}, bf16[400,768]{1,0:T(8,128)(2,1)}, u32[]{:S(2)}, u32[]{:S(2)}) %collective-permute-start.65) | collective-permute-done | bytes 614432 | tf_op jit(solution)/shard_map/ppermute | solution.py:1179
  (401 shorter events, 175.7 us)
Async XLA Ops:
  3.8 30.4 %collective-permute-start.1 = (bf16[784,768]{1,0:T(8,128)(2,1)S(1)}, bf16[784,768]{1,0:T(8,128)(2,1)S(1)}, u32[]{:S(2)}, u32[]{:S(2)}) collective-permute-start(bf16[784,768]{1,0:T(8,128)(2,1)S(1)} %piece_1_pack.1.refs_2_.refs_0_), channel_id=1, source_target_pairs={{0,4},{1,5},{2,6},{3,7},{4,0},{5,1},{6,2},{7,3},{8,12},{9,13},{10,... | collective-permute-start | bytes 3612680 | tf_op jit(solution)/shard_map/ppermute | solution.py:329
  6.9 29.4 %collective-permute-start = (bf16[784,768]{1,0:T(8,128)(2,1)S(1)}, bf16[784,768]{1,0:T(8,128)(2,1)S(1)}, u32[]{:S(2)}, u32[]{:S(2)}) collective-permute-start(bf16[784,768]{1,0:T(8,128)(2,1)S(1)} %piece_1_pack.1.refs_2_.refs_0_), channel_id=1, source_target_pairs={{0,2},{1,3},{2,0},{3,1},{4,6},{5,7},{6,4},{7,5},{8,10},{9,11},{10,... | collective-permute-start | bytes 3612680 | tf_op jit(solution)/shard_map/ppermute | solution.py:329
  8.4 51.0 %collective-permute-start.5 = (bf16[768,768]{1,0:T(8,128)(2,1)S(1)}, bf16[768,768]{1,0:T(8,128)(2,1)S(1)}, u32[]{:S(2)}, u32[]{:S(2)}) collective-permute-start(bf16[768,768]{1,0:T(8,128)(2,1)S(1)} %piece_2_pack.1.refs_2_.refs_0_), channel_id=1, source_target_pairs={{0,4},{1,5},{2,6},{3,7},{4,0},{5,1},{6,2},{7,3},{8,12},{9,13},{10,... | collective-permute-start | bytes 3538952 | tf_op jit(solution)/shard_map/ppermute | solution.py:329
  9.0 52.5 %collective-permute-start.4 = (bf16[768,768]{1,0:T(8,128)(2,1)S(1)}, bf16[768,768]{1,0:T(8,128)(2,1)S(1)}, u32[]{:S(2)}, u32[]{:S(2)}) collective-permute-start(bf16[768,768]{1,0:T(8,128)(2,1)S(1)} %piece_2_pack.1.refs_2_.refs_0_), channel_id=1, source_target_pairs={{0,2},{1,3},{2,0},{3,1},{4,6},{5,7},{6,4},{7,5},{8,10},{9,11},{10,... | collective-permute-start | bytes 3538952 | tf_op jit(solution)/shard_map/ppermute | solution.py:329
  36.4 49.5 %collective-permute-start.3 = (bf16[400,768]{1,0:T(8,128)(2,1)S(1)}, bf16[400,768]{1,0:T(8,128)(2,1)S(1)}, u32[]{:S(2)}, u32[]{:S(2)}) collective-permute-start(bf16[400,768]{1,0:T(8,128)(2,1)S(1)} %get-tuple-element.150), channel_id=1, source_target_pairs={{0,2},{1,3},{2,0},{3,1},{4,6},{5,7},{6,4},{7,5},{8,10},{9,11},{10,... | collective-permute-start | bytes 1843208 | tf_op jit(solution)/shard_map/ppermute | solution.py:329
  37.9 34.2 %collective-permute-start.2 = (bf16[384,768]{1,0:T(8,128)(2,1)S(1)}, bf16[384,768]{1,0:T(8,128)(2,1)S(1)}, u32[]{:S(2)}, u32[]{:S(2)}) collective-permute-start(bf16[384,768]{1,0:T(8,128)(2,1)S(1)} %get-tuple-element.149.refs_2_), channel_id=1, source_target_pairs={{0,4},{1,5},{2,6},{3,7},{4,0},{5,1},{6,2},{7,3},{8,12},{9,13},{10,... | collective-permute-start | bytes 1769480 | tf_op jit(solution)/shard_map/ppermute | solution.py:329
  61.6 24.3 %collective-permute-start.7 = (bf16[384,768]{1,0:T(8,128)(2,1)S(1)}, bf16[384,768]{1,0:T(8,128)(2,1)S(1)}, u32[]{:S(2)}, u32[]{:S(2)}) collective-permute-start(bf16[384,768]{1,0:T(8,128)(2,1)S(1)} %get-tuple-element.152), channel_id=1, source_target_pairs={{0,2},{1,3},{2,0},{3,1},{4,6},{5,7},{6,4},{7,5},{8,10},{9,11},{10,... | collective-permute-start | bytes 1769480 | tf_op jit(solution)/shard_map/ppermute | solution.py:329
  63.2 22.7 %collective-permute-start.6 = (bf16[384,768]{1,0:T(8,128)(2,1)S(1)}, bf16[384,768]{1,0:T(8,128)(2,1)S(1)}, u32[]{:S(2)}, u32[]{:S(2)}) collective-permute-start(bf16[384,768]{1,0:T(8,128)(2,1)S(1)} %get-tuple-element.151.refs_7_), channel_id=1, source_target_pairs={{0,4},{1,5},{2,6},{3,7},{4,0},{5,1},{6,2},{7,3},{8,12},{9,13},{10,... | collective-permute-start | bytes 1769480 | tf_op jit(solution)/shard_map/ppermute | solution.py:329
  92.4 34.6 %collective-permute-start.11 = (bf16[768,768]{1,0:T(8,128)(2,1)S(1)}, bf16[768,768]{1,0:T(8,128)(2,1)S(1)}, u32[]{:S(2)}, u32[]{:S(2)}) collective-permute-start(bf16[768,768]{1,0:T(8,128)(2,1)S(1)} %piece_3_pack.1.refs_3_.refs_0_), channel_id=1, source_target_pairs={{0,4},{1,5},{2,6},{3,7},{4,0},{5,1},{6,2},{7,3},{8,12},{9,13},{10,... | collective-permute-start | bytes 3538952 | tf_op jit(solution)/shard_map/ppermute | solution.py:329
  92.8 34.3 %collective-permute-start.10 = (bf16[768,768]{1,0:T(8,128)(2,1)S(1)}, bf16[768,768]{1,0:T(8,128)(2,1)S(1)}, u32[]{:S(2)}, u32[]{:S(2)}) collective-permute-start(bf16[768,768]{1,0:T(8,128)(2,1)S(1)} %piece_3_pack.1.refs_3_.refs_0_), channel_id=1, source_target_pairs={{0,2},{1,3},{2,0},{3,1},{4,6},{5,7},{6,4},{7,5},{8,10},{9,11},{10,... | collective-permute-start | bytes 3538952 | tf_op jit(solution)/shard_map/ppermute | solution.py:329
  111.0 29.0 %collective-permute-start.15 = (bf16[384,768]{1,0:T(8,128)(2,1)S(1)}, bf16[384,768]{1,0:T(8,128)(2,1)S(1)}, u32[]{:S(2)}, u32[]{:S(2)}) collective-permute-start(bf16[384,768]{1,0:T(8,128)(2,1)S(1)} %piece_4_pack.1.refs_7_.refs_0_), channel_id=1, source_target_pairs={{0,4},{1,5},{2,6},{3,7},{4,0},{5,1},{6,2},{7,3},{8,12},{9,13},{10,... | collective-permute-start | bytes 1769480 | tf_op jit(solution)/shard_map/ppermute | solution.py:329
  111.3 28.7 %collective-permute-start.14 = (bf16[384,768]{1,0:T(8,128)(2,1)S(1)}, bf16[384,768]{1,0:T(8,128)(2,1)S(1)}, u32[]{:S(2)}, u32[]{:S(2)}) collective-permute-start(bf16[384,768]{1,0:T(8,128)(2,1)S(1)} %piece_4_pack.1.refs_7_.refs_0_), channel_id=1, source_target_pairs={{0,2},{1,3},{2,0},{3,1},{4,6},{5,7},{6,4},{7,5},{8,10},{9,11},{10,... | collective-permute-start | bytes 1769480 | tf_op jit(solution)/shard_map/ppermute | solution.py:329
  197.6 28.0 %collective-permute-start.27 = (bf16[768,768]{1,0:T(8,128)(2,1)S(1)}, bf16[768,768]{1,0:T(8,128)(2,1)S(1)}, u32[]{:S(2)}, u32[]{:S(2)}) collective-permute-start(bf16[768,768]{1,0:T(8,128)(2,1)S(1)} %add_1.1.refs_13_), channel_id=1, source_target_pairs={{0,2},{1,3},{2,0},{3,1},{4,6},{5,7},{6,4},{7,5},{8,10},{9,11},{10,... | collective-permute-start | bytes 3538952 | tf_op jit(solution)/shard_map/ppermute | solution.py:329
  213.8 40.9 %collective-permute-start.30 = (bf16[768,768]{1,0:T(8,128)(2,1)}, bf16[768,768]{1,0:T(8,128)(2,1)}, u32[]{:S(2)}, u32[]{:S(2)}) collective-permute-start(bf16[768,768]{1,0:T(8,128)(2,1)} %add_2.1.refs_6_), channel_id=1, source_target_pairs={{0,4},{1,5},{2,6},{3,7},{4,0},{5,1},{6,2},{7,3},{8,12},{9,13},{10,... | collective-permute-start | bytes 3538952 | tf_op jit(solution)/shard_map/ppermute | solution.py:329
  232.4 24.6 %collective-permute-start.29 = (bf16[768,768]{1,0:T(8,128)(2,1)}, bf16[768,768]{1,0:T(8,128)(2,1)}, u32[]{:S(2)}, u32[]{:S(2)}) collective-permute-start(bf16[768,768]{1,0:T(8,128)(2,1)} %get-tuple-element.235), channel_id=1, source_target_pairs={{0,1},{1,0},{2,3},{3,2},{4,5},{5,4},{6,7},{7,6},{8,9},{9,8},{10,11... | collective-permute-start | bytes 3538952 | tf_op jit(solution)/shard_map/ppermute | solution.py:329
  232.5 24.5 %collective-permute-start.28 = (bf16[768,768]{1,0:T(8,128)(2,1)}, bf16[768,768]{1,0:T(8,128)(2,1)}, u32[]{:S(2)}, u32[]{:S(2)}) collective-permute-start(bf16[768,768]{1,0:T(8,128)(2,1)} %get-tuple-element.234), channel_id=1, source_target_pairs={{0,1},{1,0},{2,3},{3,2},{4,5},{5,4},{6,7},{7,6},{8,9},{9,8},{10,11... | collective-permute-start | bytes 3538952 | tf_op jit(solution)/shard_map/ppermute | solution.py:329
  234.7 39.4 %collective-permute-start.35 = (bf16[768,768]{1,0:T(8,128)(2,1)}, bf16[768,768]{1,0:T(8,128)(2,1)}, u32[]{:S(2)}, u32[]{:S(2)}) collective-permute-start(bf16[768,768]{1,0:T(8,128)(2,1)} %add_3b.1.refs_8_), channel_id=1, source_target_pairs={{0,2},{1,3},{2,0},{3,1},{4,6},{5,7},{6,4},{7,5},{8,10},{9,11},{10,... | collective-permute-start | bytes 3538952 | tf_op jit(solution)/shard_map/ppermute | solution.py:329
  260.5 41.4 %collective-permute-start.36 = (bf16[800,768]{1,0:T(8,128)(2,1)S(1)}, bf16[800,768]{1,0:T(8,128)(2,1)}, u32[]{:S(2)}, u32[]{:S(2)}) collective-permute-start(bf16[800,768]{1,0:T(8,128)(2,1)S(1)} %add_4b.1.refs_15_), channel_id=1, source_target_pairs={{0,4},{1,5},{2,6},{3,7},{4,0},{5,1},{6,2},{7,3},{8,12},{9,13},{10,... | collective-permute-start | bytes 3686408 | tf_op jit(solution)/shard_map/ppermute | solution.py:329
  277.9 28.5 %collective-permute-start.39 = (bf16[800,768]{1,0:T(8,128)(2,1)}, bf16[800,768]{1,0:T(8,128)(2,1)S(1)}, u32[]{:S(2)}, u32[]{:S(2)}) collective-permute-start(bf16[800,768]{1,0:T(8,128)(2,1)} %get-tuple-element.251), channel_id=1, source_target_pairs={{0,1},{1,0},{2,3},{3,2},{4,5},{5,4},{6,7},{7,6},{8,9},{9,8},{10,11... | collective-permute-start | bytes 3686408 | tf_op jit(solution)/shard_map/ppermute | solution.py:329
  278.0 23.9 %collective-permute-start.38 = (bf16[768,768]{1,0:T(8,128)(2,1)}, bf16[768,768]{1,0:T(8,128)(2,1)S(1)}, u32[]{:S(2)}, u32[]{:S(2)}) collective-permute-start(bf16[768,768]{1,0:T(8,128)(2,1)} %get-tuple-element.250), channel_id=1, source_target_pairs={{0,1},{1,0},{2,3},{3,2},{4,5},{5,4},{6,7},{7,6},{8,9},{9,8},{10,11... | collective-permute-start | bytes 3538952 | tf_op jit(solution)/shard_map/ppermute | solution.py:329
  278.5 28.0 %collective-permute-start.37 = (bf16[768,768]{1,0:T(8,128)(2,1)S(1)}, bf16[768,768]{1,0:T(8,128)(2,1)S(1)}, u32[]{:S(2)}, u32[]{:S(2)}) collective-permute-start(bf16[768,768]{1,0:T(8,128)(2,1)S(1)} %add_5b.1.refs_14_), channel_id=1, source_target_pairs={{0,2},{1,3},{2,0},{3,1},{4,6},{5,7},{6,4},{7,5},{8,10},{9,11},{10,... | collective-permute-start | bytes 3538952 | tf_op jit(solution)/shard_map/ppermute | solution.py:329
  280.0 21.9 %collective-permute-start.40 = (bf16[384,768]{1,0:T(8,128)(2,1)}, bf16[384,768]{1,0:T(8,128)(2,1)S(1)}, u32[]{:S(2)}, u32[]{:S(2)}) collective-permute-start(bf16[384,768]{1,0:T(8,128)(2,1)} %add_5a.1.refs_5_), channel_id=1, source_target_pairs={{0,4},{1,5},{2,6},{3,7},{4,0},{5,1},{6,2},{7,3},{8,12},{9,13},{10,... | collective-permute-start | bytes 1769480 | tf_op jit(solution)/shard_map/ppermute | solution.py:329
  312.9 32.5 %collective-permute-start.48 = (bf16[768,768]{1,0:T(8,128)(2,1)}, bf16[768,768]{1,0:T(8,128)(2,1)S(1)}, u32[]{:S(2)}, u32[]{:S(2)}) collective-permute-start(bf16[768,768]{1,0:T(8,128)(2,1)} %get-tuple-element.262.refs_0_), channel_id=1, source_target_pairs={{0,8},{24,16},{1,9},{25,17},{2,10},{26,18},{3,11},{27,19},{4,12},{... | collective-permute-start | bytes 3538952 | tf_op jit(solution)/shard_map/ppermute | solution.py:1158
  347.5 27.8 %collective-permute-start.51 = (bf16[768,768]{1,0:T(8,128)(2,1)S(1)}, bf16[768,768]{1,0:T(8,128)(2,1)S(1)}, u32[]{:S(2)}, u32[]{:S(2)}) collective-permute-start(bf16[768,768]{1,0:T(8,128)(2,1)S(1)} %add_7.1.refs_8_.refs_10_), channel_id=1, source_target_pairs={{8,16},{16,8},{9,17},{17,9},{10,18},{18,10},{11,19},{19,11},{12,20... | collective-permute-start | bytes 3538952 | tf_op jit(solution)/shard_map/ppermute | solution.py:1172
  357.5 26.0 %collective-permute-start.55 = (bf16[768,768]{1,0:T(8,128)(2,1)S(1)}, bf16[768,768]{1,0:T(8,128)(2,1)S(1)}, u32[]{:S(2)}, u32[]{:S(2)}) collective-permute-start(bf16[768,768]{1,0:T(8,128)(2,1)S(1)} %copy-done.53), channel_id=1, source_target_pairs={{0,8},{24,16},{1,9},{25,17},{2,10},{26,18},{3,11},{27,19},{4,12},{... | collective-permute-start | bytes 3538952 | tf_op jit(solution)/shard_map/ppermute | solution.py:1158
  381.6 33.8 %collective-permute-start.59 = (bf16[768,768]{1,0:T(8,128)(2,1)}, bf16[768,768]{1,0:T(8,128)(2,1)S(1)}, u32[]{:S(2)}, u32[]{:S(2)}) collective-permute-start(bf16[768,768]{1,0:T(8,128)(2,1)} %get-tuple-element.277.refs_1_), channel_id=1, source_target_pairs={{8,0},{16,24},{9,1},{17,25},{10,2},{18,26},{11,3},{19,27},{12,4},{... | collective-permute-start | bytes 3538952 | tf_op jit(solution)/shard_map/ppermute | solution.py:1179
  385.7 29.8 %collective-permute-start.60 = (bf16[768,768]{1,0:T(8,128)(2,1)S(1)}, bf16[768,768]{1,0:T(8,128)(2,1)S(1)}, u32[]{:S(2)}, u32[]{:S(2)}) collective-permute-start(bf16[768,768]{1,0:T(8,128)(2,1)S(1)} %add_10.1.refs_7_.refs_0_), channel_id=1, source_target_pairs={{8,16},{16,8},{9,17},{17,9},{10,18},{18,10},{11,19},{19,11},{12,20... | collective-permute-start | bytes 3538952 | tf_op jit(solution)/shard_map/ppermute | solution.py:1172
  408.9 25.4 %collective-permute-start.57 = (bf16[416,768]{1,0:T(8,128)(2,1)}, bf16[416,768]{1,0:T(8,128)(2,1)}, u32[]{:S(2)}, u32[]{:S(2)}) collective-permute-start(bf16[416,768]{1,0:T(8,128)(2,1)} %get-tuple-element.275.refs_2_), channel_id=1, source_target_pairs={{0,8},{24,16},{1,9},{25,17},{2,10},{26,18},{3,11},{27,19},{4,12},{... | collective-permute-start | bytes 1916936 | tf_op jit(solution)/shard_map/ppermute | solution.py:1158
  411.9 22.5 %collective-permute-start.58 = (bf16[400,768]{1,0:T(8,128)(2,1)}, bf16[400,768]{1,0:T(8,128)(2,1)}, u32[]{:S(2)}, u32[]{:S(2)}) collective-permute-start(bf16[400,768]{1,0:T(8,128)(2,1)} %get-tuple-element.276.refs_4_), channel_id=1, source_target_pairs={{0,8},{24,16},{1,9},{25,17},{2,10},{26,18},{3,11},{27,19},{4,12},{... | collective-permute-start | bytes 1843208 | tf_op jit(solution)/shard_map/ppermute | solution.py:1158
  416.6 25.5 %collective-permute-start.63 = (bf16[768,768]{1,0:T(8,128)(2,1)S(1)}, bf16[768,768]{1,0:T(8,128)(2,1)S(1)}, u32[]{:S(2)}, u32[]{:S(2)}) collective-permute-start(bf16[768,768]{1,0:T(8,128)(2,1)S(1)} %add_12.1.refs_3_.refs_1_), channel_id=1, source_target_pairs={{8,0},{16,24},{9,1},{17,25},{10,2},{18,26},{11,3},{19,27},{12,4},{... | collective-permute-start | bytes 3538952 | tf_op jit(solution)/shard_map/ppermute | solution.py:1179
  438.7 24.1 %collective-permute-start.61 = (bf16[400,768]{1,0:T(8,128)(2,1)S(1)}, bf16[400,768]{1,0:T(8,128)(2,1)S(1)}, u32[]{:S(2)}, u32[]{:S(2)}) collective-permute-start(bf16[400,768]{1,0:T(8,128)(2,1)S(1)} %get-tuple-element.279.refs_0_), channel_id=1, source_target_pairs={{8,16},{16,8},{9,17},{17,9},{10,18},{18,10},{11,19},{19,11},{12,20... | collective-permute-start | bytes 1843208 | tf_op jit(solution)/shard_map/ppermute | solution.py:1172
  442.9 31.3 %collective-permute-start.66 = (bf16[416,768]{1,0:T(8,128)(2,1)S(1)}, bf16[416,768]{1,0:T(8,128)(2,1)}, u32[]{:S(2)}, u32[]{:S(2)}) collective-permute-start(bf16[416,768]{1,0:T(8,128)(2,1)S(1)} %add_14.1.refs_3_.refs_1_), channel_id=1, source_target_pairs={{8,0},{16,24},{9,1},{17,25},{10,2},{18,26},{11,3},{19,27},{12,4},{... | collective-permute-start | bytes 1916936 | tf_op jit(solution)/shard_map/ppermute | solution.py:1179
  (154 other events, 1065.4 us)
